TPU v7x, 32 devices: a whole 2x2x4 slice. The times are simulated.
32 devices in a mesh: section: 2 (over x), wide: 16 (over z, y, core).
Axes of the slice: x: 2, y: 2, z: 4, core: 2. Of those that a mesh axis runs over, the one named last changes fastest.
Arguments:
- inputs: bfloat16 [2, 16, 512, 768], P(None, 'wide'), may hold values from -6 to 6
- cotangent: bfloat16 [2, 16, 512, 768], P(None, 'wide'), may hold values from -6 to 6
- token_size: int32 [2, 16, 512], P(None, 'wide'), may hold values from 1 to 16
- image_id: int32 [2, 16, 512], P(None, 'wide'), may hold values from 0 to 2, as said below
- w_in: bfloat16 [2, 768, 5376], P('section', 'wide'), may hold values from -0.21875 to 0.21875
- w_out: bfloat16 [2, 3840, 768], P('section', 'wide')
- ln_gain: bfloat16 [2, 768], P('section', 'wide'), may hold values from 0.099609375 to 1.8984375
- q_gain: bfloat16 [2, 64], P('section', 'wide'), may hold values from 0.099609375 to 1.8984375
- k_gain: bfloat16 [2, 64], P('section', 'wide'), may hold values from 0.099609375 to 1.8984375
Outputs:
- section_out: bfloat16 [2, 2, 16, 512, 768], P('section', None, 'wide')
- grad_in: float32 [2, 2, 16, 512, 768], P('section', None, 'wide')
- grad_w_in: float32 [2, 768, 5376], P('section', 'wide')
- grad_w_out: float32 [2, 3840, 768], P('section', 'wide')
- grad_ln_gain: float32 [2, 768], P('section', 'wide')
- grad_q_gain: float32 [2, 64], P('section', 'wide')
- grad_k_gain: float32 [2, 64], P('section', 'wide')
Inputs may be any that keep to these rules, and one draw needn't show every extreme that they name: `image_id`: each row holds 2 images of 60 to 196 consecutive slots, numbered 0 to 1 from the row's start; one image of each row has exactly 196 slots; the remaining slots at the row's end, one or more, carry the number 2 and form one more group.
All inputs are finite; a program needn't handle non-finite values.
Results may differ from a plain program's by a relative error of at most 0.033.
Values may be sent and summed in bfloat16 or wider, within the bound.
A program may use at most 192 MiB of HBM per device.

v0:
```python
import jax
import jax.numpy as jnp
from jax import lax
from jax.sharding import PartitionSpec as P

HEADS = 12
HD = 64


EPSILON = 1e-06
NEGATIVE = -1e30


def from_behind(block, axis, distance):
    devices = range(lax.axis_size(axis))
    route = [(i - distance, i) for i in devices if i - distance in devices]
    return lax.ppermute(block, axis, route)


def layer_norm(values, gain_vec):
    average = jnp.mean(values, -1, keepdims=True)
    centred = values - average
    variance = jnp.mean(centred * centred, -1, keepdims=True)
    return centred * lax.rsqrt(variance + EPSILON) * gain_vec


def exact_gelu(values):
    return jax.nn.gelu(values, approximate=False)


def head_norms(queries, keys_in, query_gain, key_gain):
    return (layer_norm(queries, query_gain), layer_norm(keys_in, key_gain))


def score_rows(queries, keys_in, image_ids, key_bias):
    scores = (
        jnp.einsum("qhd,khd->hqk", queries, keys_in, preferred_element_type=jnp.float32) * 0.125
        + key_bias[None, None, :]
    )
    same_image = image_ids[:, None] == image_ids[None, :]
    return jnp.where(same_image[None], scores, NEGATIVE)


def attend_forward(row_block):
    queries, keys_in, values, image_ids, key_bias = row_block
    scores = score_rows(queries, keys_in, image_ids, key_bias)
    largest = jnp.max(scores, -1, keepdims=True)
    exponent = jnp.exp(scores - largest)
    row_total = jnp.sum(exponent, -1, keepdims=True)
    weights = (exponent / row_total).astype(jnp.bfloat16)
    output = jnp.einsum("hqk,khd->qhd", weights, values, preferred_element_type=jnp.float32)
    return (output, largest + jnp.log(row_total))


def attend_backward(row_block):
    queries, keys_in, values, image_ids, key_bias, log_total, grad_out = row_block
    scores = score_rows(queries, keys_in, image_ids, key_bias)
    probabilities = jnp.exp(scores - log_total)
    grad_values = jnp.einsum(
        "hqk,qhd->khd",
        probabilities.astype(jnp.bfloat16),
        grad_out,
        preferred_element_type=jnp.float32,
    )
    grad_probs = jnp.einsum("qhd,khd->hqk", grad_out, values, preferred_element_type=jnp.float32)
    grad_scores = probabilities * (
        grad_probs - jnp.sum(probabilities * grad_probs, -1, keepdims=True)
    )
    grad_scores = grad_scores.astype(jnp.bfloat16)
    grad_queries = (
        jnp.einsum("hqk,khd->qhd", grad_scores, keys_in, preferred_element_type=jnp.float32) * 0.125
    )
    grad_keys = (
        jnp.einsum("hqk,qhd->khd", grad_scores, queries, preferred_element_type=jnp.float32) * 0.125
    )
    return (grad_queries, grad_keys, grad_values)


def layer_pieces(hidden, weights, image_ids, key_bias):
    w_in, w_out, ln_gain, q_gain, k_gain = weights
    row_count, slot_count, model_width = hidden.shape
    normed, norm_back = jax.vjp(layer_norm, hidden, ln_gain.astype(jnp.float32))
    normed_low = normed.astype(jnp.bfloat16).reshape(row_count * slot_count, model_width)
    projected = jnp.dot(normed_low, w_in, preferred_element_type=jnp.float32)
    head_shape = (row_count, slot_count, HEADS, HD)
    queries = projected[:, :model_width].reshape(head_shape)
    keys_in = projected[:, model_width : 2 * model_width].reshape(head_shape)
    values = (
        projected[:, 2 * model_width : 3 * model_width].reshape(head_shape).astype(jnp.bfloat16)
    )
    normed_heads, norms_back = jax.vjp(
        head_norms, queries, keys_in, q_gain.astype(jnp.float32), k_gain.astype(jnp.float32)
    )
    queries_low = normed_heads[0].astype(jnp.bfloat16)
    keys_low = normed_heads[1].astype(jnp.bfloat16)
    attended, log_total = lax.map(
        attend_forward, (queries_low, keys_low, values, image_ids, key_bias)
    )
    activated, gelu_back = jax.vjp(exact_gelu, projected[:, 3 * model_width :])
    combined = jnp.concatenate(
        [attended.reshape(row_count * slot_count, model_width), activated], 1
    ).astype(jnp.bfloat16)
    return (
        norm_back,
        normed_low,
        norms_back,
        queries_low,
        keys_low,
        values,
        log_total,
        gelu_back,
        combined,
    )


def layer_forward(hidden, weights, image_ids, key_bias):
    pieces = layer_pieces(hidden, weights, image_ids, key_bias)
    branch = jnp.dot(pieces[8], weights[1], preferred_element_type=jnp.float32)
    return hidden + branch.reshape(hidden.shape)


def layer_backward(hidden, grad_low, weights, image_ids, key_bias):
    (
        norm_back,
        normed_low,
        norms_back,
        queries_low,
        keys_low,
        values,
        log_total,
        gelu_back,
        combined,
    ) = layer_pieces(hidden, weights, image_ids, key_bias)
    row_count, slot_count, model_width = hidden.shape
    flat_rows = row_count * slot_count
    grad_flat = grad_low.reshape(flat_rows, model_width)
    contract_last = (((1,), (1,)), ((), ()))
    grad_combined = lax.dot_general(
        grad_flat, weights[1], contract_last, preferred_element_type=jnp.float32
    )
    grad_attended = (
        grad_combined[:, :model_width]
        .astype(jnp.bfloat16)
        .reshape(row_count, slot_count, HEADS, HD)
    )
    grad_up = gelu_back(grad_combined[:, model_width:])[0]
    grad_q, grad_k, grad_v = lax.map(
        attend_backward,
        (queries_low, keys_low, values, image_ids, key_bias, log_total, grad_attended),
    )
    grad_queries, grad_keys, grad_qgain, grad_kgain = norms_back((grad_q, grad_k))
    grad_projected = jnp.concatenate(
        [
            grad_queries.reshape(flat_rows, model_width),
            grad_keys.reshape(flat_rows, model_width),
            grad_v.reshape(flat_rows, model_width),
            grad_up,
        ],
        1,
    ).astype(jnp.bfloat16)
    grad_normed = lax.dot_general(
        grad_projected, weights[0], contract_last, preferred_element_type=jnp.float32
    )
    grad_hidden, grad_lngain = norm_back(grad_normed.reshape(hidden.shape))
    return (
        grad_low.astype(jnp.float32) + grad_hidden,
        grad_lngain,
        grad_qgain,
        grad_kgain,
        normed_low,
        grad_projected,
        combined,
        grad_flat,
    )


def unpack(gathered):
    return tuple((piece[0] for piece in gathered))


def on_device(inputs, cotangent, token_size, image_id, w_in, w_out, ln_gain, q_gain, k_gain):
    micro_count = inputs.shape[0]
    row_count, slot_count, model_width = (inputs.shape[1], inputs.shape[2], inputs.shape[3])
    flat_rows = row_count * slot_count
    section_index = lax.axis_index("section")
    first_section = section_index == 0

    def fetch_weights():
        return unpack(
            (
                lax.all_gather(w_in, "wide", axis=1, tiled=True),
                lax.all_gather(w_out, "wide", axis=1, tiled=True),
                lax.all_gather(ln_gain, "wide", axis=1, tiled=True),
                lax.all_gather(q_gain, "wide", axis=1, tiled=True),
                lax.all_gather(k_gain, "wide", axis=1, tiled=True),
            )
        )

    outputs_tick, inputs_tick = ([], [])
    received = jnp.zeros_like(inputs[0])
    for tick in range(micro_count + 1):
        weights_now = fetch_weights()
        micro_index = tick - section_index
        active = (micro_index >= 0) & (micro_index < micro_count)
        own_index = min(tick, micro_count - 1)
        prev_index = max(tick - 1, 0)
        layer_input = jnp.where(first_section, inputs[own_index], received)
        ids_now = jnp.where(first_section, image_id[own_index], image_id[prev_index])
        sizes_now = jnp.where(first_section, token_size[own_index], token_size[prev_index])
        bias_now = jnp.log(sizes_now.astype(jnp.float32))
        result = lax.cond(
            active,
            lambda: layer_forward(
                layer_input.astype(jnp.float32), weights_now, ids_now, bias_now
            ).astype(jnp.bfloat16),
            lambda: jnp.zeros_like(layer_input),
        )
        outputs_tick.append(result)
        inputs_tick.append(layer_input)
        if tick < micro_count:
            received = from_behind(result, "section", 1)
    section_out = jnp.stack(
        [
            jnp.where(first_section, outputs_tick[index], outputs_tick[index + 1])
            for index in range(micro_count)
        ]
    )
    width_in = w_in.shape[2]
    width_mid = w_out.shape[1] * 0 + width_in - 2 * model_width
    head_size = q_gain.shape[1] * lax.axis_size("wide")

    def spare_results():
        return (
            jnp.zeros((row_count, slot_count, model_width), jnp.float32),
            jnp.zeros((model_width,), jnp.float32),
            jnp.zeros((head_size,), jnp.float32),
            jnp.zeros((head_size,), jnp.float32),
            jnp.zeros((flat_rows, model_width), jnp.bfloat16),
            jnp.zeros((flat_rows, width_in), jnp.bfloat16),
            jnp.zeros((flat_rows, width_mid), jnp.bfloat16),
            jnp.zeros((flat_rows, model_width), jnp.bfloat16),
        )

    grads_tick, kept_tick = ([], [])
    gain_sums = [
        jnp.zeros((model_width,), jnp.float32),
        jnp.zeros((head_size,), jnp.float32),
        jnp.zeros((head_size,), jnp.float32),
    ]
    received_grad = jnp.zeros_like(cotangent[0])
    for tick in range(micro_count + 1):
        weights_now = fetch_weights()
        micro_index = tick - (1 - section_index)
        active = (micro_index >= 0) & (micro_index < micro_count)
        early = max(tick - 1, 0)
        late = min(tick, micro_count - 1)
        grad_low = jnp.where(first_section, received_grad, cotangent[late])
        layer_input = jnp.where(
            first_section, inputs_tick[early], inputs_tick[min(tick + 1, micro_count)]
        )
        ids_now = jnp.where(first_section, image_id[early], image_id[late])
        sizes_now = jnp.where(first_section, token_size[early], token_size[late])
        bias_now = jnp.log(sizes_now.astype(jnp.float32))
        results = lax.cond(
            active,
            lambda: layer_backward(
                layer_input.astype(jnp.float32), grad_low, weights_now, ids_now, bias_now
            ),
            spare_results,
        )
        grads_tick.append(results[0])
        kept_tick.append(results[4:])
        for position in range(3):
            gain_sums[position] = gain_sums[position] + results[position + 1]
        if tick < micro_count:
            received_grad = from_behind(results[0].astype(jnp.bfloat16), "section", -1)
    grad_in = jnp.stack(
        [
            jnp.where(first_section, grads_tick[index + 1], grads_tick[index])
            for index in range(micro_count)
        ]
    )
    chosen = [
        [
            jnp.where(first_section, kept_tick[index + 1][member], kept_tick[index][member])
            for index in range(micro_count)
        ]
        for member in range(4)
    ]
    normed_all = jnp.concatenate(chosen[0], 0)
    grad_proj_all = jnp.concatenate(chosen[1], 0)
    combined_all = jnp.concatenate(chosen[2], 0)
    grad_out_all = jnp.concatenate(chosen[3], 0)
    contract_rows = (((0,), (0,)), ((), ()))
    terms_in = lax.dot_general(
        normed_all, grad_proj_all, contract_rows, preferred_element_type=jnp.float32
    )
    terms_out = lax.dot_general(
        combined_all, grad_out_all, contract_rows, preferred_element_type=jnp.float32
    )
    owned = (
        lax.psum_scatter(terms_in[None], "wide", scatter_dimension=1, tiled=True),
        lax.psum_scatter(terms_out[None], "wide", scatter_dimension=1, tiled=True),
        lax.psum_scatter(gain_sums[0][None], "wide", scatter_dimension=1, tiled=True),
        lax.psum_scatter(gain_sums[1][None], "wide", scatter_dimension=1, tiled=True),
        lax.psum_scatter(gain_sums[2][None], "wide", scatter_dimension=1, tiled=True),
    )
    return (section_out[None], grad_in[None], owned[0], owned[1], owned[2], owned[3], owned[4])


def solution(mesh):
    return jax.shard_map(
        on_device,
        mesh=mesh,
        in_specs=(
            P(None, "wide", None, None),
            P(None, "wide", None, None),
            P(None, "wide", None),
            P(None, "wide", None),
            P("section", "wide", None),
            P("section", "wide", None),
            P("section", "wide"),
            P("section", "wide"),
            P("section", "wide"),
        ),
        out_specs=(
            P("section", None, "wide", None, None),
            P("section", None, "wide", None, None),
            P("section", "wide", None),
            P("section", "wide", None),
            P("section", "wide"),
            P("section", "wide"),
            P("section", "wide"),
        ),
        check_vma=False,
    )
```

profile of v0, /device:TPU:8, one launch (start us, length us, event | category | flops | bytes accessed | tf_op | source)
XLA Modules:
  0.0 1112.4 jit_solution(3857362333509408329)
XLA Ops:
  13.9 26.2 %all-reduce.6 = (bf16[768]{0:T(1024)(128)(2,1)S(1)}, bf16[64]{0:T(256)(128)(2,1)}, bf16[64]{0:T(256)(128)(2,1)}) all-reduce(bf16[768]{0:T(1024)(128)(2,1)S(1)} %dynamic-update-slice, bf16[64]{0:T(256)(128)(2,1)S(1)} %dynamic-update-slice.1, bf16[64]{0:T(256)(128)(2,1)S(1)} %dynamic-update-slice.2), channel_id=1, replica_groups=mesh['section'=2,'wide'=16] {'wide'}, use_global_device_ids=true, to_apply=%add | all-reduce | flops 896 | bytes 3584 | tf_op jit(solution)/shard_map/squeeze | solution.py:178
  43.4 28.0 %all-gather.5.cloned.1.call-done = bf16[1,3840,768]{2,1,0:T(8,128)(2,1)} async-done(((bf16[1,240,768]{2,1,0:T(8,128)(2,1)}), bf16[1,3840,768]{2,1,0:T(8,128)(2,1)}) %all-gather.5.cloned.1.call-update) | async-done | bytes 5898256 | tf_op jit(solution)/shard_map/all_gather | solution.py:192
  71.4 74.5 %all-gather.3.cloned.1.call-done = bf16[1,768,5376]{2,1,0:T(8,128)(2,1)} async-done(((bf16[1,48,5376]{2,1,0:T(8,128)(2,1)}), bf16[1,768,5376]{2,1,0:T(8,128)(2,1)}) %all-gather.3.cloned.1.call-update) | async-done | bytes 8257552 | tf_op jit(solution)/shard_map/all_gather | solution.py:191
  145.8 68.5 %conditional.6 = (bf16[1,512,768]{2,1,0:T(8,128)(2,1)S(1)}) conditional(s32[]{:T(128)} %convert_element_type.405, () %tuple.77, (bf16[1,512,768]{2,1,0:T(8,128)(2,1)S(1)}, bf16[768]{0:T(1024)(128)(2,1)S(1)}, bf16[768,5376]{1,0:T(8,128)(2,1)}, s32[1,512]{1,0:T(1,128)S(1)}, bf16[64]{0:T(256)(128)(2,1)}, /*index=5*/bf16[64]{0:T(256)(128)(2,1)}, ...), branch_computations={%region_0.1_spmd, %region_1.10_spmd} | conditional | flops 8197649920 | bytes 144177984 | solution.py:211
  149.0 7.0 fusion.33
  161.4 15.5 %fusion.4 = bf16[512,3072]{1,0:T(8,128)(2,1)} fusion(f32[512,5376]{1,0:T(8,128)} %copy-done.25), kind=kLoop, calls=%fused_computation.8 | loop fusion | flops 102236160 | bytes 9437184 | tf_op jit(solution)/shard_map/convert.1
  189.3 11.9 %fusion.267 = (f32[12,512]{1,0:T(8,128)}, f32[12,512,512]{1,2,0:T(8,128)}) fusion(f32[512]{0:T(512)} %bitcast.7, pred[512,512]{0,1:T(8,128)(4,1)S(1)} %broadcast_compare_fusion, f32[512,12,64]{0,2,1:T(8,128)} %bitcast.381, f32[64]{0:T(128)} %convert_element_type.329, f32[512,12]{0,1:T(8,128)S(1)} %get-tuple-element.627, ...), kind=kOutput, calls=%fused_computation.527 | convolution fusion | flops 421528064 | bytes 16116224 | tf_op jit(solution)/shard_map/cond/branch_1_fun/while/body/eval_jaxpr/sub | solution.py:48
  201.3 5.8 fusion.29
  207.3 6.8 fusion.26
  216.3 16.9 %collective-permute-done = bf16[1,512,768]{2,1,0:T(8,128)(2,1)S(1)} collective-permute-done((bf16[1,512,768]{2,1,0:T(8,128)(2,1)S(1)}, bf16[1,512,768]{2,1,0:T(8,128)(2,1)S(1)}, u32[]{:S(2)}, u32[]{:S(2)}) %collective-permute-start) | collective-permute-done | bytes 786464 | tf_op jit(solution)/shard_map/ppermute | solution.py:17
  234.4 70.2 %conditional.7 = (bf16[1,512,768]{2,1,0:T(8,128)(2,1)}) conditional(s32[]{:T(128)} %convert_element_type.407, () %tuple.79, (bf16[1,512,768]{2,1,0:T(8,128)(2,1)S(1)}, bf16[768]{0:T(1024)(128)(2,1)S(1)}, bf16[768,5376]{1,0:T(8,128)(2,1)}, pred[1,512]{1,0:T(4,128)(4,1)S(1)}, s32[1,512]{1,0:T(1,128)S(1)}, /*index=5*/s32[1,512]{1,0:T(1,128)S(1)}, ...), branch_computations={%region_10.11_spmd, %region_11.20_spmd} | conditional | flops 8197650432 | bytes 141042976 | solution.py:211
  238.1 7.0 fusion.74
  250.6 15.6 %fusion.45 = bf16[512,3072]{1,0:T(8,128)(2,1)} fusion(f32[512,5376]{1,0:T(8,128)} %copy-done.26), kind=kLoop, calls=%fused_computation.72 | loop fusion | flops 102236160 | bytes 9437184 | tf_op jit(solution)/shard_map/convert.6
  279.2 11.2 %fusion.269 = (f32[12,512]{1,0:T(8,128)S(1)}, f32[12,512,512]{1,2,0:T(8,128)}) fusion(f32[512]{0:T(512)} %bitcast.428, pred[512,512]{0,1:T(8,128)(4,1)S(1)} %broadcast_compare_fusion.1, f32[512,12,64]{0,2,1:T(8,128)} %bitcast.378, f32[64]{0:T(128)} %convert_element_type.339, f32[512,12]{0,1:T(8,128)} %get-tuple-element.633, ...), kind=kOutput, calls=%fused_computation.529 | convolution fusion | flops 421528064 | bytes 16116224 | tf_op jit(solution)/shard_map/cond/branch_1_fun/while/body/eval_jaxpr/sub | solution.py:48
  290.5 6.0 fusion.70
  296.8 7.8 fusion.67
  304.6 5.4 collective-permute-start.1
  310.0 14.9 %conditional.9 = (f32[1,512,768]{2,1,0:T(8,128)S(1)}, f32[768]{0:T(1024)S(1)}, f32[64]{0:T(128)S(1)}, f32[64]{0:T(128)S(1)}, bf16[512,768]{1,0:T(8,128)(2,1)}, /...) conditional(s32[]{:T(128)} %convert_element_type.413, () %tuple.84, ...), branch_computations={%region_30.31_spmd, %region_31.50_spmd} | conditional | flops 14146677760 | bytes 501453248 | solution.py:264
  330.2 127.9 %collective-permute-done.2 = bf16[1,512,768]{2,1,0:T(8,128)(2,1)S(1)} collective-permute-done((bf16[1,512,768]{2,1,0:T(8,128)(2,1)S(1)}, bf16[1,512,768]{2,1,0:T(8,128)(2,1)S(1)}, u32[]{:S(2)}, u32[]{:S(2)}) %collective-permute-start.2) | collective-permute-done | bytes 786464 | tf_op jit(solution)/shard_map/ppermute | solution.py:17
  458.1 128.3 %conditional.10 = (f32[1,512,768]{2,1,0:T(8,128)S(1)}, f32[768]{0:T(1024)S(1)}, f32[64]{0:T(128)S(1)}, f32[64]{0:T(128)S(1)}, bf16[512,768]{1,0:T(8,128)(2,1)}, ...) conditional(s32[]{:T(128)} %convert_element_type.412, () %tuple.83, ...), branch_computations={%region_50.51_spmd, %region_51.70_spmd} | conditional | flops 14146679808 | bytes 509328416 | solution.py:264
  465.1 4.4 fusion.282
  474.0 7.0 fusion.281
  493.0 15.5 %multiply_convert_fusion.39 = (bf16[512,3072]{1,0:T(8,128)(2,1)}, f32[512,3072]{1,0:T(8,128)S(1)}) fusion(f32[512,5376]{1,0:T(8,128)} %copy-done.4), kind=kLoop, calls=%fused_computation.298 | loop fusion | flops 102236160 | bytes 15728640 | tf_op jit(solution)/shard_map/convert.30
  508.5 5.9 add_convert_fusion.3
  527.9 4.4 pad_maximum_fusion.3
  532.3 7.5 fusion.189
  542.1 7.6 multiply_reduce_fusion.9
  549.7 7.2 multiply_convert_fusion.38
  570.5 5.2 pad_maximum_fusion.2
  575.7 9.1 fusion.184
  589.0 19.2 %collective-permute-done.3 = bf16[1,512,768]{2,1,0:T(8,128)(2,1)S(1)} collective-permute-done((bf16[1,512,768]{2,1,0:T(8,128)(2,1)S(1)}, bf16[1,512,768]{2,1,0:T(8,128)(2,1)S(1)}, u32[]{:S(2)}, u32[]{:S(2)}) %collective-permute-start.3) | collective-permute-done | bytes 786464 | tf_op jit(solution)/shard_map/ppermute | solution.py:17
  608.2 130.6 %conditional.11 = (f32[1,512,768]{2,1,0:T(8,128)}, f32[768]{0:T(1024)S(1)}, f32[64]{0:T(128)S(1)}, f32[64]{0:T(128)S(1)}, bf16[512,768]{1,0:T(8,128)(2,1)}, /*in...) conditional(s32[]{:T(128)} %convert_element_type.417, () %tuple.87, ...), branch_computations={%region_70.71_spmd, %region_71.90_spmd} | conditional | flops 14146677760 | bytes 506171904 | solution.py:264
  616.3 4.4 fusion.284
  625.1 7.0 fusion.283
  644.1 15.5 %multiply_convert_fusion.47 = (bf16[512,3072]{1,0:T(8,128)(2,1)}, f32[512,3072]{1,0:T(8,128)S(1)}) fusion(f32[512,5376]{1,0:T(8,128)} %copy-done.5), kind=kLoop, calls=%fused_computation.393 | loop fusion | flops 102236160 | bytes 15728640 | tf_op jit(solution)/shard_map/convert.44
  659.7 5.9 add_convert_fusion.6
  679.1 4.3 pad_maximum_fusion.5
  683.4 7.5 fusion.229
  693.1 7.6 multiply_reduce_fusion.12
  700.8 7.2 multiply_convert_fusion.46
  721.6 5.2 pad_maximum_fusion.4
  726.7 9.1 fusion.224
  745.7 9.1 fusion.250
  754.9 4.9 broadcast_select_fusion.6
  759.8 11.9 %convolution_bitcast_fusion = f32[1,768,5376]{2,1,0:T(8,128)} fusion(bf16[512,5376]{1,0:T(8,128)(2,1)S(1)} %get-tuple-element.689, bf16[512,5376]{1,0:T(8,128)(2,1)S(1)} %get-tuple-element.688, bf16[512,768]{1,0:T(8,128)(2,1)S(1)} %get-tuple-element.708, bf16[512,768]{1,0:T(8,128)(2,1)S(1)} %get-tuple-element.709), kind=kOutput, calls=%fused_computation.477 | convolution fusion | flops 8480882688 | bytes 29097984 | tf_op jit(solution)/shard_map/dot_general | solution.py:295
  778.6 22.7 %all-reduce.5 = (f32[1,64]{1,0:T(1,128)S(1)}, f32[1,64]{1,0:T(1,128)S(1)}) all-reduce(f32[1,64]{1,0:T(1,128)S(1)} %get-tuple-element.711, f32[1,64]{1,0:T(1,128)S(1)} %get-tuple-element.710), channel_id=5, replica_groups=mesh['section'=2,'wide'=16] {'wide'}, use_global_device_ids=true, to_apply=%region_93.94.clone | all-reduce | flops 128 | bytes 1024
  807.8 117.9 %reduce-scatter.10.cloned.1.call-done = f32[1,240,768]{2,1,0:T(8,128)} async-done(((f32[1,3840,768]{2,1,0:T(8,128)}), f32[1,240,768]{2,1,0:T(8,128)}) %reduce-scatter.10.cloned.1.call-update) | async-done | bytes 737296 | tf_op jit(solution)/shard_map/reduce_scatter | solution.py:303
  925.7 179.9 %reduce-scatter.8.cloned.1.call-done = f32[1,48,5376]{2,1,0:T(8,128)} async-done(((f32[1,768,5376]{2,1,0:T(8,128)}), f32[1,48,5376]{2,1,0:T(8,128)}) %reduce-scatter.8.cloned.1.call-update) | async-done | bytes 1032208 | tf_op jit(solution)/shard_map/reduce_scatter | solution.py:302
  (316 shorter events, 200.5 us)
Async XLA Ops:
  7.2 64.2 %all-gather.5.cloned.1.call-start = ((), (), s32[]{:S(2)}) async-start(), calls=%async_computation.4 | async-start | bytes 6266880 | tf_op jit(solution)/shard_map/all_gather | solution.py:192
  7.9 137.9 %all-gather.3.cloned.1.call-start = ((), (), s32[]{:S(2)}) async-start(), calls=%async_computation.3 | async-start | bytes 8773632 | tf_op jit(solution)/shard_map/all_gather | solution.py:191
  8.6 797.8 %reduce-scatter.12.cloned.1.call-start = ((), (), s32[]{:S(2)}) async-start(), calls=%async_computation.7 | async-start | bytes 417792
  43.3 266.7 %copy-start.15 = (bf16[1,512,768]{2,1,0:T(8,128)(2,1)}, bf16[1,512,768]{2,1,0:T(8,128)(2,1)S(1)}, u32[]{:S(2)}) copy-start(bf16[1,512,768]{2,1,0:T(8,128)(2,1)S(1)} %select_bitcast_fusion.4) | copy-start | bytes 2359300
  145.8 69.9 %copy-start.50 = (s32[2,1,512]{2,1,0:T(1,128)S(1)}, s32[2,1,512]{2,1,0:T(1,128)}, u32[]{:S(2)}) copy-start(s32[2,1,512]{2,1,0:T(1,128)} %param.23) | copy-start | bytes 12292
  189.3 11.9 %copy-start.46 = (bf16[512,768]{0,1:T(8,128)(2,1)S(1)}, bf16[512,768]{0,1:T(8,128)(2,1)}, u32[]{:S(2)}) copy-start(bf16[512,768]{0,1:T(8,128)(2,1)} %copy.150) | copy-start | bytes 2359300 | tf_op jit(solution)/shard_map/cond
  214.4 18.8 %collective-permute-start = (bf16[1,512,768]{2,1,0:T(8,128)(2,1)S(1)}, bf16[1,512,768]{2,1,0:T(8,128)(2,1)S(1)}, u32[]{:S(2)}, u32[]{:S(2)}) collective-permute-start(bf16[1,512,768]{2,1,0:T(8,128)(2,1)S(1)} %get-tuple-element.760), channel_id=1, source_target_pairs={{0,16},{1,17},{2,18},{3,19},{4,20},{5,21},{6,22},{7,23},{8,24},{9,... | collective-permute-start | bytes 2359304 | tf_op jit(solution)/shard_map/ppermute | solution.py:17
  234.4 75.6 %copy-start.14 = (bf16[1,512,768]{2,1,0:T(8,128)(2,1)}, bf16[1,512,768]{2,1,0:T(8,128)(2,1)S(1)}, u32[]{:S(2)}) copy-start(bf16[1,512,768]{2,1,0:T(8,128)(2,1)S(1)} %bitcast_select_fusion.1) | copy-start | bytes 2359300
  304.6 24.0 %collective-permute-start.1 = (bf16[1,512,768]{2,1,0:T(8,128)(2,1)}, bf16[1,512,768]{2,1,0:T(8,128)(2,1)}, u32[]{:S(2)}, u32[]{:S(2)}) collective-permute-start(bf16[1,512,768]{2,1,0:T(8,128)(2,1)} %get-tuple-element.761), channel_id=1, source_target_pairs={{0,16},{1,17},{2,18},{3,19},{4,20},{5,21},{6,22},{7,23},{8,24},{9,... | collective-permute-start | bytes 2359304 | tf_op jit(solution)/shard_map/ppermute | solution.py:17
  324.9 133.1 %copy-start.57 = (f32[64]{0:T(128)}, f32[64]{0:T(128)S(1)}, u32[]{:S(2)}) copy-start(f32[64]{0:T(128)S(1)} %get-tuple-element.581) | copy-start | bytes 772
  325.0 133.1 %copy-start.51 = (f32[768]{0:T(1024)}, f32[768]{0:T(1024)S(1)}, u32[]{:S(2)}) copy-start(f32[768]{0:T(1024)S(1)} %get-tuple-element.575) | copy-start | bytes 9220
  325.0 133.1 %copy-start.59 = (f32[64]{0:T(128)}, f32[64]{0:T(128)S(1)}, u32[]{:S(2)}) copy-start(f32[64]{0:T(128)S(1)} %get-tuple-element.578) | copy-start | bytes 772
  325.0 133.1 %copy-start.16 = (bf16[1,512,768]{2,1,0:T(8,128)(2,1)S(1)}, bf16[1,512,768]{2,1,0:T(8,128)(2,1)}, u32[]{:S(2)}) copy-start(bf16[1,512,768]{2,1,0:T(8,128)(2,1)} %copy-done.15) | copy-start | bytes 2359300
  325.0 133.1 %copy-start.53 = (f32[1,1,512]{2,1,0:T(1,128)S(1)}, f32[1,1,512]{2,1,0:T(1,128)}, u32[]{:S(2)}) copy-start(f32[1,1,512]{2,1,0:T(1,128)} %get-tuple-element.700) | copy-start | bytes 6148
  326.1 131.9 %collective-permute-start.2 = (bf16[1,512,768]{2,1,0:T(8,128)(2,1)S(1)}, bf16[1,512,768]{2,1,0:T(8,128)(2,1)S(1)}, u32[]{:S(2)}, u32[]{:S(2)}) collective-permute-start(bf16[1,512,768]{2,1,0:T(8,128)(2,1)S(1)} %convert_element_type.414), channel_id=1, source_target_pairs={{16,0},{17,1},{18,2},{19,3},{20,4},{21,5},{22,6},{23,7},{24,8},{25... | collective-permute-start | bytes 2359304 | tf_op jit(solution)/shard_map/ppermute | solution.py:17
  328.6 129.5 %copy-start.6 = (bf16[1,512,768]{2,1,0:T(8,128)(2,1)}, bf16[1,512,768]{2,1,0:T(8,128)(2,1)S(1)}, u32[]{:S(2)}) copy-start(bf16[1,512,768]{2,1,0:T(8,128)(2,1)S(1)} %slice_bitcast_fusion) | copy-start | bytes 2359300
  330.1 128.0 %copy-start.17 = (bf16[1,512,768]{2,1,0:T(8,128)(2,1)}, bf16[1,512,768]{2,1,0:T(8,128)(2,1)S(1)}, u32[]{:S(2)}) copy-start(bf16[1,512,768]{2,1,0:T(8,128)(2,1)S(1)} %bitcast_select_fusion) | copy-start | bytes 2359300
  458.1 150.1 %copy-start.54 = (f32[1,512]{1,0:T(1,128)S(1)}, f32[1,512]{1,0:T(1,128)}, u32[]{:S(2)}) copy-start(f32[1,512]{1,0:T(1,128)} %get-tuple-element.702) | copy-start | bytes 6148
  458.1 6.0 copy-start.7
  458.1 11.4 %copy-start.38 = (bf16[1,512,768]{2,1,0:T(8,128)(2,1)}, bf16[1,512,768]{2,1,0:T(8,128)(2,1)S(1)}, u32[]{:S(2)}) copy-start(bf16[1,512,768]{2,1,0:T(8,128)(2,1)S(1)} %get-tuple-element.504) | copy-start | bytes 2359300 | tf_op jit(solution)/shard_map/cond
  458.1 7.0 copy-start.68
  492.7 15.8 %slice-start.2 = ((s8[7864320]{0:T(1024)(128)(4,1)}), s8[4194304]{0:T(1024)(128)(4,1)S(1)}, s32[]{:S(2)}) async-start(s8[7864320]{0:T(1024)(128)(4,1)} %bitcast.393), calls=%async_computation.10 | async-start | bytes 8388608 | tf_op jit(solution)/shard_map/cond
  492.9 15.5 %slice-start.3 = ((s8[7864320]{0:T(1024)(128)(4,1)}), s8[3670016]{0:T(1024)(128)(4,1)S(1)}, s32[]{:S(2)}) async-start(s8[7864320]{0:T(1024)(128)(4,1)} %bitcast.393), calls=%async_computation.11 | async-start | bytes 7340032 | tf_op jit(solution)/shard_map/cond
  508.5 6.0 copy-start.47
  517.9 4.6 copy-start
  563.7 6.8 copy-start.44
  570.2 5.5 copy-start.11
  575.7 10.0 copy-start.8
  575.7 10.0 copy-start.39
  586.4 21.8 %copy-start.61 = (f32[64]{0:T(128)}, f32[64]{0:T(128)S(1)}, u32[]{:S(2)}) copy-start(f32[64]{0:T(128)S(1)} %get-tuple-element.582) | copy-start | bytes 772
  586.4 21.8 %copy-start.63 = (f32[64]{0:T(128)}, f32[64]{0:T(128)S(1)}, u32[]{:S(2)}) copy-start(f32[64]{0:T(128)S(1)} %get-tuple-element.579) | copy-start | bytes 772
  587.6 20.5 %collective-permute-start.3 = (bf16[1,512,768]{2,1,0:T(8,128)(2,1)S(1)}, bf16[1,512,768]{2,1,0:T(8,128)(2,1)S(1)}, u32[]{:S(2)}, u32[]{:S(2)}) collective-permute-start(bf16[1,512,768]{2,1,0:T(8,128)(2,1)S(1)} %convert_element_type.418), channel_id=1, source_target_pairs={{16,0},{17,1},{18,2},{19,3},{20,4},{21,5},{22,6},{23,7},{24,8},{25... | collective-permute-start | bytes 2359304 | tf_op jit(solution)/shard_map/ppermute | solution.py:17
  608.2 130.6 %copy-start.52 = (f32[768]{0:T(1024)S(1)}, f32[768]{0:T(1024)}, u32[]{:S(2)}) copy-start(f32[768]{0:T(1024)} %copy-done.51) | copy-start | bytes 9220
  608.4 12.3 %copy-start.40 = (bf16[1,512,768]{2,1,0:T(8,128)(2,1)}, bf16[1,512,768]{2,1,0:T(8,128)(2,1)S(1)}, u32[]{:S(2)}) copy-start(bf16[1,512,768]{2,1,0:T(8,128)(2,1)S(1)} %get-tuple-element.518) | copy-start | bytes 2359300 | tf_op jit(solution)/shard_map/cond
  608.4 7.9 copy-start.69
  643.8 15.8 %slice-start.4 = ((s8[7864320]{0:T(1024)(128)(4,1)}), s8[4194304]{0:T(1024)(128)(4,1)S(1)}, s32[]{:S(2)}) async-start(s8[7864320]{0:T(1024)(128)(4,1)} %bitcast.395), calls=%async_computation.12 | async-start | bytes 8388608 | tf_op jit(solution)/shard_map/cond
  644.1 15.5 %slice-start.5 = ((s8[7864320]{0:T(1024)(128)(4,1)}), s8[3670016]{0:T(1024)(128)(4,1)S(1)}, s32[]{:S(2)}) async-start(s8[7864320]{0:T(1024)(128)(4,1)} %bitcast.395), calls=%async_computation.13 | async-start | bytes 7340032 | tf_op jit(solution)/shard_map/cond
  659.6 6.0 copy-start.49
  669.0 4.6 copy-start.2
  714.7 6.8 copy-start.45
  721.3 5.5 copy-start.13
  726.7 10.0 copy-start.9
  726.7 10.0 copy-start.41
  738.8 4.7 copy-start.65
  739.8 185.9 %reduce-scatter.10.cloned.1.call-start = ((), (), s32[]{:S(2)}) async-start(), calls=%async_computation.6 | async-start | bytes 12533760 | tf_op jit(solution)/shard_map/reduce_scatter | solution.py:303
  754.8 350.8 %reduce-scatter.8.cloned.1.call-start = ((), (), s32[]{:S(2)}) async-start(), calls=%async_computation.5 | async-start | bytes 17547264 | tf_op jit(solution)/shard_map/reduce_scatter | solution.py:302
  775.6 26.9 %copy-start.22 = (f32[1,512,768]{2,1,0:T(8,128)S(1)}, f32[1,512,768]{2,1,0:T(8,128)}, u32[]{:S(2)}) copy-start(f32[1,512,768]{2,1,0:T(8,128)} %copy-done.21) | copy-start | bytes 4718596
  775.6 26.9 %copy-start.24 = (f32[1,512,768]{2,1,0:T(8,128)S(1)}, f32[1,512,768]{2,1,0:T(8,128)}, u32[]{:S(2)}) copy-start(f32[1,512,768]{2,1,0:T(8,128)} %copy-done.23) | copy-start | bytes 4718596
  (21 other events, 69.7 us)
Sparse Core Ops, SparseCore 0:
  10.3 61.0 all-gather.4
  73.7 72.1 all-gather.2
  739.9 53.4 reduce-scatter.11
  798.6 127.1 reduce-scatter.9
  930.4 175.1 reduce-scatter.7
where the time goes:
time: 1120 us; the launch traced here: 1110 us
  waiting for transfers between devices  566 us (51%)
  other arithmetic  183 us (16%)
  matrix products  178 us (16%)
  local copies, waits for them, and re-layouts  99.8 us (9%)
  blocking collectives  48.9 us (4%)
  between operations  16.5 us (1%)
  loops' own time  11.3 us (1%)
    reduce_scatter x1, waiting for transfers between devices, on_device(): lax.psum_scatter(terms_in[None], 'wide', scatter_dimension=1, tiled=True)  180 us
    ppermute x4, waiting for transfers between devices, from_behind(): return lax.ppermute(block, axis, route)  164 us
    reduce_scatter x1, waiting for transfers between devices, on_device(): lax.psum_scatter(terms_out[None], 'wide', scatter_dimension=1, tiled=True)  118 us
    another operation x10, other arithmetic  80.7 us
    all_gather x1, waiting for transfers between devices, fetch_weights(): lax.all_gather(w_in, 'wide', axis=1, tiled=True)  74.5 us
    cond x68, local copies, waits for them, and re-layouts  28.4 us
    all_gather x1, waiting for transfers between devices, fetch_weights(): lax.all_gather(w_out, 'wide', axis=1, tiled=True)  28 us
    dot_general x4, matrix products, layer_pieces(): projected = jnp.dot(normed_low, w_in, preferred_element_type=jnp.float32)  28 us
  transfers between devices with their start and end apart: 9, of which 7 were waited for; matrix products, arithmetic and copies ran while one was open for 5% of the time, Pallas kernels for 0%

commit v1 on v0

v1 whole, which is shorter than its diff:
```python
import functools

import jax
import jax.numpy as jnp
from jax import lax
from jax.experimental import pallas as pl
from jax.experimental.pallas import tpu as pltpu
from jax.sharding import PartitionSpec as P

HEADS = 12
HD = 64


EPSILON = 1e-06
NEGATIVE = -1e30


def layer_norm(values, gain_vec):
    average = jnp.mean(values, -1, keepdims=True)
    centred = values - average
    variance = jnp.mean(centred * centred, -1, keepdims=True)
    return centred * lax.rsqrt(variance + EPSILON) * gain_vec


def exact_gelu(values):
    return jax.nn.gelu(values, approximate=False)


def head_norms(queries, keys_in, query_gain, key_gain):
    return (layer_norm(queries, query_gain), layer_norm(keys_in, key_gain))


def score_rows(queries, keys_in, image_ids, key_bias):
    scores = (
        jnp.einsum("qhd,khd->hqk", queries, keys_in, preferred_element_type=jnp.float32) * 0.125
        + key_bias[None, None, :]
    )
    same_image = image_ids[:, None] == image_ids[None, :]
    return jnp.where(same_image[None], scores, NEGATIVE)


def attend_forward(row_block):
    queries, keys_in, values, image_ids, key_bias = row_block
    scores = score_rows(queries, keys_in, image_ids, key_bias)
    largest = jnp.max(scores, -1, keepdims=True)
    exponent = jnp.exp(scores - largest)
    row_total = jnp.sum(exponent, -1, keepdims=True)
    weights = (exponent / row_total).astype(jnp.bfloat16)
    output = jnp.einsum("hqk,khd->qhd", weights, values, preferred_element_type=jnp.float32)
    return (output, largest + jnp.log(row_total))


def attend_backward(row_block):
    queries, keys_in, values, image_ids, key_bias, log_total, grad_out = row_block
    scores = score_rows(queries, keys_in, image_ids, key_bias)
    probabilities = jnp.exp(scores - log_total)
    grad_values = jnp.einsum(
        "hqk,qhd->khd",
        probabilities.astype(jnp.bfloat16),
        grad_out,
        preferred_element_type=jnp.float32,
    )
    grad_probs = jnp.einsum("qhd,khd->hqk", grad_out, values, preferred_element_type=jnp.float32)
    grad_scores = probabilities * (
        grad_probs - jnp.sum(probabilities * grad_probs, -1, keepdims=True)
    )
    grad_scores = grad_scores.astype(jnp.bfloat16)
    grad_queries = (
        jnp.einsum("hqk,khd->qhd", grad_scores, keys_in, preferred_element_type=jnp.float32) * 0.125
    )
    grad_keys = (
        jnp.einsum("hqk,qhd->khd", grad_scores, queries, preferred_element_type=jnp.float32) * 0.125
    )
    return (grad_queries, grad_keys, grad_values)


def layer_pieces(hidden, weights, image_ids, key_bias):
    w_in, w_out, ln_gain, q_gain, k_gain = weights
    row_count, slot_count, model_width = hidden.shape
    normed, norm_back = jax.vjp(layer_norm, hidden, ln_gain.astype(jnp.float32))
    normed_low = normed.astype(jnp.bfloat16).reshape(row_count * slot_count, model_width)
    projected = jnp.dot(normed_low, w_in, preferred_element_type=jnp.float32)
    head_shape = (row_count, slot_count, HEADS, HD)
    queries = projected[:, :model_width].reshape(head_shape)
    keys_in = projected[:, model_width : 2 * model_width].reshape(head_shape)
    values = (
        projected[:, 2 * model_width : 3 * model_width].reshape(head_shape).astype(jnp.bfloat16)
    )
    normed_heads, norms_back = jax.vjp(
        head_norms, queries, keys_in, q_gain.astype(jnp.float32), k_gain.astype(jnp.float32)
    )
    queries_low = normed_heads[0].astype(jnp.bfloat16)
    keys_low = normed_heads[1].astype(jnp.bfloat16)
    attended, log_total = lax.map(
        attend_forward, (queries_low, keys_low, values, image_ids, key_bias)
    )
    activated, gelu_back = jax.vjp(exact_gelu, projected[:, 3 * model_width :])
    combined = jnp.concatenate(
        [attended.reshape(row_count * slot_count, model_width), activated], 1
    ).astype(jnp.bfloat16)
    return (
        norm_back,
        normed_low,
        norms_back,
        queries_low,
        keys_low,
        values,
        log_total,
        gelu_back,
        combined,
    )


def layer_backward(hidden, grad_low, pieces, weights, image_ids, key_bias):
    (
        norm_back,
        normed_low,
        norms_back,
        queries_low,
        keys_low,
        values,
        log_total,
        gelu_back,
        combined,
    ) = pieces
    row_count, slot_count, model_width = hidden.shape
    flat_rows = row_count * slot_count
    grad_flat = grad_low.reshape(flat_rows, model_width)
    contract_last = (((1,), (1,)), ((), ()))
    grad_combined = lax.dot_general(
        grad_flat, weights[1], contract_last, preferred_element_type=jnp.float32
    )
    grad_attended = (
        grad_combined[:, :model_width]
        .astype(jnp.bfloat16)
        .reshape(row_count, slot_count, HEADS, HD)
    )
    grad_up = gelu_back(grad_combined[:, model_width:])[0]
    grad_q, grad_k, grad_v = lax.map(
        attend_backward,
        (queries_low, keys_low, values, image_ids, key_bias, log_total, grad_attended),
    )
    grad_queries, grad_keys, grad_qgain, grad_kgain = norms_back((grad_q, grad_k))
    grad_projected = jnp.concatenate(
        [
            grad_queries.reshape(flat_rows, model_width),
            grad_keys.reshape(flat_rows, model_width),
            grad_v.reshape(flat_rows, model_width),
            grad_up,
        ],
        1,
    ).astype(jnp.bfloat16)
    grad_normed = lax.dot_general(
        grad_projected, weights[0], contract_last, preferred_element_type=jnp.float32
    )
    grad_hidden, grad_lngain = norm_back(grad_normed.reshape(hidden.shape))
    return (
        grad_low.astype(jnp.float32) + grad_hidden,
        grad_lngain,
        grad_qgain,
        grad_kgain,
        normed_low,
        grad_projected,
        combined,
        grad_flat,
    )


MESH = pl.DeviceIdType.MESH
NZ = 4
BLOCK = ((48, 5376), (240, 768))
CUT_IN, CUT_OUT = 2176, 96
PART = ((48, CUT_IN), (CUT_OUT, 768))
REST = ((48, 5376 - 2 * CUT_IN), (240 - 2 * CUT_OUT, 768))


class Place:
    def __init__(self):
        self.x, self.wide = lax.axis_index("section"), lax.axis_index("wide")
        self.y, self.z, self.c = (self.wide // 2) % 2, self.wide // 4, self.wide % 2

    def at(self, x, y, z, c=None):
        return (x, z * 4 + y * 2 + (self.c if c is None else c))

    def along(self, colour, block_z, far_first, far_second):
        dx = jnp.where(colour == 0, far_first, far_second)
        dy = jnp.where(colour == 0, far_second, far_first)
        return self.flip(self.x, dx), self.flip(self.y, dy), block_z

    @staticmethod
    def flip(value, far):
        return value + far - 2 * value * far

    def first(self, colour):
        return self.at(*self.along(colour, self.z, 1, 0))

    def second(self, colour):
        return self.at(*self.along(colour, self.z, 0, 1))

    def sibling(self):
        return self.at(self.x, self.y, self.z, 1 - self.c)


def greet(place):
    barrier = pltpu.get_barrier_semaphore()
    x, y, z = place.x, place.y, place.z

    def signal(device):
        pl.semaphore_signal(barrier, inc=1, device_id=device, device_id_type=MESH)

    signal(place.at(1 - x, y, z))
    signal(place.at(x, 1 - y, z))
    signal(place.sibling())
    pl.when(z < NZ - 1)(lambda: signal(place.at(x, y, z + 1)))
    pl.when(z > 0)(lambda: signal(place.at(x, y, z - 1)))
    pl.semaphore_wait(barrier, 3 + (z < NZ - 1).astype(jnp.int32) + (z > 0).astype(jnp.int32))


def number_of(block):
    return block[0] * 8 + block[1] * 4 + block[2]


def cut(ref, array, colour):
    rows, cols = BLOCK[array]
    if array == 0:
        if colour is None:
            return ref.at[:, pl.ds(2 * CUT_IN, cols - 2 * CUT_IN)]
        return ref.at[:, pl.ds(pl.multiple_of(colour * CUT_IN, 128), CUT_IN)]
    if colour is None:
        return ref.at[pl.ds(2 * CUT_OUT, rows - 2 * CUT_OUT), :]
    return ref.at[pl.ds(pl.multiple_of(colour * CUT_OUT, 16), CUT_OUT), :]


def loop(count, body):
    def step(index, carry):
        body(index)
        return carry
    lax.fori_loop(0, count, step, 0)


class Gather:
    def __init__(self, place, array, own, full, send_sem, recv_sem, core_sem):
        self.place, self.array, self.own, self.full = place, array, own, full
        self.send_sem, self.recv_sem, self.core_sem = send_sem, recv_sem, core_sem

    def view(self, block, colour, plane=None):
        rows = BLOCK[self.array][0]
        place = self.place
        start = (block[2] * 4 + block[1] * 2 + (place.c if plane is None else plane)) * rows
        return cut(self.full.at[block[0], pl.ds(pl.multiple_of(start, 16), rows), :], self.array, colour)

    def copy(self, link, device, block, colour, own=False, other_plane=False):
        kind = 2 if colour is None else colour
        number = number_of(block)
        target = self.view(block, colour, 1 - self.place.c if other_plane else None)
        source = cut(self.own, self.array, colour) if own else target
        sems = self.core_sem if link == 4 else self.recv_sem
        return pltpu.make_async_remote_copy(
            src_ref=source, dst_ref=target, send_sem=self.send_sem.at[link, kind, number], recv_sem=sems.at[kind, number],
            device_id=device, device_id_type=MESH)

    def visit(self, block, colour, onward, first, second, drain, condition=None, own=False):
        place = self.place

        def body():
            if not drain and not own:
                self.copy(0, place.sibling(), block, colour).wait_recv()

            def send(link, device):
                copy = self.copy(link, device, block, colour, own)
                copy.wait_send() if drain else copy.start()

            for link, step in onward:
                target = place.z + step
                pl.when((target >= 0) & (target < NZ))(functools.partial(send, link, place.at(place.x, place.y, target)))
            if first is not None:
                send(2, first)
            if second is not None:
                if isinstance(second, tuple) and len(second) == 3:
                    pl.when(second[2])(functools.partial(send, 3, second[:2]))
                else:
                    send(3, second)
            send(4, place.sibling())
        if condition is None:
            body()
        else:
            pl.when(condition)(body)

    def begin(self, drain=False):
        place = self.place
        me = (place.x, place.y, place.z)
        everywhere = ((0, 1), (1, -1))
        self.visit(me, None, everywhere, place.at(1 - place.x, place.y, place.z), place.at(place.x, 1 - place.y, place.z), drain, own=True)

        def body(colour):
            self.visit(me, colour, everywhere, place.first(colour), place.second(colour), drain, own=True)
        loop(2, body)

    def square(self, drain=False):
        place = self.place

        def body(index):
            far_x, far_y = (index != 1).astype(jnp.int32), (index != 0).astype(jnp.int32)
            block = (place.flip(place.x, far_x), place.flip(place.y, far_y), place.z)
            self.visit(block, None, ((0, 1), (1, -1)), None, place.at(place.x, 1 - place.y, place.z) + (index == 0,), drain)
        loop(3, body)

    def sided(self, distance, body):
        place = self.place

        def side_body(side):
            step = 1 - 2 * side
            block_z = place.z - step * distance
            body(side, block_z, (block_z >= 0) & (block_z < NZ) & ((distance > 0) | (side == 0)))
        loop(2, side_body)

    def onward(self, side):
        return ((0, 1), (1, -1))[side]

    def z_step(self, distance, drain=False):
        place = self.place
        for side in (0, 1):
            step = 1 - 2 * side
            block_z = place.z - step * distance

            def body(colour):
                self.visit((place.x, place.y, block_z), colour, ((side, step),), place.first(colour), place.second(colour), drain)
            pl.when((block_z >= 0) & (block_z < NZ))(lambda: loop(2, body))

    def line(self, distance, drain=False):
        place = self.place
        for side in (0, 1):
            step = 1 - 2 * side
            block_z = place.z - step * distance

            def body(index):
                block = (place.flip(place.x, index % 2), place.flip(place.y, index // 2), block_z)
                self.visit(block, None, ((side, step),), None, None, drain)
            pl.when((block_z >= 0) & (block_z < NZ))(lambda: loop(4, body))

    def a_step(self, distance, drain=False):
        place = self.place

        def body(side, block_z, there):
            def inner(colour):
                self.visit(place.along(colour, block_z, 1, 0), colour, (), None, place.second(colour), drain)
            pl.when(there)(lambda: loop(2, inner))
        self.sided(distance, body)

    def b_step(self, distance, drain=False):
        place = self.place

        def body(side, block_z, there):
            def inner(index):
                colour = index // 2
                self.visit(place.along(colour, block_z, index % 2, 1), colour, (), None, None, drain)
            pl.when(there)(lambda: loop(4, inner))
        self.sided(distance, body)

    def from_core(self):
        place = self.place

        def body(number):
            block = (number // 8, (number // 4) % 2, number % 4)
            self.copy(4, place.sibling(), block, None, other_plane=True).wait_recv()
            for colour in (0, 1):
                self.copy(4, place.sibling(), block, colour, other_plane=True).wait_recv()
        loop(16, body)

    def drain(self):
        self.begin(True)
        self.square(True)

        def body(index):
            self.z_step(index + 1, True)
            self.line(index + 1, True)
            self.a_step(index, True)
            self.b_step(index, True)
        loop(NZ, body)


def gather_kernel(w_in, w_out, full_in, full_out, *sems):
    place = Place()
    greet(place)
    first = Gather(place, 0, w_in, full_in, *sems[:3])
    second = Gather(place, 1, w_out, full_out, *sems[3:6])
    copies = []
    for array, (own, full) in enumerate(((w_in, full_in), (w_out, full_out))):
        rows = BLOCK[array][0]
        copy = pltpu.make_async_copy(own, full.at[place.x, pl.ds(pl.multiple_of(place.wide * rows, 16), rows), :], sems[6].at[array])
        copy.start()
        copies.append(copy)
    first.begin()
    first.square()

    def early(index):
        first.z_step(index + 1)
        first.a_step(index)
        first.line(index + 1)
    loop(NZ, early)
    second.begin()
    second.square()

    def late(index):
        first.b_step(index)
        second.z_step(index + 1)
        second.a_step(index)
        second.line(index + 1)
    loop(NZ, late)
    loop(NZ, second.b_step)
    first.from_core()
    second.from_core()
    for copy in copies:
        copy.wait()
    first.drain()
    second.drain()


def gather_weights(w_in, w_out):
    any_space = pl.BlockSpec(memory_space=pl.ANY)
    dma = pltpu.SemaphoreType.DMA
    return pl.pallas_call(
        gather_kernel,
        out_shape=(jax.ShapeDtypeStruct((2, 768, 5376), jnp.bfloat16), jax.ShapeDtypeStruct((2, 3840, 768), jnp.bfloat16)),
        in_specs=[any_space] * 2, out_specs=(any_space,) * 2,
        scratch_shapes=[dma((5, 3, 16)), dma((3, 16)), dma((3, 16))] * 2 + [dma((2,))],
        compiler_params=pltpu.CompilerParams(collective_id=0, has_side_effects=True),
        name="gather_weights",
    )(w_in, w_out)


def gather_all(piece, axis):
    return lax.all_gather(lax.all_gather(piece, "wide", axis=axis, tiled=True), "section", axis=0, tiled=True)


def scatter_all(terms, axis):
    own = lax.psum_scatter(terms, "section", scatter_dimension=0, tiled=True)
    return lax.psum_scatter(own, "wide", scatter_dimension=axis, tiled=True)


def on_device(inputs, cotangent, token_size, image_id, w_in, w_out, ln_gain, q_gain, k_gain):
    section = lax.axis_index("section")
    wide = lax.axis_size("wide")
    model_width = inputs.shape[3]
    blocks_fit = wide == 16 and w_in.shape[1] == BLOCK[0][0] and w_out.shape[1] == BLOCK[1][0]
    if blocks_fit:
        full_in, full_out = gather_weights(w_in[0], w_out[0])
    else:
        full_in, full_out = gather_all(w_in, 1), gather_all(w_out, 1)
    cuts = (ln_gain.shape[1], ln_gain.shape[1] + q_gain.shape[1])
    gains = gather_all(jnp.concatenate([ln_gain, q_gain, k_gain], 1)[:, None], 1)
    full_ln, full_q, full_k = [
        part.reshape(2, -1) for part in (gains[:, :, : cuts[0]], gains[:, :, cuts[0] : cuts[1]], gains[:, :, cuts[1] :])
    ]
    weights = [(full_in[layer], full_out[layer], full_ln[layer], full_q[layer], full_k[layer]) for layer in range(2)]
    ids = image_id[section]
    bias = jnp.log(token_size[section].astype(jnp.float32))
    hidden = inputs[section]
    kept, outs = [], []
    for layer in range(2):
        hidden = hidden.astype(jnp.float32)
        pieces = layer_pieces(hidden, weights[layer], ids, bias)
        branch = jnp.dot(pieces[8], weights[layer][1], preferred_element_type=jnp.float32)
        kept.append((hidden, pieces))
        hidden = (hidden + branch.reshape(hidden.shape)).astype(jnp.bfloat16)
        outs.append(hidden)
    grad_low = cotangent[section]
    grads, gain_terms, terms_in, terms_out = [None, None], [None, None], [None, None], [None, None]
    contract_rows = (((0,), (0,)), ((), ()))
    for layer in (1, 0):
        results = layer_backward(kept[layer][0], grad_low, kept[layer][1], weights[layer], ids, bias)
        grads[layer] = results[0]
        gain_terms[layer] = results[1:4]
        terms_in[layer] = lax.dot_general(results[4], results[5], contract_rows, preferred_element_type=jnp.bfloat16)
        terms_out[layer] = lax.dot_general(results[6], results[7], contract_rows, preferred_element_type=jnp.bfloat16)
        grad_low = results[0].astype(jnp.bfloat16)
    terms_in, terms_out = jnp.stack(terms_in), jnp.stack(terms_out)
    own_in = scatter_all(terms_in, 1).astype(jnp.float32)
    own_out = scatter_all(terms_out, 1).astype(jnp.float32)
    gain_rows = [
        jnp.stack([gain_terms[layer][position] for layer in range(2)]).reshape(2, wide, -1) for position in range(3)
    ]
    own_gains = scatter_all(jnp.concatenate(gain_rows, 2), 1)[:, 0]
    swap = [(0, 1), (1, 0)]

    def both_micro(pair):
        mine = jnp.where(section == 0, pair[0], pair[1])
        other = lax.ppermute(jnp.where(section == 0, pair[1], pair[0]).astype(jnp.bfloat16), "section", swap)
        other = other.astype(mine.dtype)
        return jnp.where(section == 0, jnp.stack([mine, other]), jnp.stack([other, mine]))[None]

    return (
        both_micro(outs),
        both_micro(grads),
        own_in,
        own_out,
        own_gains[:, : cuts[0]],
        own_gains[:, cuts[0] : cuts[1]],
        own_gains[:, cuts[1] :],
    )


def solution(mesh):
    return jax.shard_map(
        on_device,
        mesh=mesh,
        in_specs=(
            P(None, "wide", None, None),
            P(None, "wide", None, None),
            P(None, "wide", None),
            P(None, "wide", None),
            P("section", "wide", None),
            P("section", "wide", None),
            P("section", "wide"),
            P("section", "wide"),
            P("section", "wide"),
        ),
        out_specs=(
            P("section", None, "wide", None, None),
            P("section", None, "wide", None, None),
            P("section", "wide", None),
            P("section", "wide", None),
            P("section", "wide"),
            P("section", "wide"),
            P("section", "wide"),
        ),
        check_vma=False,
    )
```

time: 1120 us -> 872 us (0.78)
  waiting for transfers between devices: 566 us -> 382 us
  Pallas kernels: 0 us -> 113 us
  other arithmetic: 183 us -> 114 us
  local copies, waits for them, and re-layouts: 99.8 us -> 43.4 us
  matrix products: 178 us -> 145 us
  loops' own time: 11.3 us -> 0 us
    ppermute x4 -> x2, waiting for transfers between devices: 164 us -> 0.83 us  [both_micro(): lax.ppermute(jnp.where(section == 0, pair[1], pair[0]).astype(jnp.bfloat1...]
    pallas_call x0 -> x1, Pallas kernels: none -> 113 us  [gather_weights(): pl.pallas_call(gather_kernel, out_shape=(jax.ShapeDtypeStruct((2, 768, 53...]
    all_gather x2 -> x0, waiting for transfers between devices: 102 us -> none  [the longest x1 74.5 us: fetch_weights(): lax.all_gather(w_in, 'wide', axis=1, tiled=True)]
    reduce_scatter x2 -> x5, waiting for transfers between devices: 298 us -> 381 us  [the longest x3 224 us: scatter_all(): own = lax.psum_scatter(terms, 'section', scatter_dimension=0, tiled=True)]
    cond x68 -> x0, local copies, waits for them, and re-layouts: 28.4 us -> none
    squeeze x1 -> x0, blocking collectives: 26.2 us -> none  [unpack(): return tuple((piece[0] for piece in gathered))]
    sub x2 -> x0, matrix products: 23.2 us -> none  [attend_forward(): exponent = jnp.exp(scores - largest)]
    all_gather x0 -> x2, blocking collectives: none -> 23 us  [the longest x1 18.7 us: gather_all(): lax.all_gather(piece, 'wide', axis=axis, tiled=True)]
  transfers between devices with their start and end apart: 9 -> 7, of which waited for: 7 -> 5; matrix products, arithmetic and copies ran while one was open for 5% -> 13% of each run, Pallas kernels for 0% -> 0%
where the time goes in v1:
time: 872 us; the launch traced here: 864 us
  waiting for transfers between devices  382 us (44%)
  matrix products  145 us (17%)
  other arithmetic  114 us (13%)
  Pallas kernels  113 us (13%)
  blocking collectives  48.3 us (6%)
  local copies, waits for them, and re-layouts  43.4 us (5%)
  between operations  15.4 us (2%)
    reduce_scatter x3, waiting for transfers between devices, scatter_all(): own = lax.psum_scatter(terms, 'section', scatter_dimension=0, tiled=True)  224 us
    reduce_scatter x2, waiting for transfers between devices, scatter_all(): return lax.psum_scatter(own, 'wide', scatter_dimension=axis, tiled=True)  157 us
    pallas_call x1, Pallas kernels, gather_weights(): pl.pallas_call(gather_kernel, out_shape=(jax.ShapeDtypeStruct((2, 768, 53...  113 us
    another operation x8, other arithmetic  52 us
    unnamed x1, blocking collectives  25.2 us
    dot_general x2, matrix products, layer_backward(): lax.dot_general(grad_projected, weights[0], contract_last, preferred_elem...  20.3 us
    dot_general x2, matrix products, attend_backward(): jnp.einsum('qhd,khd->hqk', grad_out, values, preferred_element_type=jnp.f...  19.8 us
    all_gather x1, blocking collectives, gather_all(): lax.all_gather(piece, 'wide', axis=axis, tiled=True)  18.7 us
  transfers between devices with their start and end apart: 7, of which 5 were waited for; matrix products, arithmetic and copies ran while one was open for 13% of the time, Pallas kernels for 0%

profile of v1, /device:TPU:8, one launch (start us, length us, event | category | flops | bytes accessed | tf_op | source)
XLA Modules:
  0.0 864.1 jit_solution(1184055716483330587)
XLA Ops:
  8.0 18.7 %all-gather.2 = bf16[16,1,56]{2,1,0:T(2,128)(2,1)S(1)} all-gather(bf16[1,1,56]{2,1,0:T(2,128)(2,1)S(1)} %maximum_bitcast_fusion), channel_id=2, replica_groups=mesh['section'=2,'wide'=16] {'wide'}, dimensions={0}, use_global_device_ids=true | all-gather | bytes 1904 | tf_op jit(solution)/shard_map/all_gather | solution.py:433
  26.7 4.3 all-gather.1
  34.0 113.1 %gather_weights.1 = (bf16[2,768,5376]{2,1,0:T(8,128)(2,1)}, bf16[2,3840,768]{2,1,0:T(8,128)(2,1)}) custom-call(bf16[48,5376]{1,0:T(8,128)(2,1)} %bitcast.261, bf16[240,768]{1,0:T(8,128)(2,1)} %bitcast.262), custom_call_target="tpu_custom_call" | custom-call | tf_op jit(solution)/shard_map/gather_weights/pallas_call | solution.py:422
  147.1 7.2 fusion.10
  154.4 15.0 %multiply_convert_fusion.3 = (bf16[512,3072]{1,0:T(8,128)(2,1)}, f32[512,3072]{1,0:T(8,128)}) fusion(f32[512,5376]{1,0:T(8,128)S(1)} %fusion.10), kind=kLoop, calls=%fused_computation.55 | loop fusion | flops 102236160 | bytes 15728640 | tf_op jit(solution)/shard_map/convert.32
  176.6 3.5 fusion.149
  182.0 2.7 copy-done.2
  184.8 2.4 fusion.95
  187.6 7.1 convert_reduce_fusion.1
  195.1 7.4 fusion.6
  205.1 7.8 fusion.36
  212.9 15.7 %add_convert_fusion.1 = (bf16[512,3072]{1,0:T(8,128)(2,1)}, f32[512,3072]{1,0:T(8,128)}) fusion(f32[512,3840]{1,0:T(8,128)S(1)} %fusion.36, f32[512,5376]{1,0:T(8,128)S(1)} %fusion.6), kind=kLoop, calls=%fused_computation.40 | loop fusion | flops 113246208 | bytes 22020096 | tf_op jit(solution)/shard_map/convert.20
  234.3 4.3 fusion.150
  240.5 2.5 copy-done.3
  243.1 3.3 fusion.94
  246.4 2.3 copy.124
  248.7 7.9 fusion.88
  257.4 8.9 %multiply_reduce_fusion.1 = (f32[12,512]{1,0:T(8,128)S(1)}, f32[12,512,512]{1,2,0:T(8,128)}) fusion(f32[12,512,512]{1,2,0:T(8,128)S(1)} %copy-done.4, f32[12,512]{1,0:T(8,128)S(1)} %log_add_fusion.1, bf16[512,12,64]{0,2,1:T(8,128)(2,1)} %bitcast.248, bf16[512,12,64]{0,2,1:T(8,128)(2,1)} %bitcast.251), kind=kOutput, calls=%fused_computation.5 | convolution fusion | flops 412084224 | bytes 26787840 | tf_op jit(solution)/shard_map/while/body/eval_jaxpr/qhd,khd->hqk/dot_general | solution.py:63
  266.3 6.0 multiply_convert_fusion.2
  272.2 2.3 copy.123
  274.6 2.3 copy.130
  276.9 9.7 %multiply_convert_fusion.1 = bf16[12,512,512]{1,2,0:T(8,128)(2,1)S(1)} fusion(f32[12,512,512]{1,2,0:T(8,128)} %get-tuple-element.164, f32[12,512,512]{1,2,0:T(8,128)} %copy-done.3, f32[12,512]{1,0:T(8,128)S(1)} %get-tuple-element.163, f32[12,512]{1,0:T(8,128)S(1)} %log_add_fusion.1), kind=kLoop, calls=%fused_computation.4 | loop fusion | flops 12582912 | bytes 31506432 | tf_op jit(solution)/shard_map/while/body/eval_jaxpr/convert_element_type | solution.py:67
  286.6 2.1 fusion.82
  290.1 2.1 fusion.76
  293.7 2.4 copy.129
  298.4 9.6 %fusion.68 = (f32[512]{0:T(512)S(1)}, f32[512,768]{1,0:T(8,128)S(1)}) fusion(bf16[512,768]{1,0:T(8,128)(2,1)S(1)} %copy-done.16, f32[768]{0:T(1024)S(1)} %reshape.1013, f32[512]{0:T(512)S(1)} %broadcast_multiply_fusion.4, bf16[2,768,5376]{2,1,0:T(8,128)(2,1)} %get-tuple-element.90, bf16[512,3072]{1,0:T(8,128)(2,1)} %get-tuple-element.117, ...), kind=kOutput, calls=%fused_computation.126 | convolution fusion | flops 4251844096 | bytes 16129024 | tf_op jit(solution)/shard_map/dot_general | solution.py:153
  310.1 3.6 convolution_bitcast_fusion.3
  313.7 3.6 convolution_bitcast_fusion.2
  317.4 5.1 pad_maximum_fusion.1
  322.6 5.9 fusion.40
  328.5 3.6 copy-done.19
  332.5 6.8 fusion.91
  340.5 10.9 %multiply_reduce_fusion = (f32[12,512]{1,0:T(8,128)S(1)}, f32[12,512,512]{1,2,0:T(8,128)}) fusion(f32[12,512,512]{1,2,0:T(8,128)} %copy-done.2, f32[12,512]{1,0:T(8,128)S(1)} %log_add_fusion, bf16[512,12,64]{0,2,1:T(8,128)(2,1)S(1)} %bitcast.246, bf16[512,12,64]{0,2,1:T(8,128)(2,1)S(1)} %bitcast.250), kind=kOutput, calls=%fused_computation.2 | convolution fusion | flops 412084224 | bytes 26787840 | tf_op jit(solution)/shard_map/while/body/eval_jaxpr/qhd,khd->hqk/dot_general | solution.py:63
  353.6 7.2 multiply_convert_fusion
  365.8 2.3 copy.136
  368.2 4.2 fusion.81
  374.9 9.9 %add_convert_fusion = bf16[512,3072]{1,0:T(8,128)(2,1)} fusion(f32[512,3072]{1,0:T(8,128)} %get-tuple-element.131, f32[512,3840]{1,0:T(8,128)} %copy-done.19, f32[512,5376]{1,0:T(8,128)} %copy-done.10), kind=kLoop, calls=%fused_computation.38 | loop fusion | flops 22020096 | bytes 22020096 | tf_op jit(solution)/shard_map/convert.11
  384.9 7.1 convolution_bitcast_fusion.1
  392.1 8.8 %convolution_bitcast_fusion = bf16[1,768,5376]{2,1,0:T(8,128)(2,1)} fusion(bf16[512,3072]{1,0:T(8,128)(2,1)} %get-tuple-element.117, bf16[512,768]{1,0:T(8,128)(2,1)S(1)} %copy-done.36, bf16[512,768]{1,0:T(8,128)(2,1)S(1)} %copy-done.39, bf16[512,768]{1,0:T(8,128)(2,1)S(1)} %copy-done.41, bf16[512,768]{1,0:T(8,128)(2,1)S(1)} %copy-done.18, ...), kind=kOutput, calls=%fused_computation.20 | convolution fusion | flops 4251844608 | bytes 14556160 | tf_op jit(solution)/shard_map/dot_general | solution.py:474
  400.9 10.8 %pad_maximum_fusion = bf16[2,768,5376]{2,1,0:T(8,128)(2,1)} fusion(bf16[1,768,5376]{2,1,0:T(8,128)(2,1)} %convolution_bitcast_fusion, bf16[1,768,5376]{2,1,0:T(8,128)(2,1)S(1)} %convolution_bitcast_fusion.1), kind=kLoop, calls=%fused_computation | loop fusion | flops 8257536 | bytes 33030144 | tf_op jit(solution)/shard_map/stack | solution.py:477
  412.4 10.6 %fusion.64 = (f32[768]{0:T(1024)S(1)}, f32[512]{0:T(512)S(1)}, f32[512,768]{1,0:T(8,128)}) fusion(f32[512]{0:T(512)S(1)} %copy-done.55, f32[512]{0:T(512)S(1)} %copy-done.61, bf16[2,1,512,768]{3,2,1,0:T(8,128)(2,1)S(1)} %copy-done.22, s32[]{:T(128)S(6)} %select_n.81, f32[768]{0:T(1024)S(1)} %copy-done.59, bf16[2,768,5376]{2,1,0:T(8,128)(2,1)} %get-tuple-element.90, ...), kind=kOutput, calls=%fused_computation.122 | convolution fusion | flops 4253022976 | bytes 16134148 | tf_op jit(solution)/shard_map/dot_general | solution.py:153
  423.9 35.9 %reduce-scatter.11.cloned.1.call-done = bf16[1,3840,768]{2,1,0:T(8,128)(2,1)} async-done(((bf16[2,3840,768]{2,1,0:T(8,128)(2,1)}), bf16[1,3840,768]{2,1,0:T(8,128)(2,1)}) %reduce-scatter.11.cloned.1.call-update) | async-done | bytes 5898256 | tf_op jit(solution)/shard_map/reduce_scatter | solution.py:437
  459.8 188.6 %reduce-scatter.7.cloned.1.call-done = bf16[1,768,5376]{2,1,0:T(8,128)(2,1)} async-done(((bf16[2,768,5376]{2,1,0:T(8,128)(2,1)}), bf16[1,768,5376]{2,1,0:T(8,128)(2,1)}) %reduce-scatter.7.cloned.1.call-update) | async-done | bytes 8257552 | tf_op jit(solution)/shard_map/reduce_scatter | solution.py:437
  648.5 8.2 select_bitcast_fusion.2
  662.6 25.2 %all-reduce = f32[1,16,56]{2,1,0:T(8,128)S(1)} all-reduce(f32[1,16,56]{2,1,0:T(8,128)} %reduce-scatter.15.cloned.1.call-done), channel_id=9, replica_groups=mesh['section'=2,'wide'=16] {'wide'}, use_global_device_ids=true, to_apply=%region_41.42.clone | all-reduce | flops 896 | bytes 7168
  689.1 3.3 maximum_select_fusion.1
  696.5 51.3 %reduce-scatter.13.cloned.1.call-done = bf16[1,240,768]{2,1,0:T(8,128)(2,1)} async-done(((bf16[1,3840,768]{2,1,0:T(8,128)(2,1)}), bf16[1,240,768]{2,1,0:T(8,128)(2,1)}) %reduce-scatter.13.cloned.1.call-update) | async-done | bytes 368656 | tf_op jit(solution)/shard_map/reduce_scatter | solution.py:438
  749.7 105.6 %reduce-scatter.9.cloned.1.call-done = bf16[1,48,5376]{2,1,0:T(8,128)(2,1)} async-done(((bf16[1,768,5376]{2,1,0:T(8,128)(2,1)}), bf16[1,48,5376]{2,1,0:T(8,128)(2,1)}) %reduce-scatter.9.cloned.1.call-update) | async-done | bytes 516112 | tf_op jit(solution)/shard_map/reduce_scatter | solution.py:438
  (262 shorter events, 59.2 us)
Async XLA Ops:
  7.2 169.2 %copy-start = (s32[2,1,512]{2,1,0:T(1,128)S(1)}, s32[2,1,512]{2,1,0:T(1,128)}, u32[]{:S(2)}) copy-start(s32[2,1,512]{2,1,0:T(1,128)} %param.12) | copy-start | bytes 12292
  7.2 452.6 %reduce-scatter.11.cloned.1.call-start = ((), (), s32[]{:S(2)}) async-start(), calls=%async_computation.7 | async-start | bytes 17694720 | tf_op jit(solution)/shard_map/reduce_scatter | solution.py:437
  31.1 123.3 %copy-start.58 = (f32[768]{0:T(1024)}, f32[768]{0:T(1024)S(1)}, u32[]{:S(2)}) copy-start(f32[768]{0:T(1024)S(1)} %reshape.1010) | copy-start | bytes 9220
  32.5 121.9 %copy-start.54 = (f32[512]{0:T(512)}, f32[512]{0:T(512)S(1)}, u32[]{:S(2)}) copy-start(f32[512]{0:T(512)S(1)} %broadcast_multiply_fusion.5) | copy-start | bytes 6148
  34.0 120.5 %copy-start.56 = (f32[512]{0:T(512)}, f32[512]{0:T(512)S(1)}, u32[]{:S(2)}) copy-start(f32[512]{0:T(512)S(1)} %fusion.75) | copy-start | bytes 6148
  34.0 120.4 %copy-start.60 = (f32[512]{0:T(512)}, f32[512]{0:T(512)S(1)}, u32[]{:S(2)}) copy-start(f32[512]{0:T(512)S(1)} %fusion.118) | copy-start | bytes 6148
  154.4 15.1 %copy-start.10 = (f32[512,5376]{1,0:T(8,128)}, f32[512,5376]{1,0:T(8,128)S(1)}, u32[]{:S(2)}) copy-start(f32[512,5376]{1,0:T(8,128)S(1)} %fusion.10) | copy-start | bytes 33030148
  172.6 7.5 copy-start.7
  172.7 7.4 copy-start.62
  194.7 7.8 copy-start.15
  202.6 10.3 %copy-start.11 = (f32[512,5376]{1,0:T(8,128)}, f32[512,5376]{1,0:T(8,128)S(1)}, u32[]{:S(2)}) copy-start(f32[512,5376]{1,0:T(8,128)S(1)} %fusion.6) | copy-start | bytes 33030148
  248.7 8.7 %copy-start.4 = (f32[12,512,512]{1,2,0:T(8,128)S(1)}, f32[12,512,512]{1,2,0:T(8,128)}, u32[]{:S(2)}) copy-start(f32[12,512,512]{1,2,0:T(8,128)} %copy-done.3) | copy-start | bytes 37748740
  248.7 17.5 %slice-start.3 = ((s8[6291456]{0:T(1024)(128)(4,1)}), s8[4194304]{0:T(1024)(128)(4,1)S(1)}, s32[]{:S(2)}) async-start(s8[6291456]{0:T(1024)(128)(4,1)} %bitcast.243), calls=%async_computation.13 | async-start | bytes 8388608
  257.4 8.9 %slice-start.4 = ((s8[6291456]{0:T(1024)(128)(4,1)}), s8[2097152]{0:T(1024)(128)(4,1)S(1)}, s32[]{:S(2)}) async-start(s8[6291456]{0:T(1024)(128)(4,1)} %bitcast.243), calls=%async_computation.14 | async-start | bytes 4194304
  298.3 9.7 %copy-start.40 = (bf16[512,768]{1,0:T(8,128)(2,1)}, bf16[512,768]{1,0:T(8,128)(2,1)S(1)}, u32[]{:S(2)}) copy-start(bf16[512,768]{1,0:T(8,128)(2,1)S(1)} %copy.128) | copy-start | bytes 2359300
  298.4 10.5 %copy-start.17 = (bf16[512,768]{1,0:T(8,128)(2,1)S(1)}, bf16[512,768]{1,0:T(8,128)(2,1)}, u32[]{:S(2)}) copy-start(bf16[512,768]{1,0:T(8,128)(2,1)} %copy-done.15) | copy-start | bytes 2359300
  298.4 10.5 %copy-start.48 = (bf16[2,1,512,768]{3,2,1,0:T(8,128)(2,1)S(1)}, bf16[2,1,512,768]{3,2,1,0:T(8,128)(2,1)}, u32[]{:S(2)}) copy-start(bf16[2,1,512,768]{3,2,1,0:T(8,128)(2,1)} %param.10) | copy-start | bytes 4718596
  310.1 12.4 %copy-start.12 = (f32[512,768]{1,0:T(8,128)}, f32[512,768]{1,0:T(8,128)S(1)}, u32[]{:S(2)}) copy-start(f32[512,768]{1,0:T(8,128)S(1)} %add_add_fusion.7) | copy-start | bytes 4718596
  322.5 325.9 %reduce-scatter.7.cloned.1.call-start = ((), (), s32[]{:S(2)}) async-start(), calls=%async_computation.5 | async-start | bytes 24772608 | tf_op jit(solution)/shard_map/reduce_scatter | solution.py:437
  332.5 8.0 copy-start.63
  332.5 8.0 copy-start.25
  340.5 11.0 %slice-start = ((s8[12582912]{0:T(1024)(128)(4,1)}), s8[4194304]{0:T(1024)(128)(4,1)S(1)}, s32[]{:S(2)}) async-start(s8[12582912]{0:T(1024)(128)(4,1)} %bitcast.213), calls=%async_computation.10 | async-start | bytes 8388608
  340.5 11.8 %slice-start.1 = ((s8[12582912]{0:T(1024)(128)(4,1)}), s8[4194304]{0:T(1024)(128)(4,1)S(1)}, s32[]{:S(2)}) async-start(s8[12582912]{0:T(1024)(128)(4,1)} %bitcast.213), calls=%async_computation.11 | async-start | bytes 8388608
  340.5 13.1 %slice-start.2 = ((s8[12582912]{0:T(1024)(128)(4,1)}), s8[4194304]{0:T(1024)(128)(4,1)S(1)}, s32[]{:S(2)}) async-start(s8[12582912]{0:T(1024)(128)(4,1)} %bitcast.213), calls=%async_computation.12 | async-start | bytes 8388608
  353.6 7.3 copy-start.6
  353.6 7.3 copy-start.8
  353.6 7.3 copy-start.31
  353.6 7.3 copy-start.33
  353.6 7.3 copy-start.44
  353.6 7.3 copy-start.65
  374.9 9.9 %copy-start.22 = (bf16[2,1,512,768]{3,2,1,0:T(8,128)(2,1)S(1)}, bf16[2,1,512,768]{3,2,1,0:T(8,128)(2,1)}, u32[]{:S(2)}) copy-start(bf16[2,1,512,768]{3,2,1,0:T(8,128)(2,1)} %param.9) | copy-start | bytes 4718596
  374.9 9.9 %copy-start.42 = (bf16[512,768]{1,0:T(8,128)(2,1)S(1)}, bf16[512,768]{1,0:T(8,128)(2,1)}, u32[]{:S(2)}) copy-start(bf16[512,768]{1,0:T(8,128)(2,1)} %copy.137) | copy-start | bytes 2359300
  374.9 9.9 %copy-start.55 = (f32[512]{0:T(512)S(1)}, f32[512]{0:T(512)}, u32[]{:S(2)}) copy-start(f32[512]{0:T(512)} %copy-done.54) | copy-start | bytes 6148
  374.9 9.9 %copy-start.59 = (f32[768]{0:T(1024)S(1)}, f32[768]{0:T(1024)}, u32[]{:S(2)}) copy-start(f32[768]{0:T(1024)} %copy-done.58) | copy-start | bytes 9220
  374.9 9.9 %copy-start.61 = (f32[512]{0:T(512)S(1)}, f32[512]{0:T(512)}, u32[]{:S(2)}) copy-start(f32[512]{0:T(512)} %copy-done.60) | copy-start | bytes 6148
  411.7 250.9 %reduce-scatter.15.cloned.1.call-start = ((), (), s32[]{:S(2)}) async-start(), calls=%async_computation.9 | async-start | bytes 24576 | tf_op jit(solution)/shard_map/reduce_scatter | solution.py:437
  423.8 323.9 %reduce-scatter.13.cloned.1.call-start = ((), (), s32[]{:S(2)}) async-start(), calls=%async_computation.8 | async-start | bytes 6266880 | tf_op jit(solution)/shard_map/reduce_scatter | solution.py:438
  459.8 188.7 %copy-start.35 = (bf16[512,768]{1,0:T(8,128)(2,1)S(1)}, bf16[512,768]{1,0:T(8,128)(2,1)}, u32[]{:S(2)}) copy-start(bf16[512,768]{1,0:T(8,128)(2,1)} %copy.123) | copy-start | bytes 2359300
  459.8 395.5 %reduce-scatter.9.cloned.1.call-start = ((), (), s32[]{:S(2)}) async-start(), calls=%async_computation.6 | async-start | bytes 8773632 | tf_op jit(solution)/shard_map/reduce_scatter | solution.py:438
  648.5 8.8 %copy-start.57 = (f32[512]{0:T(512)S(1)}, f32[512]{0:T(512)}, u32[]{:S(2)}) copy-start(f32[512]{0:T(512)} %copy-done.56) | copy-start | bytes 6148
  648.5 8.8 %copy-start.23 = (bf16[2,1,512,768]{3,2,1,0:T(8,128)(2,1)S(1)}, bf16[2,1,512,768]{3,2,1,0:T(8,128)(2,1)}, u32[]{:S(2)}) copy-start(bf16[2,1,512,768]{3,2,1,0:T(8,128)(2,1)} %param.9) | copy-start | bytes 4718596
  648.5 8.8 %copy-start.29 = (f32[512,768]{1,0:T(8,128)S(1)}, f32[512,768]{1,0:T(8,128)}, u32[]{:S(2)}) copy-start(f32[512,768]{1,0:T(8,128)} %get-tuple-element.177) | copy-start | bytes 4718596
  648.5 9.5 %copy-start.13 = (f32[512,768]{1,0:T(8,128)S(1)}, f32[512,768]{1,0:T(8,128)}, u32[]{:S(2)}) copy-start(f32[512,768]{1,0:T(8,128)} %copy-done.12) | copy-start | bytes 4718596
  656.7 32.4 %collective-permute-start = (bf16[1,512,768]{2,1,0:T(8,128)(2,1)}, bf16[1,512,768]{2,1,0:T(8,128)(2,1)}, u32[]{:S(2)}, u32[]{:S(2)}) collective-permute-start(bf16[1,512,768]{2,1,0:T(8,128)(2,1)} %get-tuple-element.137), channel_id=1, source_target_pairs={{0,16},{16,0},{1,17},{17,1},{2,18},{18,2},{3,19},{19,3},{4,20},{20... | collective-permute-start | bytes 2359304 | tf_op jit(solution)/shard_map/ppermute | solution.py:488
  659.2 34.1 %collective-permute-start.1 = (bf16[1,512,768]{2,1,0:T(8,128)(2,1)}, bf16[1,512,768]{2,1,0:T(8,128)(2,1)}, u32[]{:S(2)}, u32[]{:S(2)}) collective-permute-start(bf16[1,512,768]{2,1,0:T(8,128)(2,1)} %fusion.98), channel_id=1, source_target_pairs={{0,16},{16,0},{1,17},{17,1},{2,18},{18,2},{3,19},{19,3},{4,20},{20... | collective-permute-start | bytes 2359304 | tf_op jit(solution)/shard_map/ppermute | solution.py:488
  662.6 31.9 %copy-start.20 = (f32[1,1,1,512,768]{4,3,2,1,0:T(8,128)S(1)}, f32[1,1,1,512,768]{4,3,2,1,0:T(8,128)}, u32[]{:S(2)}) copy-start(f32[1,1,1,512,768]{4,3,2,1,0:T(8,128)} %select_bitcast_fusion) | copy-start | bytes 4718596
  688.5 8.0 copy-start.66
  689.1 168.3 %copy-start.1 = (s32[2,1,512]{2,1,0:T(1,128)S(1)}, s32[2,1,512]{2,1,0:T(1,128)}, u32[]{:S(2)}) copy-start(s32[2,1,512]{2,1,0:T(1,128)} %param.12) | copy-start | bytes 12292
  (33 other events, 139.1 us)
Sparse Core Ops, SparseCore 0:
  322.6 137.1 reduce-scatter.10
  462.1 186.3 reduce-scatter.6
  651.3 9.7 reduce-scatter.14
  665.4 82.3 reduce-scatter.12
  751.7 103.5 reduce-scatter.8

commit v2 on v1

--- a/solution.py
+++ b/solution.py
@@ -427,6 +427,224 @@
         compiler_params=pltpu.CompilerParams(collective_id=0, has_side_effects=True),
         name="gather_weights",
     )(w_in, w_out)
+
+
+def add_into(target, source):
+    rows = target.shape[0]
+
+    def body(step):
+        part = pl.ds(pl.multiple_of(step * 16, 16), 16)
+        target[part, :] = (target[part, :].astype(jnp.float32) + source[part, :].astype(jnp.float32)).astype(jnp.bfloat16)
+    loop(rows // 16, body)
+
+
+class Scatter:
+    def __init__(self, place, array, terms, held, core_land, land, rest_land, sems):
+        self.place, self.array, self.terms, self.held, self.core_land = place, array, terms, held, core_land
+        self.land, self.rest_land = land, rest_land
+        self.send_sem, self.recv_sem, self.rest_send, self.rest_recv, self.core_send, self.core_recv, self.local_sem = sems
+
+    def part(self, block, colour):
+        return cut(self.held.at[number_of(block)], self.array, colour)
+
+    def copy(self, device, block, colour, slot):
+        if colour is None:
+            target, send_sem, recv_sem = self.rest_land.at[slot], self.rest_send.at[slot], self.rest_recv.at[slot]
+        else:
+            target, send_sem, recv_sem = self.land.at[colour, slot], self.send_sem.at[colour, slot], self.recv_sem.at[colour, slot]
+        return pltpu.make_async_remote_copy(
+            src_ref=self.part(block, colour), dst_ref=target, send_sem=send_sem, recv_sem=recv_sem, device_id=device,
+            device_id_type=MESH)
+
+    def send(self, device, block, colour, slot, drain):
+        copy = self.copy(device, block, colour, slot)
+        copy.wait_send() if drain else copy.start()
+
+    def arrive(self, block, colour, slot, drain):
+        if not drain:
+            self.copy(self.place.sibling(), block, colour, slot).wait_recv()
+            add_into(self.part(block, colour), self.rest_land.at[slot] if colour is None else self.land.at[colour, slot])
+
+    def core_copy(self, block, mine):
+        rows = BLOCK[self.array][0]
+        place = self.place
+        number = number_of(block)
+        start = (block[2] * 4 + block[1] * 2 + (place.c if mine else 1 - place.c)) * rows
+        source = self.terms.at[block[0], pl.ds(pl.multiple_of(start, 16), rows), :]
+        if mine:
+            return pltpu.make_async_copy(source, self.held.at[number], self.local_sem.at[number])
+        return pltpu.make_async_remote_copy(
+            src_ref=source, dst_ref=self.core_land.at[number], send_sem=self.core_send.at[number],
+            recv_sem=self.core_recv.at[number], device_id=place.sibling(), device_id_type=MESH)
+
+    def sided(self, distance, body):
+        place = self.place
+
+        def side_body(side):
+            block_z = place.z + (2 * side - 1) * distance
+            there = (block_z >= 0) & (block_z < NZ) & (distance < NZ) & (distance >= 0) & ((distance > 0) | (side == 0))
+            pl.when(there)(lambda: body(block_z))
+        loop(2, side_body)
+
+    def start(self, distance):
+        place = self.place
+
+        def body(block_z):
+            def inner(index):
+                block = (place.flip(place.x, 1 - index % 2), place.flip(place.y, 1 - index // 2), block_z)
+                self.core_copy(block, False).start()
+                self.core_copy(block, True).start()
+            loop(4, inner)
+        self.sided(distance, body)
+
+    def k_step(self, distance, drain=False):
+        place = self.place
+
+        def body(block_z):
+            def inner(index):
+                far_x, far_y = 1 - index % 2, 1 - index // 2
+                block = (place.flip(place.x, far_x), place.flip(place.y, far_y), block_z)
+                if not drain:
+                    self.core_copy(block, True).wait()
+                    copy = self.core_copy(block, False)
+                    copy.wait_recv()
+                    add_into(self.held.at[number_of(block)], self.core_land.at[number_of(block)])
+                    copy.wait_send()
+
+                def out(colour):
+                    far_first = jnp.where(colour == 0, far_x, far_y)
+                    far_second = jnp.where(colour == 0, far_y, far_x)
+                    pl.when(far_second == 1)(lambda: self.send(place.second(colour), block, colour, far_first * 4 + block_z, drain))
+                loop(2, out)
+            loop(4, inner)
+        self.sided(distance, body)
+
+    def a_step(self, distance, drain=False):
+        place = self.place
+
+        def body(block_z):
+            def inner(index):
+                colour, far_first = index % 2, 1 - index // 2
+                block = place.along(colour, block_z, far_first, 0)
+                self.arrive(block, colour, far_first * 4 + block_z, drain)
+                pl.when(far_first == 1)(lambda: self.send(place.first(colour), block, colour, 8 + block_z, drain))
+            loop(4, inner)
+        self.sided(distance, body)
+
+    def b_step(self, distance):
+        place = self.place
+
+        def body(block_z):
+            loop(2, lambda colour: self.arrive((place.x, place.y, block_z), colour, 8 + block_z, False))
+        self.sided(distance, body)
+
+    def toward(self, distance, body):
+        place = self.place
+        for side, step in ((0, -1), (1, 1)):
+            block_z, behind = place.z + step * distance, place.z - step
+            there = (block_z >= 0) & (block_z < NZ) & (distance < NZ) & (distance >= 0)
+            pl.when(there)(functools.partial(body, block_z, side, step, (behind >= 0) & (behind < NZ)))
+
+    def z_step(self, distance, drain=False):
+        place = self.place
+
+        def body(block_z, side, step, more):
+            block = (place.x, place.y, block_z)
+            slot = 12 + 4 * side + block_z
+
+            def inner(colour):
+                pl.when(more)(lambda: self.arrive(block, colour, slot, drain))
+                pl.when(distance > 0)(lambda: self.send(place.at(place.x, place.y, place.z + step), block, colour, slot, drain))
+            loop(2, inner)
+        self.toward(distance, body)
+
+    def line(self, distance, drain=False):
+        place = self.place
+
+        def body(block_z, side, step, more):
+            def inner(index):
+                block = (place.flip(place.x, 1 - index % 2), place.flip(place.y, 1 - index // 2), block_z)
+                slot = 16 * side + number_of(block)
+                pl.when(more)(lambda: self.arrive(block, None, slot, drain))
+                pl.when(distance > 0)(lambda: self.send(place.at(place.x, place.y, place.z + step), block, None, slot, drain))
+            loop(4, inner)
+        self.toward(distance, body)
+
+    def square(self, drain=False):
+        place = self.place
+        over_x, over_y = place.at(1 - place.x, place.y, place.z), place.at(place.x, 1 - place.y, place.z)
+        far = (1 - place.x, place.y, place.z)
+        self.send(over_y, (1 - place.x, 1 - place.y, place.z), None, 33, drain)
+        self.send(over_y, (place.x, 1 - place.y, place.z), None, 32, drain)
+        self.arrive(far, None, 33, drain)
+        self.send(over_x, far, None, 34, drain)
+        self.arrive((place.x, place.y, place.z), None, 32, drain)
+        self.arrive((place.x, place.y, place.z), None, 34, drain)
+
+    def drain(self):
+        def body(distance):
+            self.k_step(distance, True)
+            self.a_step(distance, True)
+            self.z_step(distance, True)
+            self.line(distance, True)
+        loop(NZ, body)
+        self.square(True)
+
+
+def scatter_kernel(terms_in, terms_out, out_in, out_out, *rest):
+    place = Place()
+    greet(place)
+    arrays = [Scatter(place, array, (terms_in, terms_out)[array], *rest[4 * array : 4 * array + 4], rest[8 + 7 * array : 15 + 7 * array])
+              for array in range(2)]
+    order = arrays[::-1]
+
+    def begin(index):
+        for array in order:
+            array.start(NZ - 1 - index)
+    loop(NZ, begin)
+
+    def body(index):
+        distance = NZ - 1 - index
+        for array in order:
+            array.k_step(distance)
+        for array in order:
+            array.line(distance + 1)
+        for array in order:
+            array.a_step(distance + 1)
+        for array in order:
+            array.b_step(distance + 2)
+            array.z_step(distance + 2)
+    loop(NZ + 2, body)
+    for array in order:
+        array.square()
+    for array, out in zip(arrays, (out_in, out_out)):
+        number = number_of((place.x, place.y, place.z))
+
+        def last(step):
+            part = pl.ds(pl.multiple_of(step * 16, 16), 16)
+            out[part, :] = array.held[number, part, :].astype(jnp.float32)
+        loop(out.shape[0] // 16, last)
+    for array in order:
+        array.drain()
+
+
+def scatter_terms(terms_in, terms_out):
+    any_space = pl.BlockSpec(memory_space=pl.ANY)
+    vmem = pl.BlockSpec(memory_space=pltpu.VMEM)
+    dma = pltpu.SemaphoreType.DMA
+    buffers, sems = [], []
+    for array in range(2):
+        buffers += [pltpu.VMEM((16,) + BLOCK[array], jnp.bfloat16)] * 2
+        buffers += [pltpu.VMEM((2, 20) + PART[array], jnp.bfloat16), pltpu.VMEM((35,) + REST[array], jnp.bfloat16)]
+        sems += [dma((2, 20)), dma((2, 20)), dma((35,)), dma((35,)), dma((16,)), dma((16,)), dma((16,))]
+    return pl.pallas_call(
+        scatter_kernel,
+        out_shape=tuple(jax.ShapeDtypeStruct(block, jnp.float32) for block in BLOCK),
+        in_specs=[any_space] * 2, out_specs=(vmem,) * 2,
+        scratch_shapes=buffers + sems,
+        compiler_params=pltpu.CompilerParams(collective_id=1, has_side_effects=True, vmem_limit_bytes=58 * 2**20),
+        name="scatter_terms",
+    )(terms_in, terms_out)
 
 
 def gather_all(piece, axis):
@@ -475,8 +693,12 @@
         terms_out[layer] = lax.dot_general(results[6], results[7], contract_rows, preferred_element_type=jnp.bfloat16)
         grad_low = results[0].astype(jnp.bfloat16)
     terms_in, terms_out = jnp.stack(terms_in), jnp.stack(terms_out)
-    own_in = scatter_all(terms_in, 1).astype(jnp.float32)
-    own_out = scatter_all(terms_out, 1).astype(jnp.float32)
+    if blocks_fit:
+        own_in, own_out = scatter_terms(terms_in, terms_out)
+        own_in, own_out = own_in[None], own_out[None]
+    else:
+        own_in = scatter_all(terms_in, 1).astype(jnp.float32)
+        own_out = scatter_all(terms_out, 1).astype(jnp.float32)
     gain_rows = [
         jnp.stack([gain_terms[layer][position] for layer in range(2)]).reshape(2, wide, -1) for position in range(3)
     ]

time: 872 us -> 619 us (0.71)
  waiting for transfers between devices: 382 us -> 0.02 us
  Pallas kernels: 113 us -> 244 us
    reduce_scatter x3 -> x1, waiting for transfers between devices: 224 us -> 0.01 us  [scatter_all(): own = lax.psum_scatter(terms, 'section', scatter_dimension=0, tiled=True)]
    reduce_scatter x2 -> x0, waiting for transfers between devices: 157 us -> none  [scatter_all(): return lax.psum_scatter(own, 'wide', scatter_dimension=axis, tiled=True)]
    pallas_call x0 -> x1, Pallas kernels: none -> 130 us  [scatter_terms(): pl.pallas_call(scatter_kernel, out_shape=tuple((jax.ShapeDtypeStruct(bloc...]
  transfers between devices with their start and end apart: 7 -> 3, of which waited for: 5 -> 0; matrix products, arithmetic and copies ran while one was open for 13% -> 29% of each run, Pallas kernels for 0% -> 21%
where the time goes in v2:
time: 619 us; the launch traced here: 610 us
  Pallas kernels  244 us (39%)
  matrix products  150 us (24%)
  other arithmetic  106 us (17%)
  local copies, waits for them, and re-layouts  46.3 us (7%)
  blocking collectives  46 us (7%)
  between operations  15.9 us (3%)
    pallas_call x1, Pallas kernels, scatter_terms(): pl.pallas_call(scatter_kernel, out_shape=tuple((jax.ShapeDtypeStruct(bloc...  130 us
    pallas_call x1, Pallas kernels, gather_weights(): pl.pallas_call(gather_kernel, out_shape=(jax.ShapeDtypeStruct((2, 768, 53...  113 us
    another operation x8, other arithmetic  46.5 us
    unnamed x1, blocking collectives  22.9 us
    convert_element_type x2, other arithmetic, attend_backward(): grad_scores = grad_scores.astype(jnp.bfloat16)  20.9 us
    dot_general x2, matrix products, layer_backward(): lax.dot_general(grad_projected, weights[0], contract_last, preferred_elem...  19.4 us
    all_gather x1, blocking collectives, gather_all(): lax.all_gather(piece, 'wide', axis=axis, tiled=True)  18.7 us
    dot_general x2, matrix products, attend_backward(): jnp.einsum('qhd,khd->hqk', grad_out, values, preferred_element_type=jnp.f...  18.3 us
  transfers between devices with their start and end apart: 3, of which 0 were waited for; matrix products, arithmetic and copies ran while one was open for 29% of the time, Pallas kernels for 21%

profile of v2, /device:TPU:8, one launch (start us, length us, event | category | flops | bytes accessed | tf_op | source)
XLA Modules:
  0.0 609.5 jit_solution(17378893358409878273)
XLA Ops:
  8.0 18.7 %all-gather.2 = bf16[16,1,56]{2,1,0:T(2,128)(2,1)S(1)} all-gather(bf16[1,1,56]{2,1,0:T(2,128)(2,1)S(1)} %maximum_bitcast_fusion), channel_id=2, replica_groups=mesh['section'=2,'wide'=16] {'wide'}, dimensions={0}, use_global_device_ids=true | all-gather | bytes 1904 | tf_op jit(solution)/shard_map/all_gather | solution.py:651
  26.7 4.3 all-gather.1
  34.0 113.1 %gather_weights.1 = (bf16[2,768,5376]{2,1,0:T(8,128)(2,1)}, bf16[2,3840,768]{2,1,0:T(8,128)(2,1)}) custom-call(bf16[48,5376]{1,0:T(8,128)(2,1)} %bitcast.267, bf16[240,768]{1,0:T(8,128)(2,1)} %bitcast.268), custom_call_target="tpu_custom_call" | custom-call | tf_op jit(solution)/shard_map/gather_weights/pallas_call | solution.py:422
  147.1 7.2 %fusion.10 = f32[512,5376]{1,0:T(8,128)S(1)} fusion(bf16[2,768,5376]{2,1,0:T(8,128)(2,1)} %get-tuple-element.92, f32[768]{0:T(1024)S(1)} %reshape.1010, f32[512]{0:T(512)S(1)} %fusion.118, f32[512]{0:T(512)S(1)} %broadcast_multiply_fusion.5, bf16[2,1,512,768]{3,2,1,0:T(8,128)(2,1)} %param.9, s32[]{:T(128)S(6)} %select_n.81), kind=kOutput, calls=%fused_computation.28 | convolution fusion | flops 4229824512 | bytes 20061188 | tf_op jit(solution)/shard_map/dot_general | solution.py:82
  154.4 15.4 %multiply_convert_fusion.3 = (bf16[512,3072]{1,0:T(8,128)(2,1)}, f32[512,3072]{1,0:T(8,128)}) fusion(f32[512,5376]{1,0:T(8,128)S(1)} %fusion.10), kind=kLoop, calls=%fused_computation.55 | loop fusion | flops 102236160 | bytes 15728640 | tf_op jit(solution)/shard_map/convert.32
  177.0 3.4 fusion.149
  182.3 2.7 copy-done.2
  185.1 2.4 fusion.95
  187.9 7.1 %convert_reduce_fusion.1 = (f32[512]{0:T(512)S(1)}, bf16[512,768]{1,0:T(8,128)(2,1)S(1)}) fusion(bf16[2,3840,768]{2,1,0:T(8,128)(2,1)} %get-tuple-element.93, bf16[512,3072]{1,0:T(8,128)(2,1)} %get-tuple-element.134, bf16[512,768]{1,0:T(8,128)(2,1)S(1)} %copy.116, bf16[2,1,512,768]{3,2,1,0:T(8,128)(2,1)S(1)} %copy-done.21, s32[]{:T(128)S(6)} %select_n.81), kind=kOutput, calls=%fused_computation.105 | convolution fusion | flops 3029728768 | bytes 11405316 | tf_op jit(solution)/shard_map/dot_general | solution.py:681
  195.4 7.2 %fusion.6 = f32[512,5376]{1,0:T(8,128)S(1)} fusion(bf16[2,768,5376]{2,1,0:T(8,128)(2,1)} %get-tuple-element.92, bf16[512,768]{1,0:T(8,128)(2,1)S(1)} %get-tuple-element.164, f32[768]{0:T(1024)S(1)} %reshape.1013, f32[512]{0:T(512)S(1)} %fusion.119, f32[512]{0:T(512)S(1)} %broadcast_multiply_fusion.4), kind=kOutput, calls=%fused_computation.24 | convolution fusion | flops 4229824512 | bytes 20061184 | tf_op jit(solution)/shard_map/dot_general | solution.py:82
  205.0 5.5 fusion.36
  210.5 15.8 %add_convert_fusion.1 = (bf16[512,3072]{1,0:T(8,128)(2,1)}, f32[512,3072]{1,0:T(8,128)S(1)}) fusion(f32[512,3840]{1,0:T(8,128)S(1)} %fusion.36, f32[512,5376]{1,0:T(8,128)S(1)} %fusion.6), kind=kLoop, calls=%fused_computation.40 | loop fusion | flops 113246208 | bytes 22020096 | tf_op jit(solution)/shard_map/convert.20
  226.4 2.8 multiply_convert_fusion.2
  229.2 2.3 copy.117
  235.0 4.3 fusion.150
  241.2 2.7 copy-done.3
  243.9 3.4 fusion.94
  247.3 2.3 copy.123
  249.6 8.8 %select_bitcast_fusion.2 = (bf16[1,1,1,512,768]{4,3,2,1,0:T(8,128)(2,1)}, bf16[1,512,768]{2,1,0:T(8,128)(2,1)}) fusion(bf16[512,768]{1,0:T(8,128)(2,1)} %copy-done.14, pred[]{:T(512)S(6)} %eq.76, bf16[2,3840,768]{2,1,0:T(8,128)(2,1)} %get-tuple-element.93, bf16[512,3072]{1,0:T(8,128)(2,1)} %multiply_convert_fusion.2, bf16[512,768]{1,0:T(8,128)(2,1)} %copy.123), kind=kOutput, calls=%fused_computation.190 | convolution fusion | flops 3029729280 | bytes 12189697 | tf_op jit(solution)/shard_map/dot_general | solution.py:681
  260.0 2.4 slice.206
  262.4 2.3 copy.124
  264.7 7.9 %fusion.88 = bf16[12,64,512]{2,1,0:T(8,128)(2,1)} fusion(bf16[512,12,64]{0,2,1:T(8,128)(2,1)} %bitcast.249, f32[12,512,512]{1,2,0:T(8,128)} %copy-done.3, f32[12,512]{1,0:T(8,128)S(1)} %log_add_fusion.1), kind=kOutput, calls=%fused_computation.175 | convolution fusion | flops 409337856 | bytes 14180352 | tf_op jit(solution)/shard_map/while/body/eval_jaxpr/hqk,qhd->khd/dot_general | solution.py:57
  272.6 8.7 %multiply_reduce_fusion.1 = (f32[12,512]{1,0:T(8,128)S(1)}, f32[12,512,512]{1,2,0:T(8,128)}) fusion(f32[12,512,512]{1,2,0:T(8,128)} %copy-done.3, f32[12,512]{1,0:T(8,128)S(1)} %log_add_fusion.1, bf16[512,12,64]{0,2,1:T(8,128)(2,1)S(1)} %bitcast.250, bf16[512,12,64]{0,2,1:T(8,128)(2,1)S(1)} %bitcast.256), kind=kOutput, calls=%fused_computation.5 | convolution fusion | flops 412084224 | bytes 26787840 | tf_op jit(solution)/shard_map/while/body/eval_jaxpr/qhd,khd->hqk/dot_general | solution.py:63
  281.3 2.3 copy.130
  283.6 10.1 %multiply_convert_fusion.1 = bf16[12,512,512]{1,2,0:T(8,128)(2,1)S(1)} fusion(f32[12,512,512]{1,2,0:T(8,128)} %get-tuple-element.168, f32[12,512,512]{1,2,0:T(8,128)} %copy-done.3, f32[12,512]{1,0:T(8,128)S(1)} %get-tuple-element.167, f32[12,512]{1,0:T(8,128)S(1)} %log_add_fusion.1), kind=kLoop, calls=%fused_computation.4 | loop fusion | flops 12582912 | bytes 31506432 | tf_op jit(solution)/shard_map/while/body/eval_jaxpr/convert_element_type | solution.py:67
  293.7 2.1 fusion.82
  297.3 2.1 fusion.76
  300.8 2.4 copy.129
  305.5 9.6 %fusion.68 = (f32[512]{0:T(512)S(1)}, f32[512,768]{1,0:T(8,128)S(1)}) fusion(bf16[512,768]{1,0:T(8,128)(2,1)S(1)} %copy-done.15, f32[768]{0:T(1024)S(1)} %reshape.1013, f32[512]{0:T(512)S(1)} %broadcast_multiply_fusion.4, bf16[2,768,5376]{2,1,0:T(8,128)(2,1)} %get-tuple-element.92, bf16[512,3072]{1,0:T(8,128)(2,1)} %get-tuple-element.132, ...), kind=kOutput, calls=%fused_computation.126 | convolution fusion | flops 4251844096 | bytes 16129024 | tf_op jit(solution)/shard_map/dot_general | solution.py:153
  316.6 6.3 %fusion.40 = f32[512,3840]{1,0:T(8,128)S(1)} fusion(bf16[2,3840,768]{2,1,0:T(8,128)(2,1)} %get-tuple-element.93, f32[512,768]{1,0:T(8,128)S(1)} %add_add_fusion.7), kind=kOutput, calls=%fused_computation.80 | convolution fusion | flops 3020292096 | bytes 15335424 | tf_op jit(solution)/shard_map/dot_general | solution.py:130
  322.9 3.1 copy-done.17
  326.4 6.8 %fusion.91 = bf16[12,64,512]{2,1,0:T(8,128)(2,1)S(1)} fusion(bf16[512,12,64]{0,2,1:T(8,128)(2,1)S(1)} %bitcast.251, f32[12,512,512]{1,2,0:T(8,128)} %copy-done.2, f32[12,512]{1,0:T(8,128)S(1)} %log_add_fusion), kind=kOutput, calls=%fused_computation.176 | convolution fusion | flops 409337856 | bytes 14180352 | tf_op jit(solution)/shard_map/while/body/eval_jaxpr/hqk,qhd->khd/dot_general | solution.py:57
  333.3 9.6 %multiply_reduce_fusion = (f32[12,512]{1,0:T(8,128)S(1)}, f32[12,512,512]{1,2,0:T(8,128)}) fusion(f32[12,512,512]{1,2,0:T(8,128)} %copy-done.2, f32[12,512]{1,0:T(8,128)S(1)} %log_add_fusion, bf16[512,12,64]{0,2,1:T(8,128)(2,1)S(1)} %bitcast.252, bf16[512,12,64]{0,2,1:T(8,128)(2,1)S(1)} %bitcast.254), kind=kOutput, calls=%fused_computation.2 | convolution fusion | flops 412084224 | bytes 26787840 | tf_op jit(solution)/shard_map/while/body/eval_jaxpr/qhd,khd->hqk/dot_general | solution.py:63
  343.0 6.1 add_convert_fusion
  350.2 10.8 %multiply_convert_fusion = bf16[12,512,512]{1,2,0:T(8,128)(2,1)S(1)} fusion(f32[12,512,512]{1,2,0:T(8,128)} %get-tuple-element.176, f32[12,512,512]{1,2,0:T(8,128)} %copy-done.2, f32[12,512]{1,0:T(8,128)S(1)} %get-tuple-element.175, f32[12,512]{1,0:T(8,128)S(1)} %log_add_fusion), kind=kLoop, calls=%fused_computation.1 | loop fusion | flops 12582912 | bytes 31506432 | tf_op jit(solution)/shard_map/while/body/eval_jaxpr/convert_element_type | solution.py:67
  361.1 2.1 fusion.80
  366.1 2.3 copy.136
  368.4 4.2 fusion.81
  376.4 9.8 %fusion.64 = (f32[768]{0:T(1024)S(1)}, f32[512]{0:T(512)S(1)}, f32[512,768]{1,0:T(8,128)S(1)}) fusion(f32[512]{0:T(512)S(1)} %copy-done.54, f32[512]{0:T(512)S(1)} %copy-done.60, bf16[2,1,512,768]{3,2,1,0:T(8,128)(2,1)S(1)} %copy-done.22, s32[]{:T(128)S(6)} %select_n.81, f32[768]{0:T(1024)S(1)} %copy-done.58, bf16[2,768,5376]{2,1,0:T(8,128)(2,1)} %get-tuple-element.92, ...), kind=kOutput, calls=%fused_computation.122 | convolution fusion | flops 4253022976 | bytes 16134148 | tf_op jit(solution)/shard_map/dot_general | solution.py:153
  390.5 7.8 %convolution_bitcast_fusion = bf16[1,768,5376]{2,1,0:T(8,128)(2,1)S(1)} fusion(bf16[512,3072]{1,0:T(8,128)(2,1)} %get-tuple-element.132, bf16[512,768]{1,0:T(8,128)(2,1)} %copy.130, bf16[512,768]{1,0:T(8,128)(2,1)} %copy.129, bf16[512,768]{1,0:T(8,128)(2,1)} %copy-done.38, bf16[512,768]{1,0:T(8,128)(2,1)} %copy-done.14, f32[768]{0:T(1024)S(1)} %reshape.1013, ...), kind=kOutput, calls=%fused_computation.20 | convolution fusion | flops 4251844608 | bytes 14556160 | tf_op jit(solution)/shard_map/dot_general | solution.py:692
  398.3 10.5 %convolution_bitcast_fusion.1 = bf16[1,768,5376]{2,1,0:T(8,128)(2,1)} fusion(bf16[512,3072]{1,0:T(8,128)(2,1)} %add_convert_fusion, bf16[512,768]{1,0:T(8,128)(2,1)} %copy.137, bf16[512,768]{1,0:T(8,128)(2,1)} %copy.136, bf16[512,768]{1,0:T(8,128)(2,1)} %copy-done.39, f32[512]{0:T(512)S(1)} %copy-done.54, f32[512]{0:T(512)S(1)} %copy-done.60, ...), kind=kOutput, calls=%fused_computation.21 | convolution fusion | flops 4251844608 | bytes 14557188 | tf_op jit(solution)/shard_map/dot_general | solution.py:692
  408.8 8.0 %convolution_bitcast_fusion.2 = bf16[1,3840,768]{2,1,0:T(8,128)(2,1)} fusion(bf16[512,3072]{1,0:T(8,128)(2,1)} %multiply_convert_fusion.2, bf16[512,768]{1,0:T(8,128)(2,1)S(1)} %copy-done.37, bf16[2,1,512,768]{3,2,1,0:T(8,128)(2,1)} %param.10, s32[]{:T(128)S(6)} %select_n.81), kind=kOutput, calls=%fused_computation.72 | convolution fusion | flops 3027763200 | bytes 10616836 | tf_op jit(solution)/shard_map/dot_general | solution.py:693
  416.8 5.3 convolution_bitcast_fusion.3
  422.1 8.3 %pad_maximum_fusion.terms_in = bf16[2,768,5376]{2,1,0:T(8,128)(2,1)} fusion(bf16[1,768,5376]{2,1,0:T(8,128)(2,1)S(1)} %convolution_bitcast_fusion, bf16[1,768,5376]{2,1,0:T(8,128)(2,1)S(1)} %bitcast.248), kind=kLoop, calls=%fused_computation | loop fusion | flops 8257536 | bytes 33030144 | tf_op jit(solution)/shard_map/stack | solution.py:695
  432.2 5.4 pad_maximum_fusion.1.terms_out
  439.0 130.5 %scatter_terms.1 = (f32[48,5376]{1,0:T(8,128)}, f32[240,768]{1,0:T(8,128)}) custom-call(bf16[2,768,5376]{2,1,0:T(8,128)(2,1)} %pad_maximum_fusion.terms_in, bf16[2,3840,768]{2,1,0:T(8,128)(2,1)} %pad_maximum_fusion.1.terms_out), custom_call_target="tpu_custom_call" | custom-call | tf_op jit(solution)/shard_map/scatter_terms/pallas_call | solution.py:640
  570.1 22.9 %all-reduce = f32[1,16,56]{2,1,0:T(8,128)S(1)} all-reduce(f32[1,16,56]{2,1,0:T(8,128)} %reduce-scatter.3.cloned.1.call-done), channel_id=5, replica_groups=mesh['section'=2,'wide'=16] {'wide'}, use_global_device_ids=true, to_apply=%region_37.38.clone | all-reduce | flops 896 | bytes 7168
  594.3 2.8 maximum_select_fusion.1
  (246 shorter events, 51.6 us)
Async XLA Ops:
  7.2 169.5 %copy-start = (s32[2,1,512]{2,1,0:T(1,128)S(1)}, s32[2,1,512]{2,1,0:T(1,128)}, u32[]{:S(2)}) copy-start(s32[2,1,512]{2,1,0:T(1,128)} %param.12) | copy-start | bytes 12292
  7.2 562.9 %reduce-scatter.3.cloned.1.call-start = ((), (), s32[]{:S(2)}) async-start(), calls=%async_computation.1 | async-start | bytes 24576 | tf_op jit(solution)/shard_map/reduce_scatter | solution.py:655
  31.1 123.2 %copy-start.57 = (f32[768]{0:T(1024)}, f32[768]{0:T(1024)S(1)}, u32[]{:S(2)}) copy-start(f32[768]{0:T(1024)S(1)} %reshape.1010) | copy-start | bytes 9220
  32.5 121.9 %copy-start.53 = (f32[512]{0:T(512)}, f32[512]{0:T(512)S(1)}, u32[]{:S(2)}) copy-start(f32[512]{0:T(512)S(1)} %broadcast_multiply_fusion.5) | copy-start | bytes 6148
  34.0 120.4 %copy-start.55 = (f32[512]{0:T(512)}, f32[512]{0:T(512)S(1)}, u32[]{:S(2)}) copy-start(f32[512]{0:T(512)S(1)} %fusion.75) | copy-start | bytes 6148
  34.0 120.4 %copy-start.59 = (f32[512]{0:T(512)}, f32[512]{0:T(512)S(1)}, u32[]{:S(2)}) copy-start(f32[512]{0:T(512)S(1)} %fusion.118) | copy-start | bytes 6148
  154.4 15.5 %copy-start.9 = (f32[512,5376]{1,0:T(8,128)}, f32[512,5376]{1,0:T(8,128)S(1)}, u32[]{:S(2)}) copy-start(f32[512,5376]{1,0:T(8,128)S(1)} %fusion.10) | copy-start | bytes 33030148
  174.2 6.3 %copy-start.44 = (f32[512,12]{0,1:T(8,128)}, f32[512,12]{0,1:T(8,128)S(1)}, u32[]{:S(2)}) copy-start(f32[512,12]{0,1:T(8,128)S(1)} %fusion.115) | copy-start | bytes 73732
  180.5 4.6 copy-start.2
  180.5 4.6 copy-start.25
  187.8 7.2 %copy-start.35 = (bf16[512,768]{1,0:T(8,128)(2,1)}, bf16[512,768]{1,0:T(8,128)(2,1)S(1)}, u32[]{:S(2)}) copy-start(bf16[512,768]{1,0:T(8,128)(2,1)S(1)} %copy.116) | copy-start | bytes 2359300
  195.0 7.6 %copy-start.14 = (bf16[512,768]{1,0:T(8,128)(2,1)}, bf16[512,768]{1,0:T(8,128)(2,1)S(1)}, u32[]{:S(2)}) copy-start(bf16[512,768]{1,0:T(8,128)(2,1)S(1)} %get-tuple-element.164) | copy-start | bytes 2359300
  210.5 15.9 %copy-start.16 = (f32[512,3840]{1,0:T(8,128)}, f32[512,3840]{1,0:T(8,128)S(1)}, u32[]{:S(2)}) copy-start(f32[512,3840]{1,0:T(8,128)S(1)} %fusion.36) | copy-start | bytes 23592964
  258.4 335.9 %collective-permute-start = (bf16[1,512,768]{2,1,0:T(8,128)(2,1)}, bf16[1,512,768]{2,1,0:T(8,128)(2,1)}, u32[]{:S(2)}, u32[]{:S(2)}) collective-permute-start(bf16[1,512,768]{2,1,0:T(8,128)(2,1)} %get-tuple-element.152), channel_id=1, source_target_pairs={{0,16},{16,0},{1,17},{17,1},{2,18},{18,2},{3,19},{19,3},{4,20},{20... | collective-permute-start | bytes 2359304 | tf_op jit(solution)/shard_map/ppermute | solution.py:710
  264.7 7.9 %copy-start.13 = (bf16[512,768]{0,1:T(8,128)(2,1)S(1)}, bf16[512,768]{0,1:T(8,128)(2,1)}, u32[]{:S(2)}) copy-start(bf16[512,768]{0,1:T(8,128)(2,1)} %copy.124) | copy-start | bytes 2359300
  264.7 7.9 %copy-start.28 = (bf16[512,768]{0,1:T(8,128)(2,1)S(1)}, bf16[512,768]{0,1:T(8,128)(2,1)}, u32[]{:S(2)}) copy-start(bf16[512,768]{0,1:T(8,128)(2,1)} %copy.117) | copy-start | bytes 2359300
  300.8 4.7 copy-start.15
  305.5 9.7 %copy-start.38 = (bf16[512,768]{1,0:T(8,128)(2,1)}, bf16[512,768]{1,0:T(8,128)(2,1)S(1)}, u32[]{:S(2)}) copy-start(bf16[512,768]{1,0:T(8,128)(2,1)S(1)} %copy.128) | copy-start | bytes 2359300
  305.5 10.5 %copy-start.47 = (bf16[2,1,512,768]{3,2,1,0:T(8,128)(2,1)S(1)}, bf16[2,1,512,768]{3,2,1,0:T(8,128)(2,1)}, u32[]{:S(2)}) copy-start(bf16[2,1,512,768]{3,2,1,0:T(8,128)(2,1)} %param.10) | copy-start | bytes 4718596
  316.6 6.3 %copy-start.10 = (f32[512,768]{1,0:T(8,128)}, f32[512,768]{1,0:T(8,128)S(1)}, u32[]{:S(2)}) copy-start(f32[512,768]{1,0:T(8,128)S(1)} %add_add_fusion.7) | copy-start | bytes 4718596
  326.4 6.9 %copy-start.26 = (bf16[512,768]{0,1:T(8,128)(2,1)S(1)}, bf16[512,768]{0,1:T(8,128)(2,1)}, u32[]{:S(2)}) copy-start(bf16[512,768]{0,1:T(8,128)(2,1)} %copy.110) | copy-start | bytes 2359300
  326.4 16.5 %slice-start = ((s8[6291456]{0:T(1024)(128)(4,1)}), s8[4194304]{0:T(1024)(128)(4,1)S(1)}, s32[]{:S(2)}) async-start(s8[6291456]{0:T(1024)(128)(4,1)} %bitcast.243), calls=%async_computation.2 | async-start | bytes 8388608
  326.4 16.5 %slice-start.2 = ((s8[11010048]{0:T(1024)(128)(4,1)}), s8[4194304]{0:T(1024)(128)(4,1)S(1)}, s32[]{:S(2)}) async-start(s8[11010048]{0:T(1024)(128)(4,1)} %bitcast.245), calls=%async_computation.4 | async-start | bytes 8388608
  326.4 16.5 %slice-start.3 = ((s8[11010048]{0:T(1024)(128)(4,1)}), s8[4194304]{0:T(1024)(128)(4,1)S(1)}, s32[]{:S(2)}) async-start(s8[11010048]{0:T(1024)(128)(4,1)} %bitcast.245), calls=%async_computation.5 | async-start | bytes 8388608
  333.3 9.7 %slice-start.1 = ((s8[6291456]{0:T(1024)(128)(4,1)}), s8[2097152]{0:T(1024)(128)(4,1)S(1)}, s32[]{:S(2)}) async-start(s8[6291456]{0:T(1024)(128)(4,1)} %bitcast.243), calls=%async_computation.3 | async-start | bytes 4194304
  333.3 9.7 %slice-start.4 = ((s8[11010048]{0:T(1024)(128)(4,1)}), s8[2621440]{0:T(1024)(128)(4,1)S(1)}, s32[]{:S(2)}) async-start(s8[11010048]{0:T(1024)(128)(4,1)} %bitcast.245), calls=%async_computation.6 | async-start | bytes 5242880
  350.2 10.8 %copy-start.5 = (f32[512,768]{0,1:T(8,128)S(1)}, f32[512,768]{0,1:T(8,128)}, u32[]{:S(2)}) copy-start(f32[512,768]{0,1:T(8,128)} %copy-done.4) | copy-start | bytes 4718596
  350.2 10.8 %copy-start.7 = (f32[512,768]{0,1:T(8,128)S(1)}, f32[512,768]{0,1:T(8,128)}, u32[]{:S(2)}) copy-start(f32[512,768]{0,1:T(8,128)} %copy-done.6) | copy-start | bytes 4718596
  350.2 10.8 %copy-start.31 = (f32[512,12]{0,1:T(8,128)S(1)}, f32[512,12]{0,1:T(8,128)}, u32[]{:S(2)}) copy-start(f32[512,12]{0,1:T(8,128)} %copy-done.30) | copy-start | bytes 73732
  350.2 10.8 %copy-start.33 = (f32[512,12]{0,1:T(8,128)S(1)}, f32[512,12]{0,1:T(8,128)}, u32[]{:S(2)}) copy-start(f32[512,12]{0,1:T(8,128)} %copy-done.32) | copy-start | bytes 73732
  350.2 10.8 %copy-start.43 = (f32[512,12]{0,1:T(8,128)S(1)}, f32[512,12]{0,1:T(8,128)}, u32[]{:S(2)}) copy-start(f32[512,12]{0,1:T(8,128)} %copy-done.42) | copy-start | bytes 73732
  376.4 9.8 %copy-start.39 = (bf16[512,768]{1,0:T(8,128)(2,1)}, bf16[512,768]{1,0:T(8,128)(2,1)S(1)}, u32[]{:S(2)}) copy-start(bf16[512,768]{1,0:T(8,128)(2,1)S(1)} %copy.135) | copy-start | bytes 2359300
  376.4 9.8 %copy-start.56 = (f32[512]{0:T(512)S(1)}, f32[512]{0:T(512)}, u32[]{:S(2)}) copy-start(f32[512]{0:T(512)} %copy-done.55) | copy-start | bytes 6148
  376.4 9.8 %copy-start.23 = (bf16[2,1,512,768]{3,2,1,0:T(8,128)(2,1)S(1)}, bf16[2,1,512,768]{3,2,1,0:T(8,128)(2,1)}, u32[]{:S(2)}) copy-start(bf16[2,1,512,768]{3,2,1,0:T(8,128)(2,1)} %param.9) | copy-start | bytes 4718596
  388.7 208.4 %collective-permute-start.1 = (bf16[1,512,768]{2,1,0:T(8,128)(2,1)}, bf16[1,512,768]{2,1,0:T(8,128)(2,1)}, u32[]{:S(2)}, u32[]{:S(2)}) collective-permute-start(bf16[1,512,768]{2,1,0:T(8,128)(2,1)} %fusion.98), channel_id=1, source_target_pairs={{0,16},{16,0},{1,17},{17,1},{2,18},{18,2},{3,19},{19,3},{4,20},{20... | collective-permute-start | bytes 2359304 | tf_op jit(solution)/shard_map/ppermute | solution.py:710
  390.4 7.8 %copy-start.24 = (bf16[2,1,512,768]{3,2,1,0:T(8,128)(2,1)S(1)}, bf16[2,1,512,768]{3,2,1,0:T(8,128)(2,1)}, u32[]{:S(2)}) copy-start(bf16[2,1,512,768]{3,2,1,0:T(8,128)(2,1)} %param.9) | copy-start | bytes 4718596
  398.3 10.5 %copy-start.37 = (bf16[512,768]{1,0:T(8,128)(2,1)S(1)}, bf16[512,768]{1,0:T(8,128)(2,1)}, u32[]{:S(2)}) copy-start(bf16[512,768]{1,0:T(8,128)(2,1)} %copy.123) | copy-start | bytes 2359300
  408.7 8.0 %copy-start.29 = (bf16[512,3072]{1,0:T(8,128)(2,1)S(1)}, bf16[512,3072]{1,0:T(8,128)(2,1)}, u32[]{:S(2)}) copy-start(bf16[512,3072]{1,0:T(8,128)(2,1)} %get-tuple-element.134) | copy-start | bytes 9437188
  408.7 8.0 %copy-start.36 = (bf16[512,768]{1,0:T(8,128)(2,1)S(1)}, bf16[512,768]{1,0:T(8,128)(2,1)}, u32[]{:S(2)}) copy-start(bf16[512,768]{1,0:T(8,128)(2,1)} %copy-done.35) | copy-start | bytes 2359300
  408.7 13.3 %slice-start.5 = ((s8[8257536]{0:T(1024)(128)(4,1)}), s8[4194304]{0:T(1024)(128)(4,1)S(1)}, s32[]{:S(2)}) async-start(s8[8257536]{0:T(1024)(128)(4,1)} %bitcast.247), calls=%async_computation.7 | async-start | bytes 8388608
  416.8 5.3 slice-start.6
  422.1 8.3 %copy-start.19 = (bf16[1,3840,768]{2,1,0:T(8,128)(2,1)S(1)}, bf16[1,3840,768]{2,1,0:T(8,128)(2,1)}, u32[]{:S(2)}) copy-start(bf16[1,3840,768]{2,1,0:T(8,128)(2,1)} %convolution_bitcast_fusion.2) | copy-start | bytes 17694724
  422.1 10.1 %copy-start.20 = (bf16[1,3840,768]{2,1,0:T(8,128)(2,1)S(1)}, bf16[1,3840,768]{2,1,0:T(8,128)(2,1)}, u32[]{:S(2)}) copy-start(bf16[1,3840,768]{2,1,0:T(8,128)(2,1)} %convolution_bitcast_fusion.3) | copy-start | bytes 17694724
  439.0 130.5 %copy-start.63 = (u32[32]{0:T(128)S(1)}, u32[32]{0:T(128)}, u32[]{:S(2)}) copy-start(u32[32]{0:T(128)} %constant.209) | copy-start | bytes 388
  439.0 155.3 %copy-start.40 = (bf16[1,1,1,512,768]{4,3,2,1,0:T(8,128)(2,1)S(1)}, bf16[1,1,1,512,768]{4,3,2,1,0:T(8,128)(2,1)}, u32[]{:S(2)}) copy-start(bf16[1,1,1,512,768]{4,3,2,1,0:T(8,128)(2,1)} %get-tuple-element.140) | copy-start | bytes 2359300
  569.5 29.0 %copy-start.18 = (f32[1,1,1,512,768]{4,3,2,1,0:T(8,128)S(1)}, f32[1,1,1,512,768]{4,3,2,1,0:T(8,128)}, u32[]{:S(2)}) copy-start(f32[1,1,1,512,768]{4,3,2,1,0:T(8,128)} %select_bitcast_fusion) | copy-start | bytes 4718596
  593.7 6.7 %copy-start.61 = (f32[1,56]{1,0:T(1,128)}, f32[1,56]{1,0:T(1,128)S(1)}, u32[]{:S(2)}) copy-start(f32[1,56]{1,0:T(1,128)S(1)} %dynamic-slice_bitcast_fusion) | copy-start | bytes 676
  597.1 5.1 copy-start.1
  (26 other events, 86.1 us)
Sparse Core Ops, SparseCore 0:
  390.6 10.4 reduce-scatter.2

commit v3 on v2

--- a/solution.py
+++ b/solution.py
@@ -2,173 +2,15 @@
 
 import jax
 import jax.numpy as jnp
+import numpy as np
 from jax import lax
 from jax.experimental import pallas as pl
 from jax.experimental.pallas import tpu as pltpu
 from jax.sharding import PartitionSpec as P
 
-HEADS = 12
-HD = 64
-
-
-EPSILON = 1e-06
-NEGATIVE = -1e30
-
-
-def layer_norm(values, gain_vec):
-    average = jnp.mean(values, -1, keepdims=True)
-    centred = values - average
-    variance = jnp.mean(centred * centred, -1, keepdims=True)
-    return centred * lax.rsqrt(variance + EPSILON) * gain_vec
-
-
-def exact_gelu(values):
-    return jax.nn.gelu(values, approximate=False)
-
-
-def head_norms(queries, keys_in, query_gain, key_gain):
-    return (layer_norm(queries, query_gain), layer_norm(keys_in, key_gain))
-
-
-def score_rows(queries, keys_in, image_ids, key_bias):
-    scores = (
-        jnp.einsum("qhd,khd->hqk", queries, keys_in, preferred_element_type=jnp.float32) * 0.125
-        + key_bias[None, None, :]
-    )
-    same_image = image_ids[:, None] == image_ids[None, :]
-    return jnp.where(same_image[None], scores, NEGATIVE)
-
-
-def attend_forward(row_block):
-    queries, keys_in, values, image_ids, key_bias = row_block
-    scores = score_rows(queries, keys_in, image_ids, key_bias)
-    largest = jnp.max(scores, -1, keepdims=True)
-    exponent = jnp.exp(scores - largest)
-    row_total = jnp.sum(exponent, -1, keepdims=True)
-    weights = (exponent / row_total).astype(jnp.bfloat16)
-    output = jnp.einsum("hqk,khd->qhd", weights, values, preferred_element_type=jnp.float32)
-    return (output, largest + jnp.log(row_total))
-
-
-def attend_backward(row_block):
-    queries, keys_in, values, image_ids, key_bias, log_total, grad_out = row_block
-    scores = score_rows(queries, keys_in, image_ids, key_bias)
-    probabilities = jnp.exp(scores - log_total)
-    grad_values = jnp.einsum(
-        "hqk,qhd->khd",
-        probabilities.astype(jnp.bfloat16),
-        grad_out,
-        preferred_element_type=jnp.float32,
-    )
-    grad_probs = jnp.einsum("qhd,khd->hqk", grad_out, values, preferred_element_type=jnp.float32)
-    grad_scores = probabilities * (
-        grad_probs - jnp.sum(probabilities * grad_probs, -1, keepdims=True)
-    )
-    grad_scores = grad_scores.astype(jnp.bfloat16)
-    grad_queries = (
-        jnp.einsum("hqk,khd->qhd", grad_scores, keys_in, preferred_element_type=jnp.float32) * 0.125
-    )
-    grad_keys = (
-        jnp.einsum("hqk,qhd->khd", grad_scores, queries, preferred_element_type=jnp.float32) * 0.125
-    )
-    return (grad_queries, grad_keys, grad_values)
-
-
-def layer_pieces(hidden, weights, image_ids, key_bias):
-    w_in, w_out, ln_gain, q_gain, k_gain = weights
-    row_count, slot_count, model_width = hidden.shape
-    normed, norm_back = jax.vjp(layer_norm, hidden, ln_gain.astype(jnp.float32))
-    normed_low = normed.astype(jnp.bfloat16).reshape(row_count * slot_count, model_width)
-    projected = jnp.dot(normed_low, w_in, preferred_element_type=jnp.float32)
-    head_shape = (row_count, slot_count, HEADS, HD)
-    queries = projected[:, :model_width].reshape(head_shape)
-    keys_in = projected[:, model_width : 2 * model_width].reshape(head_shape)
-    values = (
-        projected[:, 2 * model_width : 3 * model_width].reshape(head_shape).astype(jnp.bfloat16)
-    )
-    normed_heads, norms_back = jax.vjp(
-        head_norms, queries, keys_in, q_gain.astype(jnp.float32), k_gain.astype(jnp.float32)
-    )
-    queries_low = normed_heads[0].astype(jnp.bfloat16)
-    keys_low = normed_heads[1].astype(jnp.bfloat16)
-    attended, log_total = lax.map(
-        attend_forward, (queries_low, keys_low, values, image_ids, key_bias)
-    )
-    activated, gelu_back = jax.vjp(exact_gelu, projected[:, 3 * model_width :])
-    combined = jnp.concatenate(
-        [attended.reshape(row_count * slot_count, model_width), activated], 1
-    ).astype(jnp.bfloat16)
-    return (
-        norm_back,
-        normed_low,
-        norms_back,
-        queries_low,
-        keys_low,
-        values,
-        log_total,
-        gelu_back,
-        combined,
-    )
-
-
-def layer_backward(hidden, grad_low, pieces, weights, image_ids, key_bias):
-    (
-        norm_back,
-        normed_low,
-        norms_back,
-        queries_low,
-        keys_low,
-        values,
-        log_total,
-        gelu_back,
-        combined,
-    ) = pieces
-    row_count, slot_count, model_width = hidden.shape
-    flat_rows = row_count * slot_count
-    grad_flat = grad_low.reshape(flat_rows, model_width)
-    contract_last = (((1,), (1,)), ((), ()))
-    grad_combined = lax.dot_general(
-        grad_flat, weights[1], contract_last, preferred_element_type=jnp.float32
-    )
-    grad_attended = (
-        grad_combined[:, :model_width]
-        .astype(jnp.bfloat16)
-        .reshape(row_count, slot_count, HEADS, HD)
-    )
-    grad_up = gelu_back(grad_combined[:, model_width:])[0]
-    grad_q, grad_k, grad_v = lax.map(
-        attend_backward,
-        (queries_low, keys_low, values, image_ids, key_bias, log_total, grad_attended),
-    )
-    grad_queries, grad_keys, grad_qgain, grad_kgain = norms_back((grad_q, grad_k))
-    grad_projected = jnp.concatenate(
-        [
-            grad_queries.reshape(flat_rows, model_width),
-            grad_keys.reshape(flat_rows, model_width),
-            grad_v.reshape(flat_rows, model_width),
-            grad_up,
-        ],
-        1,
-    ).astype(jnp.bfloat16)
-    grad_normed = lax.dot_general(
-        grad_projected, weights[0], contract_last, preferred_element_type=jnp.float32
-    )
-    grad_hidden, grad_lngain = norm_back(grad_normed.reshape(hidden.shape))
-    return (
-        grad_low.astype(jnp.float32) + grad_hidden,
-        grad_lngain,
-        grad_qgain,
-        grad_kgain,
-        normed_low,
-        grad_projected,
-        combined,
-        grad_flat,
-    )
-
-
 MESH = pl.DeviceIdType.MESH
 NZ = 4
-BLOCK = ((48, 5376), (240, 768))
+BLOCK = ((48, 5376), (240, 768), (16, 128))
 CUT_IN, CUT_OUT = 2176, 96
 PART = ((48, CUT_IN), (CUT_OUT, 768))
 REST = ((48, 5376 - 2 * CUT_IN), (240 - 2 * CUT_OUT, 768))
@@ -222,6 +64,8 @@
 
 def cut(ref, array, colour):
     rows, cols = BLOCK[array]
+    if array == 2:
+        return ref
     if array == 0:
         if colour is None:
             return ref.at[:, pl.ds(2 * CUT_IN, cols - 2 * CUT_IN)]
@@ -294,7 +138,8 @@
 
         def body(colour):
             self.visit(me, colour, everywhere, place.first(colour), place.second(colour), drain, own=True)
-        loop(2, body)
+        if self.array < 2:
+            loop(2, body)
 
     def square(self, drain=False):
         place = self.place
@@ -363,7 +208,7 @@
         def body(number):
             block = (number // 8, (number // 4) % 2, number % 4)
             self.copy(4, place.sibling(), block, None, other_plane=True).wait_recv()
-            for colour in (0, 1):
+            for colour in (0, 1) if self.array < 2 else ():
                 self.copy(4, place.sibling(), block, colour, other_plane=True).wait_recv()
         loop(16, body)
 
@@ -372,30 +217,34 @@
         self.square(True)
 
         def body(index):
-            self.z_step(index + 1, True)
             self.line(index + 1, True)
-            self.a_step(index, True)
-            self.b_step(index, True)
+            if self.array < 2:
+                self.z_step(index + 1, True)
+                self.a_step(index, True)
+                self.b_step(index, True)
         loop(NZ, body)
 
 
-def gather_kernel(w_in, w_out, full_in, full_out, *sems):
+def gather_kernel(w_in, w_out, gains, full_in, full_out, full_gains, *sems):
     place = Place()
     greet(place)
-    first = Gather(place, 0, w_in, full_in, *sems[:3])
-    second = Gather(place, 1, w_out, full_out, *sems[3:6])
+    arrays = ((w_in, full_in), (w_out, full_out), (gains, full_gains))
+    first, second, third = [Gather(place, array, *arrays[array], *sems[3 * array : 3 * array + 3]) for array in range(3)]
     copies = []
-    for array, (own, full) in enumerate(((w_in, full_in), (w_out, full_out))):
+    for array, (own, full) in enumerate(arrays):
         rows = BLOCK[array][0]
-        copy = pltpu.make_async_copy(own, full.at[place.x, pl.ds(pl.multiple_of(place.wide * rows, 16), rows), :], sems[6].at[array])
+        copy = pltpu.make_async_copy(own, full.at[place.x, pl.ds(pl.multiple_of(place.wide * rows, 16), rows), :], sems[9].at[array])
         copy.start()
         copies.append(copy)
+    third.begin()
     first.begin()
+    third.square()
     first.square()
 
     def early(index):
         first.z_step(index + 1)
         first.a_step(index)
+        third.line(index + 1)
         first.line(index + 1)
     loop(NZ, early)
     second.begin()
@@ -408,25 +257,25 @@
         second.line(index + 1)
     loop(NZ, late)
     loop(NZ, second.b_step)
-    first.from_core()
-    second.from_core()
+    for array in (third, first, second):
+        array.from_core()
     for copy in copies:
         copy.wait()
-    first.drain()
-    second.drain()
-
-
-def gather_weights(w_in, w_out):
+    for array in (third, first, second):
+        array.drain()
+
+
+def gather_weights(w_in, w_out, gains):
     any_space = pl.BlockSpec(memory_space=pl.ANY)
     dma = pltpu.SemaphoreType.DMA
     return pl.pallas_call(
         gather_kernel,
-        out_shape=(jax.ShapeDtypeStruct((2, 768, 5376), jnp.bfloat16), jax.ShapeDtypeStruct((2, 3840, 768), jnp.bfloat16)),
-        in_specs=[any_space] * 2, out_specs=(any_space,) * 2,
-        scratch_shapes=[dma((5, 3, 16)), dma((3, 16)), dma((3, 16))] * 2 + [dma((2,))],
+        out_shape=tuple(jax.ShapeDtypeStruct(dims, jnp.bfloat16) for dims in ((2, 768, 5376), (2, 3840, 768), (2, 256, 128))),
+        in_specs=[any_space] * 3, out_specs=(any_space,) * 3,
+        scratch_shapes=[dma((5, 3, 16)), dma((3, 16)), dma((3, 16))] * 3 + [dma((3,))],
         compiler_params=pltpu.CompilerParams(collective_id=0, has_side_effects=True),
         name="gather_weights",
-    )(w_in, w_out)
+    )(w_in, w_out, gains)
 
 
 def add_into(target, source):
@@ -591,9 +440,65 @@
         self.square(True)
 
 
-def scatter_kernel(terms_in, terms_out, out_in, out_out, *rest):
+class Total:
+    def __init__(self, place, own, out, run, land, send_sem, recv_sem):
+        self.place, self.own, self.out, self.run, self.land = place, own, out, run, land
+        self.send_sem, self.recv_sem = send_sem, recv_sem
+        x, y, z = place.x, place.y, place.z
+        self.routes = (place.sibling(), place.at(x, 1 - y, z), place.at(1 - x, y, z), place.at(x, y, z + 1), place.at(x, y, z - 1))
+        self.sends = (None, None, None, z < NZ - 1, z > 0)
+        self.gets = (None, None, None, z > 0, z < NZ - 1)
+
+    def copy(self, link):
+        source = self.own if link == 0 else self.run.at[link]
+        return pltpu.make_async_remote_copy(
+            src_ref=source, dst_ref=self.land.at[link], send_sem=self.send_sem.at[link], recv_sem=self.recv_sem.at[link],
+            device_id=self.routes[link], device_id_type=MESH)
+
+    def step(self, index):
+        def chain(link, base):
+            self.run[link] = base[...]
+
+            def get():
+                self.copy(link).wait_recv()
+                self.run[link] += self.land[link]
+            pl.when(self.gets[link])(get)
+            pl.when(self.sends[link])(lambda: self.copy(link).start())
+
+        def swap(link):
+            if link:
+                self.copy(link - 1).wait_recv()
+                self.run[link] = (self.own[...] if link == 1 else self.run[link - 1]) + self.land[link - 1]
+            if link < 3:
+                self.copy(link).start()
+
+        for link in range(3):
+            pl.when(index == link)(functools.partial(swap, link))
+
+        @pl.when(index == 3)
+        def _():
+            self.copy(2).wait_recv()
+            self.out[...] = self.run[2] + self.land[2]
+            chain(3, self.out)
+            chain(4, self.out)
+            self.out[...] = self.run[3]
+
+            def add():
+                self.out[...] += self.land[4]
+            pl.when(self.gets[4])(add)
+
+    def drain(self):
+        for link, sent in enumerate(self.sends):
+            if sent is None:
+                self.copy(link).wait_send()
+            else:
+                pl.when(sent)(lambda: self.copy(link).wait_send())
+
+
+def scatter_kernel(terms_in, terms_out, gains, out_in, out_out, out_gains, *rest):
     place = Place()
     greet(place)
+    total = Total(place, gains, out_gains, *rest[22:26])
     arrays = [Scatter(place, array, (terms_in, terms_out)[array], *rest[4 * array : 4 * array + 4], rest[8 + 7 * array : 15 + 7 * array])
               for array in range(2)]
     order = arrays[::-1]
@@ -607,6 +512,7 @@
         distance = NZ - 1 - index
         for array in order:
             array.k_step(distance)
+        total.step(index)
         for array in order:
             array.line(distance + 1)
         for array in order:
@@ -626,9 +532,10 @@
         loop(out.shape[0] // 16, last)
     for array in order:
         array.drain()
-
-
-def scatter_terms(terms_in, terms_out):
+    total.drain()
+
+
+def scatter_terms(terms_in, terms_out, gains):
     any_space = pl.BlockSpec(memory_space=pl.ANY)
     vmem = pl.BlockSpec(memory_space=pltpu.VMEM)
     dma = pltpu.SemaphoreType.DMA
@@ -637,14 +544,321 @@
         buffers += [pltpu.VMEM((16,) + BLOCK[array], jnp.bfloat16)] * 2
         buffers += [pltpu.VMEM((2, 20) + PART[array], jnp.bfloat16), pltpu.VMEM((35,) + REST[array], jnp.bfloat16)]
         sems += [dma((2, 20)), dma((2, 20)), dma((35,)), dma((35,)), dma((16,)), dma((16,)), dma((16,))]
+    small = [pltpu.VMEM((5,) + BLOCK[2], jnp.float32)] * 2 + [dma((5,))] * 2
     return pl.pallas_call(
         scatter_kernel,
         out_shape=tuple(jax.ShapeDtypeStruct(block, jnp.float32) for block in BLOCK),
-        in_specs=[any_space] * 2, out_specs=(vmem,) * 2,
-        scratch_shapes=buffers + sems,
+        in_specs=[any_space] * 2 + [vmem], out_specs=(vmem,) * 3,
+        scratch_shapes=buffers + sems + small,
         compiler_params=pltpu.CompilerParams(collective_id=1, has_side_effects=True, vmem_limit_bytes=58 * 2**20),
         name="scatter_terms",
-    )(terms_in, terms_out)
+    )(terms_in, terms_out, gains)
+
+
+SLOTS, D, HD, PAIRS = 512, 768, 64, 6
+WIDE_PAIRS = 3
+TILES_IN, TILES_OUT = 7, 5
+EPSILON = 1e-06
+LOG2E = 1.4426950408889634
+SCALE = 0.125 * LOG2E
+APART = 256.0
+F32, BF16 = jnp.float32, jnp.bfloat16
+ACROSS, DOWN = ((1,), (1,)), ((0,), (0,))
+
+
+def dot(a, b, dims=((1,), (0,))):
+    return lax.dot_general(a, b, (dims, ((), ())), preferred_element_type=F32)
+
+
+def split(value):
+    high = value.astype(BF16)
+    return high, (value - high.astype(F32)).astype(BF16)
+
+
+def head_means(value, spread, exact=True):
+    high, low = split(value)
+    means = dot(high, spread)
+    return means + dot(low, spread) if exact else means
+
+
+def gelu_and_slope(x):
+    t = 1.0 / (1.0 + (0.3275911 * 0.7071067811865476) * jnp.abs(x))
+    bell = jnp.exp2((-0.5 * LOG2E) * (x * x))
+    poly = t * (0.127414796 + t * (-0.142248368 + t * (0.7107068705 + t * (-0.7265760135 + t * 0.5307027145))))
+    tail = poly * bell
+    phi = jnp.where(x >= 0, 1.0 - tail, tail)
+    return x * phi, phi + (0.3989422804014327 * x) * bell
+
+
+def lanes(index, width):
+    return pl.ds(pl.multiple_of(index * width, width), width)
+
+
+PROJECT, OUTPUT, OUTPUT_BACK, BACK, PROJECT_BACK = range(5)
+IN_ORDER = (3, 4, 5, 6, 0, 1, 2)
+
+
+def plan():
+    steps = [(PROJECT, 0, tile) for tile in range(TILES_IN)] + [(OUTPUT, 0, tile) for tile in range(TILES_OUT)]
+    steps += [(PROJECT, 1, tile) for tile in range(TILES_IN)] + [(OUTPUT_BACK, 1, tile) for tile in range(TILES_OUT)]
+    steps += [(PROJECT_BACK, 1, tile) for tile in IN_ORDER]
+    steps += [(BACK, 0, tile) for tile in range(TILES_OUT)] + [(PROJECT_BACK, 0, tile) for tile in IN_ORDER]
+    uses_in = [kind in (PROJECT, PROJECT_BACK) for kind, _, _ in steps]
+    gives_in = [kind == PROJECT_BACK for kind, _, _ in steps]
+    gives_out = [kind in (OUTPUT_BACK, BACK) for kind, _, _ in steps]
+
+    def coming(used):
+        table, now = [], None
+        for step, use in zip(reversed(steps), reversed(used)):
+            now = step[1:] if use else now
+            table.append(now)
+        table = table[::-1]
+        last = [step[1:] for step, use in zip(steps, used) if use][-1]
+        return [last if entry is None else entry for entry in table]
+
+    def given(made):
+        table, now = [], [step[1:] for step, use in zip(steps, made) if use][0]
+        for step, use in zip(steps, made):
+            now = step[1:] if use else now
+            table.append(now)
+        return table
+
+    tables = [coming(uses_in), coming([not use for use in uses_in]), given(gives_in), given(gives_out)]
+    columns = [[step[part] for step in steps] for part in range(3)]
+    columns += [[entry[part] for entry in table] for table in tables for part in range(2)]
+    return np.array(columns, np.int32)
+
+
+def compute_kernel(plan_ref, h_ref, cot_ref, w_in_ref, w_out_ref, ln_ref, qg_ref, kg_ref, augq_ref, augk_ref, spread_ref,
+                   out_ref, grad_ref, gain_ref, terms_in_ref, terms_out_ref,
+                   hidden, normed, scale, q, k, v, rq, rk, linv, slope, combined, dy, dproj, acc, dq, dk, do, dhigh, dlow):
+    t = pl.program_id(0)
+    kind, layer, tile = plan_ref[0, t], plan_ref[1, t], plan_ref[2, t]
+    spread = spread_ref[...]
+
+    def halves(width=256):
+        def run(body):
+            def step(index):
+                body(pl.ds(pl.multiple_of((index % 2) * 256, 256), 256), lanes(index // 2, width))
+            loop(2 * D // width, step)
+        return run
+
+    def by_rows(body):
+        loop(SLOTS // 128, lambda index: body(pl.ds(pl.multiple_of(index * 128, 128), 128)))
+
+    @pl.when(t == 0)
+    def _():
+        hidden[0] = h_ref[...]
+        gain_ref[...] = jnp.zeros_like(gain_ref)
+
+    def low_lanes():
+        return lax.broadcasted_iota(jnp.int32, (SLOTS, 128), 1) < HD
+
+    @pl.when((kind == PROJECT) & (tile == 0))
+    def _():
+        def body(rows):
+            h = hidden[layer, rows, :].astype(F32)
+            centred = h - jnp.mean(h, -1, keepdims=True)
+            root = lax.rsqrt(jnp.mean(centred * centred, -1, keepdims=True) + EPSILON)
+            scale[layer, rows, :] = jnp.broadcast_to(root, (128, 128))
+            normed[layer, rows, :] = (centred * root * ln_ref[layer]).astype(BF16)
+        by_rows(body)
+
+    @pl.when(kind == PROJECT)
+    def _():
+        acc[...] = dot(normed[layer], w_in_ref[...])
+
+        def heads(low_ref, root_ref, gain, factor):
+            @halves()
+            def _(rows, columns):
+                x = acc[rows, columns]
+                centred = x - head_means(x, spread)
+                root = lax.rsqrt(head_means(centred * centred, spread, False) + EPSILON)
+                root_ref[layer, rows, columns] = root.astype(BF16)
+                low_ref[layer, rows, columns] = (centred * root * (gain * factor)).astype(BF16)
+
+        pl.when(tile == 0)(lambda: heads(q, rq, qg_ref[layer], SCALE))
+        pl.when(tile == 1)(lambda: heads(k, rk, kg_ref[layer], 1.0))
+
+        @pl.when(tile == 2)
+        def _():
+            v[layer] = acc[...].astype(BF16)
+            low = low_lanes()
+            augq, augk = augq_ref[...], augk_ref[...]
+            ones = jnp.ones((SLOTS, 128), BF16)
+
+            def pair(index):
+                part = lanes(index, 128)
+                qp, kp, vp = q[layer, :, part], k[layer, :, part], v[layer, :, part]
+                results = []
+                for head in (0, 1):
+                    mine = low if head == 0 else ~low
+                    scores = dot(jnp.where(mine, qp, augq), jnp.where(mine, kp, augk), ACROSS)
+                    results.append(dot(jnp.exp2(scores).astype(BF16), jnp.where(mine, vp, ones)))
+                inverse = 1.0 / pltpu.roll(jnp.where(low, results[1], results[0]), HD, 1)
+                linv[layer, :, part] = inverse
+                combined[layer, 0, :, part] = (jnp.where(low, results[0], results[1]) * inverse).astype(BF16)
+            loop(PAIRS, pair)
+
+        @pl.when(tile > 2)
+        def _():
+            @halves()
+            def _(rows, columns):
+                value, rise = gelu_and_slope(acc[rows, columns])
+                slope[layer, tile - 3, rows, columns] = rise.astype(BF16)
+                combined[layer, tile - 2, rows, columns] = value.astype(BF16)
+
+    @pl.when((kind == OUTPUT) | (kind == OUTPUT_BACK))
+    def _():
+        product = dot(combined[layer, tile], w_out_ref[...])
+        pl.when(tile == 0)(lambda: dq.__setitem__(..., hidden[layer].astype(F32) + product))
+        pl.when(tile > 0)(lambda: dq.__setitem__(..., dq[...] + product))
+
+        @pl.when(tile == TILES_OUT - 1)
+        def _():
+            result = dq[...].astype(BF16)
+            out_ref[layer] = result
+            pl.when(layer == 0)(lambda: hidden.__setitem__(1, result))
+
+    @pl.when((kind == OUTPUT_BACK) & (tile == 0))
+    def _():
+        dy[...] = cot_ref[...]
+
+    @pl.when((kind == OUTPUT_BACK) | (kind == BACK))
+    def _():
+        acc[...] = dot(dy[...], w_out_ref[...], ACROSS)
+        terms_out_ref[...] = dot(combined[layer, tile], dy[...], DOWN).astype(BF16)
+
+        @pl.when(tile == 0)
+        def _():
+            @halves()
+            def _(rows, columns):
+                grad, inverse = acc[rows, columns], linv[layer, rows, columns]
+                do[rows, columns] = (grad * inverse).astype(BF16)
+                total = head_means(grad * combined[layer, 0, rows, columns].astype(F32), spread) * (inverse * -HD)
+                for half in (0, 128):
+                    part = pl.ds(pl.multiple_of(columns.start + half, 128), 128)
+                    high, low = split(pltpu.roll(total[:, half : half + 128], HD, 1))
+                    dhigh[rows, part] = high
+                    dlow[rows, part] = low
+
+        @pl.when(tile > 0)
+        def _():
+            @halves()
+            def _(rows, columns):
+                dproj[tile + 2, rows, columns] = (acc[rows, columns] * slope[layer, tile - 1, rows, columns].astype(F32)).astype(BF16)
+
+    @pl.when((kind == PROJECT_BACK) & (tile == 0))
+    def _():
+        low = low_lanes()
+        spot = lax.broadcasted_iota(jnp.int32, (SLOTS, 128), 1) % HD
+        first = spot == 0
+        augv = jnp.where(spot < 2, 1.0, 0.0).astype(BF16)
+        augq, augk = augq_ref[...], augk_ref[...]
+        none = jnp.zeros((SLOTS, 128), BF16)
+
+        def pair(index):
+            part = lanes(index, 128)
+            qp, kp, vp, dop = q[layer, :, part], k[layer, :, part], v[layer, :, part], do[:, part]
+            augd = jnp.where(first, dhigh[:, part], dlow[:, part])
+            sums = [None, None, None]
+            for head in (0, 1):
+                mine = low if head == 0 else ~low
+                e = jnp.exp2(dot(jnp.where(mine, kp, augk), jnp.where(mine, qp, augq), ACROSS))
+                dp = dot(jnp.where(mine, vp, augv), jnp.where(mine, dop, augd), ACROSS)
+                ds = (e * dp).astype(BF16)
+                parts = (dot(ds, jnp.where(mine, kp, none), DOWN), dot(ds, jnp.where(mine, qp, none)),
+                         dot(e.astype(BF16), jnp.where(mine, dop, none)))
+                sums = [part_sum if total is None else total + part_sum for total, part_sum in zip(sums, parts)]
+            dq[:, part] = sums[0] * 0.125
+            dk[:, part] = sums[1] * (1.0 / LOG2E)
+            dproj[2, :, part] = sums[2].astype(BF16)
+        loop(PAIRS, pair)
+        for which, grads, low_ref, root_ref, gain, factor in ((0, dq, q, rq, qg_ref, SCALE), (1, dk, k, rk, kg_ref, 1.0)):
+            @halves()
+            def _(rows, columns):
+                grad, gains = grads[rows, columns], gain[layer]
+                xhat = low_ref[layer, rows, columns].astype(F32) * (1.0 / (gains * factor))
+                scaled = grad * gains
+                mean = head_means(scaled, spread, False)
+                along = head_means(scaled * xhat, spread, False)
+                dproj[which, rows, columns] = (root_ref[layer, rows, columns].astype(F32) * (scaled - mean - xhat * along)).astype(BF16)
+                gain_ref[layer, which + 1 : which + 2, columns] += jnp.sum(grad * xhat, 0, keepdims=True)
+
+    @pl.when(kind == PROJECT_BACK)
+    def _():
+        product = dot(dproj[tile], w_in_ref[...], ACROSS)
+        pl.when(tile == IN_ORDER[0])(lambda: acc.__setitem__(..., product))
+        pl.when(tile != IN_ORDER[0])(lambda: acc.__setitem__(..., acc[...] + product))
+        terms_in_ref[...] = dot(normed[layer], dproj[tile], DOWN).astype(BF16)
+
+        @pl.when(tile == IN_ORDER[-1])
+        def _():
+            gains = ln_ref[layer]
+
+            def body(rows):
+                grad = acc[rows, :]
+                xhat = normed[layer, rows, :].astype(F32) * (1.0 / gains)
+                scaled = grad * gains
+                mean = jnp.mean(scaled, -1, keepdims=True)
+                along = jnp.mean(scaled * xhat, -1, keepdims=True)
+                total = dy[rows, :].astype(F32) + scale[layer, rows, :1] * (scaled - mean - xhat * along)
+                grad_ref[layer, rows, :] = total
+                dy[rows, :] = total.astype(BF16)
+                gain_ref[layer, 0:1, :] += jnp.sum(grad * xhat, 0, keepdims=True)
+            by_rows(body)
+
+
+def both_layers(h, cot, full_in, full_out, ln, qg, kg, augq, augk, spread):
+    table = plan()
+    square = (SLOTS, D)
+
+    def whole(*dims):
+        return pl.BlockSpec(dims, lambda t, p: (0,) * len(dims))
+
+    def tiled(row, by_rows):
+        if by_rows:
+            return pl.BlockSpec((None, D, D), lambda t, p: (p[row, t], p[row + 1, t], 0))
+        return pl.BlockSpec((None, D, D), lambda t, p: (p[row, t], 0, p[row + 1, t]))
+
+    low, wide = (lambda *dims: pltpu.VMEM(dims, BF16)), (lambda *dims: pltpu.VMEM(dims, F32))
+    return pl.pallas_call(
+        compute_kernel,
+        grid_spec=pltpu.PrefetchScalarGridSpec(
+            num_scalar_prefetch=1,
+            grid=(table.shape[1],),
+            in_specs=[
+                whole(*square), whole(*square), tiled(3, False), tiled(5, True), whole(2, 1, D), whole(2, 1, 256), whole(2, 1, 256),
+                whole(SLOTS, 128), whole(SLOTS, 128), whole(256, 256),
+            ],
+            out_specs=[whole(2, *square), whole(2, *square), whole(2, 8, D), tiled(7, False), tiled(9, True)],
+            scratch_shapes=[
+                low(2, *square), low(2, *square), wide(2, SLOTS, 128), low(2, *square), low(2, *square), low(2, *square), low(2, *square),
+                low(2, *square), wide(2, *square), low(2, 4, *square), low(2, 5, *square), low(*square), low(7, *square), wide(*square),
+                wide(*square), wide(*square), low(*square), low(*square), low(*square),
+            ],
+        ),
+        out_shape=[
+            jax.ShapeDtypeStruct((2,) + square, BF16), jax.ShapeDtypeStruct((2,) + square, F32), jax.ShapeDtypeStruct((2, 8, D), F32),
+            jax.ShapeDtypeStruct(full_in.shape, BF16), jax.ShapeDtypeStruct(full_out.shape, BF16),
+        ],
+        compiler_params=pltpu.CompilerParams(vmem_limit_bytes=62 * 2**20),
+        name="both_layers",
+    )(jnp.asarray(table), h, cot, full_in, full_out, ln, qg, kg, augq, augk, spread)
+
+
+def augment(image_id, token_size):
+    high, low = split(jnp.log2(token_size.astype(F32)))
+    same = (image_id[:, None] == jnp.arange(3)[None, :]).astype(BF16)
+    one = jnp.ones_like(high)
+    q = jnp.concatenate([one[:, None], one[:, None], same, one[:, None]], 1)
+    k = jnp.concatenate([high[:, None], low[:, None], same * APART, one[:, None] * -APART], 1)
+    return [jnp.tile(jnp.pad(part, ((0, 0), (0, HD - 6))), (1, 2)) for part in (q, k)]
+
+
+def spread_matrix():
+    head = jnp.arange(256) // HD
+    return ((head[:, None] == head[None, :]) / HD).astype(BF16)
 
 
 def gather_all(piece, axis):
@@ -657,69 +871,51 @@
 
 
 def on_device(inputs, cotangent, token_size, image_id, w_in, w_out, ln_gain, q_gain, k_gain):
-    section = lax.axis_index("section")
-    wide = lax.axis_size("wide")
-    model_width = inputs.shape[3]
-    blocks_fit = wide == 16 and w_in.shape[1] == BLOCK[0][0] and w_out.shape[1] == BLOCK[1][0]
+    section, wide = lax.axis_index("section"), lax.axis_index("wide")
+    width = lax.axis_size("wide")
+    blocks_fit = width == 16 and w_in.shape[1:] == BLOCK[0] and w_out.shape[1:] == BLOCK[1]
+    ends = [0]
+    for gain in (ln_gain, q_gain, k_gain):
+        ends.append(ends[-1] + gain.shape[1])
+    own_gains = jnp.concatenate([ln_gain, q_gain, k_gain], 1)
     if blocks_fit:
-        full_in, full_out = gather_weights(w_in[0], w_out[0])
+        padded = jnp.pad(own_gains, ((0, BLOCK[2][0] - 1), (0, BLOCK[2][1] - ends[3])))
+        full_in, full_out, full_gains = gather_weights(w_in[0], w_out[0], padded)
+        full_gains = full_gains.reshape((2, width) + BLOCK[2])[:, :, 0]
     else:
         full_in, full_out = gather_all(w_in, 1), gather_all(w_out, 1)
-    cuts = (ln_gain.shape[1], ln_gain.shape[1] + q_gain.shape[1])
-    gains = gather_all(jnp.concatenate([ln_gain, q_gain, k_gain], 1)[:, None], 1)
-    full_ln, full_q, full_k = [
-        part.reshape(2, -1) for part in (gains[:, :, : cuts[0]], gains[:, :, cuts[0] : cuts[1]], gains[:, :, cuts[1] :])
+        full_gains = gather_all(own_gains[:, None], 1)
+    ln, qg, kg = [full_gains[:, :, low:high].reshape(2, 1, -1).astype(F32) for low, high in zip(ends, ends[1:])]
+    augq, augk = augment(image_id[section, 0], token_size[section, 0])
+    outs, grads, gain_terms, terms_in, terms_out = both_layers(
+        inputs[section, 0], cotangent[section, 0], full_in, full_out, ln, jnp.tile(qg, (1, 1, 4)), jnp.tile(kg, (1, 1, 4)),
+        augq, augk, spread_matrix())
+    swap = [(0, 1), (1, 0)]
+
+    def both_micro(pair):
+        mine = lax.dynamic_index_in_dim(pair, section, 0, False)
+        other = lax.dynamic_index_in_dim(pair, 1 - section, 0, False).astype(BF16)
+        other = lax.ppermute(other, "section", swap).astype(mine.dtype)
+        return jnp.where(section == 0, jnp.stack([mine, other]), jnp.stack([other, mine]))[None, :, None]
+
+    heads = gain_terms[:, 1:3].reshape(2, 2, -1, HD).sum(2).reshape(2, -1)
+    totals = jnp.concatenate([gain_terms[:, 0], heads], 1)
+    places = (0, D, D + HD, D + 2 * HD)
+    if blocks_fit:
+        totals = jnp.pad(totals, ((0, 0), (0, 1024 - places[3]))).reshape(BLOCK[2])
+        own_in, own_out, totals = scatter_terms(terms_in, terms_out, totals)
+        own_in, own_out = own_in[None], own_out[None]
+        totals = totals.reshape(2, 1024)
+    else:
+        own_in = scatter_all(terms_in, 1).astype(F32)
+        own_out = scatter_all(terms_out, 1).astype(F32)
+        totals = lax.psum(totals, ("section", "wide"))
+    mine = lax.dynamic_index_in_dim(totals, section, 0, False)
+    gain_grads = [
+        lax.dynamic_slice_in_dim(mine[low:high], wide * gain.shape[1], gain.shape[1])[None]
+        for low, high, gain in zip(places, places[1:], (ln_gain, q_gain, k_gain))
     ]
-    weights = [(full_in[layer], full_out[layer], full_ln[layer], full_q[layer], full_k[layer]) for layer in range(2)]
-    ids = image_id[section]
-    bias = jnp.log(token_size[section].astype(jnp.float32))
-    hidden = inputs[section]
-    kept, outs = [], []
-    for layer in range(2):
-        hidden = hidden.astype(jnp.float32)
-        pieces = layer_pieces(hidden, weights[layer], ids, bias)
-        branch = jnp.dot(pieces[8], weights[layer][1], preferred_element_type=jnp.float32)
-        kept.append((hidden, pieces))
-        hidden = (hidden + branch.reshape(hidden.shape)).astype(jnp.bfloat16)
-        outs.append(hidden)
-    grad_low = cotangent[section]
-    grads, gain_terms, terms_in, terms_out = [None, None], [None, None], [None, None], [None, None]
-    contract_rows = (((0,), (0,)), ((), ()))
-    for layer in (1, 0):
-        results = layer_backward(kept[layer][0], grad_low, kept[layer][1], weights[layer], ids, bias)
-        grads[layer] = results[0]
-        gain_terms[layer] = results[1:4]
-        terms_in[layer] = lax.dot_general(results[4], results[5], contract_rows, preferred_element_type=jnp.bfloat16)
-        terms_out[layer] = lax.dot_general(results[6], results[7], contract_rows, preferred_element_type=jnp.bfloat16)
-        grad_low = results[0].astype(jnp.bfloat16)
-    terms_in, terms_out = jnp.stack(terms_in), jnp.stack(terms_out)
-    if blocks_fit:
-        own_in, own_out = scatter_terms(terms_in, terms_out)
-        own_in, own_out = own_in[None], own_out[None]
-    else:
-        own_in = scatter_all(terms_in, 1).astype(jnp.float32)
-        own_out = scatter_all(terms_out, 1).astype(jnp.float32)
-    gain_rows = [
-        jnp.stack([gain_terms[layer][position] for layer in range(2)]).reshape(2, wide, -1) for position in range(3)
-    ]
-    own_gains = scatter_all(jnp.concatenate(gain_rows, 2), 1)[:, 0]
-    swap = [(0, 1), (1, 0)]
-
-    def both_micro(pair):
-        mine = jnp.where(section == 0, pair[0], pair[1])
-        other = lax.ppermute(jnp.where(section == 0, pair[1], pair[0]).astype(jnp.bfloat16), "section", swap)
-        other = other.astype(mine.dtype)
-        return jnp.where(section == 0, jnp.stack([mine, other]), jnp.stack([other, mine]))[None]
-
-    return (
-        both_micro(outs),
-        both_micro(grads),
-        own_in,
-        own_out,
-        own_gains[:, : cuts[0]],
-        own_gains[:, cuts[0] : cuts[1]],
-        own_gains[:, cuts[1] :],
-    )
+    return (both_micro(outs), both_micro(grads), own_in, own_out, *gain_grads)
 
 
 def solution(mesh):

time: 619 us -> 472 us (0.76); the launches traced: 610 us -> 471 us
  Pallas kernels: 244 us -> 442 us
  matrix products: 150 us -> 0 us
  other arithmetic: 106 us -> 8.79 us
  blocking collectives: 46 us -> 0 us
  local copies, waits for them, and re-layouts: 46.3 us -> 17.7 us
  between operations: 15.9 us -> 0.79 us
    pallas_call x1 -> x2, Pallas kernels: 113 us -> 270 us  [the longest x1 152 us: both_layers(): pl.pallas_call(compute_kernel, grid_spec=pltpu.PrefetchScalarGridSpec(num...]
    dot_general x24 -> x0, matrix products: 150 us -> none  [the longest x2 19.4 us: layer_backward(): lax.dot_general(grad_projected, weights[0], contract_last, preferred_elem...]
    another operation x10 -> x0, other arithmetic: 60.2 us -> none
    pallas_call x1, Pallas kernels: 130 us -> 172 us  [scatter_terms(): pl.pallas_call(scatter_kernel, out_shape=tuple((jax.ShapeDtypeStruct(bloc...]
    all_gather x2 -> x0, blocking collectives: 23 us -> none  [the longest x1 18.7 us: gather_all(): lax.all_gather(piece, 'wide', axis=axis, tiled=True)]
    unnamed x1 -> x0, blocking collectives: 22.9 us -> none
    convert_element_type x5 -> x6, other arithmetic: 22.1 us -> 2.35 us  [the longest x1 0.81 us: split(): high = value.astype(BF16)]
    slice x15 -> x4, local copies, waits for them, and re-layouts: 17.5 us -> 2.53 us  [the longest x1 0.85 us: on_device(): full_gains = full_gains.reshape((2, width) + BLOCK[2])[:, :, 0]]
  transfers between devices with their start and end apart: 3 -> 2, of which waited for: 0 -> 0; matrix products, arithmetic and copies ran while one was open for 29% -> 2% of each run, Pallas kernels for 21% -> 36%
where the time goes in v3:
time: 472 us; the launch traced here: 471 us
  Pallas kernels  442 us (94%)
  local copies, waits for them, and re-layouts  17.7 us (4%)
  other arithmetic  8.79 us (2%)
    pallas_call x1, Pallas kernels, scatter_terms(): pl.pallas_call(scatter_kernel, out_shape=tuple((jax.ShapeDtypeStruct(bloc...  172 us
    pallas_call x1, Pallas kernels, both_layers(): pl.pallas_call(compute_kernel, grid_spec=pltpu.PrefetchScalarGridSpec(num...  152 us
    pallas_call x1, Pallas kernels, gather_weights(): pl.pallas_call(gather_kernel, out_shape=tuple((jax.ShapeDtypeStruct(dims,...  118 us
  transfers between devices with their start and end apart: 2, of which 0 were waited for; matrix products, arithmetic and copies ran while one was open for 2% of the time, Pallas kernels for 36%

profile of v3, /device:TPU:8, one launch (start us, length us, event | category | flops | bytes accessed | tf_op | source)
XLA Modules:
  0.0 471.1 jit_solution(1471622269652887615)
XLA Ops:
  0.6 0.0 copy-start
  0.6 0.0 copy-start.5
  0.7 0.8 bitcast_convert_fusion.1
  1.5 0.7 fusion.15
  2.2 0.0 copy-done
  2.2 1.4 fusion.11.gains
  3.6 118.5 %gather_weights.1 = (bf16[2,768,5376]{2,1,0:T(8,128)(2,1)}, bf16[2,3840,768]{2,1,0:T(8,128)(2,1)}, bf16[2,256,128]{2,1,0:T(8,128)(2,1)}) custom-call(bf16[48,5376]{1,0:T(8,128)(2,1)} %bitcast.43, bf16[240,768]{1,0:T(8,128)(2,1)} %bitcast.44, bf16[16,128]{1,0:T(8,128)(2,1)} %fusion.11.gains), custom_call_target="tpu_custom_call" | custom-call | tf_op jit(solution)/shard_map/gather_weights/pallas_call | solution.py:271
  122.1 0.9 slice.39
  123.0 0.1 slice_convert_fusion
  123.0 0.1 pad.32.clone
  123.1 0.1 maximum_maximum_fusion.1
  123.2 0.8 copy.20.augk_ref
  124.0 0.1 pad.35.clone
  124.1 0.1 maximum_maximum_fusion
  124.2 0.8 copy.19.augq_ref
  124.9 0.1 reshape.278
  125.0 0.7 tile.17.qg_ref
  125.7 0.1 reshape.279
  125.8 0.6 tile.19.kg_ref
  126.4 0.7 reshape.277.ln_ref
  127.1 0.8 select_convert_fusion.spread_ref
  127.8 2.4 dynamic-slice_bitcast_fusion.3
  130.3 151.5 %both_layers.1 = (bf16[2,512,768]{2,1,0:T(8,128)(2,1)}, f32[2,512,768]{2,1,0:T(8,128)}, f32[2,8,768]{2,1,0:T(8,128)}, bf16[2,768,5376]{2,1,0:T(8,128)(2,1)}, bf16[2,3840,768]{2,1,0:T(8,128)(2,1)}) custom-call(s32[11,43]{1,0:T(8,128)} %constant.82.clone.plan_ref, bf16[512,768]{1,0:T(8,128)(2,1)} %get-tuple-element.36.h_ref, ...), custom_call_target="tpu_custom_call" | custom-call | tf_op jit(solution)/shard_map/both_layers/pallas_call | solution.py:825
  281.8 1.6 fusion
  283.4 1.3 collective-permute-start.1
  284.8 0.0 copy-done.2
  284.8 0.1 dynamic-slice_bitcast_fusion.2
  284.9 0.8 collective-permute-start
  285.7 0.8 slice.35
  286.5 0.8 slice.34
  287.3 0.1 reshape.273
  287.4 0.1 reshape.274
  287.5 0.6 reshape.275.gains
  288.1 171.7 %scatter_terms.1 = (f32[48,5376]{1,0:T(8,128)}, f32[240,768]{1,0:T(8,128)}, f32[16,128]{1,0:T(8,128)}) custom-call(bf16[2,768,5376]{2,1,0:T(8,128)(2,1)} %get-tuple-element.23.terms_in, bf16[2,3840,768]{2,1,0:T(8,128)(2,1)} %get-tuple-element.24.terms_out, f32[16,128]{1,0:T(8,128)} %reshape.275.gains), custom_call_target="tpu_custom_call" | custom-call | tf_op jit(solution)/shard_map/scatter_terms/pallas_call | solution.py:548
  459.8 0.7 reshape.276
  460.5 0.1 fusion.16
  460.6 0.6 constant_dynamic-slice_fusion
  461.2 0.6 dynamic-slice.4
  461.8 0.6 constant_dynamic-slice_fusion.1
  462.3 1.5 dynamic-slice_bitcast_fusion
  463.9 0.0 collective-permute-done.1
  463.9 0.1 bitcast_convert_fusion
  464.0 1.9 maximum_select_fusion
  465.9 0.0 collective-permute-done
  465.9 2.9 maximum_select_fusion.1
  468.8 1.0 copy.29
  469.7 0.5 copy-done.4
  470.3 0.9 copy.30
  (24 shorter events, 0.2 us)
Async XLA Ops:
  0.6 1.6 copy-start
  0.6 127.2 %copy-start.5 = (bf16[2,1,512,768]{3,2,1,0:T(8,128)(2,1)S(1)}, bf16[2,1,512,768]{3,2,1,0:T(8,128)(2,1)}, u32[]{:S(2)}) copy-start(bf16[2,1,512,768]{3,2,1,0:T(8,128)(2,1)} %param.11) | copy-start | bytes 4718596
  281.8 3.0 copy-start.2
  283.4 180.4 %collective-permute-start.1 = (bf16[512,768]{1,0:T(8,128)(2,1)S(1)}, bf16[512,768]{1,0:T(8,128)(2,1)S(1)}, u32[]{:S(2)}, u32[]{:S(2)}) collective-permute-start(bf16[512,768]{1,0:T(8,128)(2,1)S(1)} %fusion), channel_id=1, source_target_pairs={{0,16},{16,0},{1,17},{17,1},{2,18},{18,2},{3,19},{19,3},{4,20},{20... | collective-permute-start | bytes 2359304 | tf_op jit(solution)/shard_map/ppermute | solution.py:898
  284.9 181.0 %collective-permute-start = (bf16[512,768]{1,0:T(8,128)(2,1)S(1)}, bf16[512,768]{1,0:T(8,128)(2,1)}, u32[]{:S(2)}, u32[]{:S(2)}) collective-permute-start(bf16[512,768]{1,0:T(8,128)(2,1)S(1)} %get-tuple-element.30), channel_id=1, source_target_pairs={{0,16},{16,0},{1,17},{17,1},{2,18},{18,2},{3,19},{19,3},{4,20},{20... | collective-permute-start | bytes 2359304 | tf_op jit(solution)/shard_map/ppermute | solution.py:898
  465.9 2.9 copy-start.3
  465.9 5.3 %copy-start.1 = (s32[2,1,512]{2,1,0:T(1,128)S(1)}, s32[2,1,512]{2,1,0:T(1,128)}, u32[]{:S(2)}) copy-start(s32[2,1,512]{2,1,0:T(1,128)} %param.13) | copy-start | bytes 12292
  468.8 1.5 copy-start.4

commit v4 on v3

--- a/solution.py
+++ b/solution.py
@@ -2,7 +2,6 @@
 
 import jax
 import jax.numpy as jnp
-import numpy as np
 from jax import lax
 from jax.experimental import pallas as pl
 from jax.experimental.pallas import tpu as pltpu
@@ -11,9 +10,8 @@
 MESH = pl.DeviceIdType.MESH
 NZ = 4
 BLOCK = ((48, 5376), (240, 768), (16, 128))
-CUT_IN, CUT_OUT = 2176, 96
-PART = ((48, CUT_IN), (CUT_OUT, 768))
-REST = ((48, 5376 - 2 * CUT_IN), (240 - 2 * CUT_OUT, 768))
+GATHER_CUTS = (2176, 96)
+SCATTER_CUTS = (2176, 96)
 
 
 class Place:
@@ -62,17 +60,22 @@
     return block[0] * 8 + block[1] * 4 + block[2]
 
 
-def cut(ref, array, colour):
+def part_shape(cuts, array, colour):
     rows, cols = BLOCK[array]
+    size = cuts[array]
+    if array == 0:
+        return rows, cols - 2 * size if colour is None else size
+    return rows - 2 * size if colour is None else size, cols
+
+
+def cut(ref, cuts, array, colour):
     if array == 2:
         return ref
+    rows, cols = part_shape(cuts, array, colour)
+    size = cuts[array]
     if array == 0:
-        if colour is None:
-            return ref.at[:, pl.ds(2 * CUT_IN, cols - 2 * CUT_IN)]
-        return ref.at[:, pl.ds(pl.multiple_of(colour * CUT_IN, 128), CUT_IN)]
-    if colour is None:
-        return ref.at[pl.ds(2 * CUT_OUT, rows - 2 * CUT_OUT), :]
-    return ref.at[pl.ds(pl.multiple_of(colour * CUT_OUT, 16), CUT_OUT), :]
+        return ref.at[:, pl.ds(2 * size if colour is None else pl.multiple_of(colour * size, 128), cols)]
+    return ref.at[pl.ds(2 * size if colour is None else pl.multiple_of(colour * size, 16), rows), :]
 
 
 def loop(count, body):
@@ -91,13 +94,13 @@
         rows = BLOCK[self.array][0]
         place = self.place
         start = (block[2] * 4 + block[1] * 2 + (place.c if plane is None else plane)) * rows
-        return cut(self.full.at[block[0], pl.ds(pl.multiple_of(start, 16), rows), :], self.array, colour)
+        return cut(self.full.at[block[0], pl.ds(pl.multiple_of(start, 16), rows), :], GATHER_CUTS, self.array, colour)
 
     def copy(self, link, device, block, colour, own=False, other_plane=False):
         kind = 2 if colour is None else colour
         number = number_of(block)
         target = self.view(block, colour, 1 - self.place.c if other_plane else None)
-        source = cut(self.own, self.array, colour) if own else target
+        source = cut(self.own, GATHER_CUTS, self.array, colour) if own else target
         sems = self.core_sem if link == 4 else self.recv_sem
         return pltpu.make_async_remote_copy(
             src_ref=source, dst_ref=target, send_sem=self.send_sem.at[link, kind, number], recv_sem=sems.at[kind, number],
@@ -294,13 +297,13 @@
         self.send_sem, self.recv_sem, self.rest_send, self.rest_recv, self.core_send, self.core_recv, self.local_sem = sems
 
     def part(self, block, colour):
-        return cut(self.held.at[number_of(block)], self.array, colour)
+        return cut(self.held.at[number_of(block)], SCATTER_CUTS, self.array, colour)
 
     def copy(self, device, block, colour, slot):
         if colour is None:
             target, send_sem, recv_sem = self.rest_land.at[slot], self.rest_send.at[slot], self.rest_recv.at[slot]
         else:
-            target, send_sem, recv_sem = self.land.at[colour, slot], self.send_sem.at[colour, slot], self.recv_sem.at[colour, slot]
+            target, send_sem, recv_sem = self.land.at[colour * 20 + slot], self.send_sem.at[colour, slot], self.recv_sem.at[colour, slot]
         return pltpu.make_async_remote_copy(
             src_ref=self.part(block, colour), dst_ref=target, send_sem=send_sem, recv_sem=recv_sem, device_id=device,
             device_id_type=MESH)
@@ -312,7 +315,7 @@
     def arrive(self, block, colour, slot, drain):
         if not drain:
             self.copy(self.place.sibling(), block, colour, slot).wait_recv()
-            add_into(self.part(block, colour), self.rest_land.at[slot] if colour is None else self.land.at[colour, slot])
+            add_into(self.part(block, colour), self.rest_land.at[slot] if colour is None else self.land.at[colour * 20 + slot])
 
     def core_copy(self, block, mine):
         rows = BLOCK[self.array][0]
@@ -495,9 +498,13 @@
                 pl.when(sent)(lambda: self.copy(link).wait_send())
 
 
-def scatter_kernel(terms_in, terms_out, gains, out_in, out_out, out_gains, *rest):
+def scatter_kernel(terms_in, terms_out, gains, grad, out_in, out_out, out_gains, grad_land, *rest):
     place = Place()
     greet(place)
+    grad_copy = pltpu.make_async_remote_copy(
+        src_ref=grad, dst_ref=grad_land, send_sem=rest[26].at[0], recv_sem=rest[26].at[1],
+        device_id=place.at(1 - place.x, place.y, place.z), device_id_type=MESH)
+    pl.when(place.x == 1)(lambda: grad_copy.start())
     total = Total(place, gains, out_gains, *rest[22:26])
     arrays = [Scatter(place, array, (terms_in, terms_out)[array], *rest[4 * array : 4 * array + 4], rest[8 + 7 * array : 15 + 7 * array])
               for array in range(2)]
@@ -533,26 +540,29 @@
     for array in order:
         array.drain()
     total.drain()
-
-
-def scatter_terms(terms_in, terms_out, gains):
+    pl.when(place.x == 1)(lambda: grad_copy.wait_send())
+    pl.when(place.x == 0)(lambda: grad_copy.wait_recv())
+
+
+def scatter_terms(terms_in, terms_out, gains, grad):
     any_space = pl.BlockSpec(memory_space=pl.ANY)
     vmem = pl.BlockSpec(memory_space=pltpu.VMEM)
     dma = pltpu.SemaphoreType.DMA
     buffers, sems = [], []
     for array in range(2):
         buffers += [pltpu.VMEM((16,) + BLOCK[array], jnp.bfloat16)] * 2
-        buffers += [pltpu.VMEM((2, 20) + PART[array], jnp.bfloat16), pltpu.VMEM((35,) + REST[array], jnp.bfloat16)]
+        buffers += [
+            pltpu.VMEM((count,) + part_shape(SCATTER_CUTS, array, colour), jnp.bfloat16) for count, colour in ((40, 0), (35, None))]
         sems += [dma((2, 20)), dma((2, 20)), dma((35,)), dma((35,)), dma((16,)), dma((16,)), dma((16,))]
-    small = [pltpu.VMEM((5,) + BLOCK[2], jnp.float32)] * 2 + [dma((5,))] * 2
+    small = [pltpu.VMEM((5,) + BLOCK[2], jnp.float32)] * 2 + [dma((5,))] * 2 + [dma((2,))]
     return pl.pallas_call(
         scatter_kernel,
-        out_shape=tuple(jax.ShapeDtypeStruct(block, jnp.float32) for block in BLOCK),
-        in_specs=[any_space] * 2 + [vmem], out_specs=(vmem,) * 3,
+        out_shape=tuple(jax.ShapeDtypeStruct(block, jnp.float32) for block in BLOCK) + (jax.ShapeDtypeStruct(grad.shape, grad.dtype),),
+        in_specs=[any_space] * 2 + [vmem, any_space], out_specs=(vmem,) * 3 + (any_space,),
         scratch_shapes=buffers + sems + small,
         compiler_params=pltpu.CompilerParams(collective_id=1, has_side_effects=True, vmem_limit_bytes=58 * 2**20),
         name="scatter_terms",
-    )(terms_in, terms_out, gains)
+    )(terms_in, terms_out, gains, grad)
 
 
 SLOTS, D, HD, PAIRS = 512, 768, 64, 6
@@ -594,46 +604,57 @@
     return pl.ds(pl.multiple_of(index * width, width), width)
 
 
-PROJECT, OUTPUT, OUTPUT_BACK, BACK, PROJECT_BACK = range(5)
-IN_ORDER = (3, 4, 5, 6, 0, 1, 2)
-
-
-def plan():
-    steps = [(PROJECT, 0, tile) for tile in range(TILES_IN)] + [(OUTPUT, 0, tile) for tile in range(TILES_OUT)]
-    steps += [(PROJECT, 1, tile) for tile in range(TILES_IN)] + [(OUTPUT_BACK, 1, tile) for tile in range(TILES_OUT)]
-    steps += [(PROJECT_BACK, 1, tile) for tile in IN_ORDER]
-    steps += [(BACK, 0, tile) for tile in range(TILES_OUT)] + [(PROJECT_BACK, 0, tile) for tile in IN_ORDER]
-    uses_in = [kind in (PROJECT, PROJECT_BACK) for kind, _, _ in steps]
-    gives_in = [kind == PROJECT_BACK for kind, _, _ in steps]
-    gives_out = [kind in (OUTPUT_BACK, BACK) for kind, _, _ in steps]
-
-    def coming(used):
-        table, now = [], None
-        for step, use in zip(reversed(steps), reversed(used)):
-            now = step[1:] if use else now
-            table.append(now)
-        table = table[::-1]
-        last = [step[1:] for step, use in zip(steps, used) if use][-1]
-        return [last if entry is None else entry for entry in table]
-
-    def given(made):
-        table, now = [], [step[1:] for step, use in zip(steps, made) if use][0]
-        for step, use in zip(steps, made):
-            now = step[1:] if use else now
-            table.append(now)
-        return table
-
-    tables = [coming(uses_in), coming([not use for use in uses_in]), given(gives_in), given(gives_out)]
-    columns = [[step[part] for step in steps] for part in range(3)]
-    columns += [[entry[part] for entry in table] for table in tables for part in range(2)]
-    return np.array(columns, np.int32)
-
-
-def compute_kernel(plan_ref, h_ref, cot_ref, w_in_ref, w_out_ref, ln_ref, qg_ref, kg_ref, augq_ref, augk_ref, spread_ref,
-                   out_ref, grad_ref, gain_ref, terms_in_ref, terms_out_ref,
-                   hidden, normed, scale, q, k, v, rq, rk, linv, slope, combined, dy, dproj, acc, dq, dk, do, dhigh, dlow):
+FIRST_OUT, SECOND_IN, SECOND_OUT, SECOND_BACK, LAST_OUT, LAST_BACK, STEPS = 7, 12, 19, 24, 31, 36, 43
+LAST_TILE = 2
+
+
+def up_first(index):
+    return (index + 3) % TILES_IN
+
+
+def clip(index, high):
+    return jnp.clip(index, 0, high)
+
+
+def in_tile(t):
+    layer = ((t >= FIRST_OUT) & (t < LAST_OUT)).astype(jnp.int32)
+    forward = jnp.where(t < FIRST_OUT, t, clip(t - SECOND_IN, 6))
+    backward = up_first(jnp.where(t < LAST_OUT, clip(t - SECOND_BACK, 6), clip(t - LAST_BACK, 6)))
+    return layer, jnp.where(t < SECOND_OUT, forward, backward)
+
+
+def out_tile(t):
+    layer = ((t >= SECOND_IN) & (t < SECOND_BACK)).astype(jnp.int32)
+    tile = jnp.where(t < SECOND_IN, clip(t - FIRST_OUT, 4), jnp.where(t < SECOND_BACK, clip(t - SECOND_OUT, 4), clip(t - LAST_OUT, 4)))
+    return layer, tile
+
+
+def in_terms(t):
+    late = t >= LAST_BACK
+    tile = up_first(jnp.where(late, t - LAST_BACK, clip(t - SECOND_BACK, 6)))
+    return 1 - late.astype(jnp.int32), tile
+
+
+def out_terms(t):
+    late = t >= LAST_OUT
+    return 1 - late.astype(jnp.int32), jnp.where(late, clip(t - LAST_OUT, 4), clip(t - SECOND_OUT, 4))
+
+
+def compute_kernel(h_ref, cot_ref, w_in_ref, w_out_ref, ln_ref, qg_ref, kg_ref, augq_ref, augk_ref, spread_ref,
+                   section_out, grad_ref, grad_low, grad_land, gain_ref, terms_in_ref, terms_out_ref,
+                   hidden, normed, scale, q, k, v, rq, rk, linv, slope, combined, dy, dproj, acc, dq, dk, do, dhigh, dlow, *swap):
     t = pl.program_id(0)
-    kind, layer, tile = plan_ref[0, t], plan_ref[1, t], plan_ref[2, t]
+    layer = in_tile(t)[0]
+    project = (t < FIRST_OUT) | ((t >= SECOND_IN) & (t < SECOND_OUT))
+    project_back = ((t >= SECOND_BACK) & (t < LAST_OUT)) | (t >= LAST_BACK)
+    output = (t >= FIRST_OUT) & (t < SECOND_IN)
+    output_both = (t >= SECOND_OUT) & (t < SECOND_BACK)
+    back = (t >= LAST_OUT) & (t < LAST_BACK)
+    layer = jnp.where(output, 0, layer)
+    tile = jnp.where(project | project_back, in_tile(t)[1], out_tile(t)[1])
+    section, trade = lax.axis_index("section"), None
+    if swap:
+        trade = Trade(section, section_out, hidden, dy, grad_land, *swap)
     spread = spread_ref[...]
 
     def halves(width=256):
@@ -649,12 +670,14 @@
     @pl.when(t == 0)
     def _():
         hidden[0] = h_ref[...]
+        if trade:
+            trade.greet()
         gain_ref[...] = jnp.zeros_like(gain_ref)
 
     def low_lanes():
         return lax.broadcasted_iota(jnp.int32, (SLOTS, 128), 1) < HD
 
-    @pl.when((kind == PROJECT) & (tile == 0))
+    @pl.when(project & (tile == 0))
     def _():
         def body(rows):
             h = hidden[layer, rows, :].astype(F32)
@@ -664,7 +687,7 @@
             normed[layer, rows, :] = (centred * root * ln_ref[layer]).astype(BF16)
         by_rows(body)
 
-    @pl.when(kind == PROJECT)
+    @pl.when(project)
     def _():
         acc[...] = dot(normed[layer], w_in_ref[...])
 
@@ -708,7 +731,7 @@
                 slope[layer, tile - 3, rows, columns] = rise.astype(BF16)
                 combined[layer, tile - 2, rows, columns] = value.astype(BF16)
 
-    @pl.when((kind == OUTPUT) | (kind == OUTPUT_BACK))
+    @pl.when(output | output_both)
     def _():
         product = dot(combined[layer, tile], w_out_ref[...])
         pl.when(tile == 0)(lambda: dq.__setitem__(..., hidden[layer].astype(F32) + product))
@@ -717,14 +740,17 @@
         @pl.when(tile == TILES_OUT - 1)
         def _():
             result = dq[...].astype(BF16)
-            out_ref[layer] = result
-            pl.when(layer == 0)(lambda: hidden.__setitem__(1, result))
-
-    @pl.when((kind == OUTPUT_BACK) & (tile == 0))
+            hidden[layer + 1] = result
+            if trade:
+                trade.give_output(layer)
+            else:
+                section_out[layer] = result
+
+    @pl.when(output_both & (tile == 0))
     def _():
         dy[...] = cot_ref[...]
 
-    @pl.when((kind == OUTPUT_BACK) | (kind == BACK))
+    @pl.when(output_both | back)
     def _():
         acc[...] = dot(dy[...], w_out_ref[...], ACROSS)
         terms_out_ref[...] = dot(combined[layer, tile], dy[...], DOWN).astype(BF16)
@@ -748,7 +774,7 @@
             def _(rows, columns):
                 dproj[tile + 2, rows, columns] = (acc[rows, columns] * slope[layer, tile - 1, rows, columns].astype(F32)).astype(BF16)
 
-    @pl.when((kind == PROJECT_BACK) & (tile == 0))
+    @pl.when(project_back & (tile == 0))
     def _():
         low = low_lanes()
         spot = lax.broadcasted_iota(jnp.int32, (SLOTS, 128), 1) % HD
@@ -785,14 +811,14 @@
                 dproj[which, rows, columns] = (root_ref[layer, rows, columns].astype(F32) * (scaled - mean - xhat * along)).astype(BF16)
                 gain_ref[layer, which + 1 : which + 2, columns] += jnp.sum(grad * xhat, 0, keepdims=True)
 
-    @pl.when(kind == PROJECT_BACK)
+    @pl.when(project_back)
     def _():
         product = dot(dproj[tile], w_in_ref[...], ACROSS)
-        pl.when(tile == IN_ORDER[0])(lambda: acc.__setitem__(..., product))
-        pl.when(tile != IN_ORDER[0])(lambda: acc.__setitem__(..., acc[...] + product))
+        pl.when(tile == up_first(0))(lambda: acc.__setitem__(..., product))
+        pl.when(tile != up_first(0))(lambda: acc.__setitem__(..., acc[...] + product))
         terms_in_ref[...] = dot(normed[layer], dproj[tile], DOWN).astype(BF16)
 
-        @pl.when(tile == IN_ORDER[-1])
+        @pl.when(tile == LAST_TILE)
         def _():
             gains = ln_ref[layer]
 
@@ -803,48 +829,102 @@
                 mean = jnp.mean(scaled, -1, keepdims=True)
                 along = jnp.mean(scaled * xhat, -1, keepdims=True)
                 total = dy[rows, :].astype(F32) + scale[layer, rows, :1] * (scaled - mean - xhat * along)
-                grad_ref[layer, rows, :] = total
-                dy[rows, :] = total.astype(BF16)
+                low = total.astype(BF16)
+                if trade:
+                    pl.when(layer == section)(lambda: grad_ref.__setitem__((rows, slice(None)), total))
+                else:
+                    grad_ref[layer, rows, :] = total
+                pl.when(layer == 1)(lambda: dy.__setitem__((rows, slice(None)), low))
+                pl.when(layer == 0)(lambda: grad_low.__setitem__((rows, slice(None)), low))
                 gain_ref[layer, 0:1, :] += jnp.sum(grad * xhat, 0, keepdims=True)
             by_rows(body)
-
-
-def both_layers(h, cot, full_in, full_out, ln, qg, kg, augq, augk, spread):
-    table = plan()
+            if trade:
+                pl.when(layer == 1)(trade.give_grad)
+                pl.when(layer == 0)(trade.finish)
+
+
+class Trade:
+    def __init__(self, section, section_out, hidden, dy, grad_land, own_sem, send_sem, recv_sem):
+        self.section, self.section_out, self.hidden, self.dy, self.grad_land = section, section_out, hidden, dy, grad_land
+        self.own_sem, self.send_sem, self.recv_sem = own_sem, send_sem, recv_sem
+        self.pair = (1 - section, lax.axis_index("wide"))
+
+    def greet(self):
+        barrier = pltpu.get_barrier_semaphore()
+        pl.semaphore_signal(barrier, inc=1, device_id=self.pair, device_id_type=MESH)
+        pl.semaphore_wait(barrier, 1)
+
+    def kept(self):
+        return pltpu.make_async_copy(self.hidden.at[self.section + 1], self.section_out.at[self.section], self.own_sem)
+
+    def copy(self, source, target, index):
+        return pltpu.make_async_remote_copy(
+            src_ref=source, dst_ref=target, send_sem=self.send_sem.at[index], recv_sem=self.recv_sem.at[index],
+            device_id=self.pair, device_id_type=MESH)
+
+    def given(self):
+        return self.copy(self.hidden.at[2 - self.section], self.section_out.at[self.section], 0)
+
+    def grad(self):
+        return self.copy(self.dy, self.grad_land, 1)
+
+    def give_output(self, layer):
+        pl.when(layer == self.section)(lambda: self.kept().start())
+        pl.when(layer != self.section)(lambda: self.given().start())
+
+    def give_grad(self):
+        pl.when(self.section == 0)(lambda: self.grad().start())
+
+    def finish(self):
+        self.kept().wait()
+        self.given().wait_send()
+        self.copy(self.hidden.at[2 - self.section], self.section_out.at[1 - self.section], 0).wait_recv()
+        pl.when(self.section == 0)(lambda: self.grad().wait_send())
+        pl.when(self.section == 1)(lambda: self.grad().wait_recv())
+
+
+def both_layers(trading, h, cot, full_in, full_out, ln, qg, kg, augq, augk, spread):
     square = (SLOTS, D)
 
     def whole(*dims):
-        return pl.BlockSpec(dims, lambda t, p: (0,) * len(dims))
-
-    def tiled(row, by_rows):
-        if by_rows:
-            return pl.BlockSpec((None, D, D), lambda t, p: (p[row, t], p[row + 1, t], 0))
-        return pl.BlockSpec((None, D, D), lambda t, p: (p[row, t], 0, p[row + 1, t]))
+        return pl.BlockSpec(dims, lambda t: (0,) * len(dims))
+
+    def of_columns(where):
+        return pl.BlockSpec((None, D, D), lambda t: (where(t)[0], 0, where(t)[1]))
+
+    def of_rows(where):
+        return pl.BlockSpec((None, D, D), lambda t: (where(t)[0], where(t)[1], 0))
 
     low, wide = (lambda *dims: pltpu.VMEM(dims, BF16)), (lambda *dims: pltpu.VMEM(dims, F32))
+    any_space, dma = pl.BlockSpec(memory_space=pl.ANY), pltpu.SemaphoreType.DMA
+    if trading:
+        out_specs = [any_space, whole(*square), whole(*square), any_space]
+        grad_shape, extra = square, [dma(()), dma((2,)), dma((2,))]
+        params = dict(collective_id=2, has_side_effects=True)
+    else:
+        out_specs = [whole(2, *square), whole(2, *square), whole(*square), whole(*square)]
+        grad_shape, extra, params = (2,) + square, [], {}
     return pl.pallas_call(
         compute_kernel,
-        grid_spec=pltpu.PrefetchScalarGridSpec(
-            num_scalar_prefetch=1,
-            grid=(table.shape[1],),
-            in_specs=[
-                whole(*square), whole(*square), tiled(3, False), tiled(5, True), whole(2, 1, D), whole(2, 1, 256), whole(2, 1, 256),
-                whole(SLOTS, 128), whole(SLOTS, 128), whole(256, 256),
-            ],
-            out_specs=[whole(2, *square), whole(2, *square), whole(2, 8, D), tiled(7, False), tiled(9, True)],
-            scratch_shapes=[
-                low(2, *square), low(2, *square), wide(2, SLOTS, 128), low(2, *square), low(2, *square), low(2, *square), low(2, *square),
-                low(2, *square), wide(2, *square), low(2, 4, *square), low(2, 5, *square), low(*square), low(7, *square), wide(*square),
-                wide(*square), wide(*square), low(*square), low(*square), low(*square),
-            ],
-        ),
+        grid=(STEPS,),
+        in_specs=[
+            whole(*square), whole(*square), of_columns(in_tile), of_rows(out_tile), whole(2, 1, D), whole(2, 1, 256), whole(2, 1, 256),
+            whole(SLOTS, 128), whole(SLOTS, 128), whole(256, 256),
+        ],
+        out_specs=out_specs + [whole(2, 8, D), of_columns(in_terms), of_rows(out_terms)],
+        scratch_shapes=[
+            low(3, *square), low(2, *square), wide(2, SLOTS, 128), low(2, *square), low(2, *square), low(2, *square), low(2, *square),
+            low(2, *square), wide(2, *square), low(2, 4, *square), low(2, 5, *square), low(*square), low(7, *square), wide(*square),
+            wide(*square), wide(*square), low(*square), low(*square), low(*square),
+        ] + extra,
         out_shape=[
-            jax.ShapeDtypeStruct((2,) + square, BF16), jax.ShapeDtypeStruct((2,) + square, F32), jax.ShapeDtypeStruct((2, 8, D), F32),
-            jax.ShapeDtypeStruct(full_in.shape, BF16), jax.ShapeDtypeStruct(full_out.shape, BF16),
+            jax.ShapeDtypeStruct((2,) + square, BF16), jax.ShapeDtypeStruct(grad_shape, F32), jax.ShapeDtypeStruct(square, BF16),
+            jax.ShapeDtypeStruct(square, BF16), jax.ShapeDtypeStruct((2, 8, D), F32), jax.ShapeDtypeStruct(full_in.shape, BF16),
+            jax.ShapeDtypeStruct(full_out.shape, BF16),
         ],
-        compiler_params=pltpu.CompilerParams(vmem_limit_bytes=62 * 2**20),
+        compiler_params=pltpu.CompilerParams(vmem_limit_bytes=63 * 2**20, **params),
         name="both_layers",
-    )(jnp.asarray(table), h, cot, full_in, full_out, ln, qg, kg, augq, augk, spread)
+    )(h, cot, full_in, full_out, ln, qg, kg, augq, augk, spread)
 
 
 def augment(image_id, token_size):
@@ -887,8 +967,8 @@
         full_gains = gather_all(own_gains[:, None], 1)
     ln, qg, kg = [full_gains[:, :, low:high].reshape(2, 1, -1).astype(F32) for low, high in zip(ends, ends[1:])]
     augq, augk = augment(image_id[section, 0], token_size[section, 0])
-    outs, grads, gain_terms, terms_in, terms_out = both_layers(
-        inputs[section, 0], cotangent[section, 0], full_in, full_out, ln, jnp.tile(qg, (1, 1, 4)), jnp.tile(kg, (1, 1, 4)),
+    outs, grads, grad_low, grad_land, gain_terms, terms_in, terms_out = both_layers(
+        blocks_fit, inputs[section, 0], cotangent[section, 0], full_in, full_out, ln, jnp.tile(qg, (1, 1, 4)), jnp.tile(kg, (1, 1, 4)),
         augq, augk, spread_matrix())
     swap = [(0, 1), (1, 0)]
 
@@ -903,19 +983,23 @@
     places = (0, D, D + HD, D + 2 * HD)
     if blocks_fit:
         totals = jnp.pad(totals, ((0, 0), (0, 1024 - places[3]))).reshape(BLOCK[2])
-        own_in, own_out, totals = scatter_terms(terms_in, terms_out, totals)
+        own_in, own_out, totals, last_land = scatter_terms(terms_in, terms_out, totals, grad_low)
+        other = jnp.where(section == 0, last_land, grad_land).astype(F32)
+        grads = jnp.where(section == 0, jnp.stack([grads, other]), jnp.stack([other, grads]))[None, :, None]
+        outs = outs[None, :, None]
         own_in, own_out = own_in[None], own_out[None]
         totals = totals.reshape(2, 1024)
     else:
         own_in = scatter_all(terms_in, 1).astype(F32)
         own_out = scatter_all(terms_out, 1).astype(F32)
         totals = lax.psum(totals, ("section", "wide"))
+        outs, grads = both_micro(outs), both_micro(grads)
     mine = lax.dynamic_index_in_dim(totals, section, 0, False)
     gain_grads = [
         lax.dynamic_slice_in_dim(mine[low:high], wide * gain.shape[1], gain.shape[1])[None]
         for low, high, gain in zip(places, places[1:], (ln_gain, q_gain, k_gain))
     ]
-    return (both_micro(outs), both_micro(grads), own_in, own_out, *gain_grads)
+    return (outs, grads, own_in, own_out, *gain_grads)
 
 
 def solution(mesh):

time: 472 us -> 454 us (0.962)
  Pallas kernels: 442 us -> 430 us
    pallas_call x1, Pallas kernels: 172 us -> 158 us  [scatter_terms(): pl.pallas_call(scatter_kernel, out_shape=tuple((jax.ShapeDtypeStruct(bloc...]
  transfers between devices with their start and end apart: 2 -> 0, of which waited for: 0 -> 0; matrix products, arithmetic and copies ran while one was open for 2% -> 0% of each run, Pallas kernels for 36% -> 0%
where the time goes in v4:
time: 454 us; the launch traced here: 453 us
  Pallas kernels  430 us (95%)
  local copies, waits for them, and re-layouts  15.5 us (3%)
  other arithmetic  6.33 us (1%)
    pallas_call x1, Pallas kernels, scatter_terms(): pl.pallas_call(scatter_kernel, out_shape=tuple((jax.ShapeDtypeStruct(bloc...  158 us
    pallas_call x1, Pallas kernels, both_layers(): pl.pallas_call(compute_kernel, grid=(STEPS,), in_specs=[whole(*square), w...  154 us
    pallas_call x1, Pallas kernels, gather_weights(): pl.pallas_call(gather_kernel, out_shape=tuple((jax.ShapeDtypeStruct(dims,...  118 us

profile of v4, /device:TPU:8, one launch (start us, length us, event | category | flops | bytes accessed | tf_op | source)
XLA Modules:
  0.0 453.0 jit_solution(1326125536957484710)
XLA Ops:
  0.6 0.0 copy-start
  0.7 0.0 copy-start.10
  0.7 0.0 copy-start.9
  0.7 0.0 copy-start.8
  0.7 0.6 copy-done
  1.3 0.7 bitcast_convert_fusion.1
  2.0 0.7 fusion.11
  2.7 0.1 pad.28.clone
  2.8 0.1 maximum_maximum_fusion.1
  2.9 0.8 copy.20.augk_ref
  3.7 2.6 dynamic-slice_bitcast_fusion
  6.3 0.1 pad.31.clone
  6.4 0.1 maximum_maximum_fusion
  6.5 0.8 copy.19.augq_ref
  7.3 0.0 copy-done.10
  7.3 0.0 copy-done.9
  7.3 0.0 copy-done.8
  7.3 0.7 fusion.10.gains
  7.9 118.5 %gather_weights.1 = (bf16[2,768,5376]{2,1,0:T(8,128)(2,1)}, bf16[2,3840,768]{2,1,0:T(8,128)(2,1)}, bf16[2,256,128]{2,1,0:T(8,128)(2,1)}) custom-call(bf16[48,5376]{1,0:T(8,128)(2,1)} %bitcast.40, bf16[240,768]{1,0:T(8,128)(2,1)} %bitcast.41, bf16[16,128]{1,0:T(8,128)(2,1)} %fusion.10.gains), custom_call_target="tpu_custom_call" | custom-call | tf_op jit(solution)/shard_map/gather_weights/pallas_call | solution.py:274
  126.4 0.9 slice.39
  127.3 0.1 slice_convert_fusion
  127.4 0.1 reshape.222
  127.5 0.7 tile.17.qg_ref
  128.2 0.1 reshape.223
  128.3 0.6 tile.19.kg_ref
  128.9 0.7 reshape.221.ln_ref
  129.6 0.8 select_convert_fusion.spread_ref
  130.3 153.8 %both_layers.1 = (bf16[2,512,768]{2,1,0:T(8,128)(2,1)}, f32[512,768]{1,0:T(8,128)}, bf16[512,768]{1,0:T(8,128)(2,1)}, bf16[512,768]{1,0:T(8,128)(2,1)}, f32[2,8,...) custom-call(bf16[512,768]{1,0:T(8,128)(2,1)} %get-tuple-element.54.h_ref, ...), custom_call_target="tpu_custom_call" | custom-call | tf_op jit(solution)/shard_map/both_layers/pallas_call | solution.py:907
  284.1 0.8 slice.35
  284.9 0.1 reshape.217
  285.0 0.1 reshape.218
  285.1 0.8 slice.34
  285.9 0.6 reshape.219.gains
  286.5 158.1 %scatter_terms.1 = (f32[48,5376]{1,0:T(8,128)}, f32[240,768]{1,0:T(8,128)}, f32[16,128]{1,0:T(8,128)}, bf16[512,768]{1,0:T(8,128)(2,1)}) custom-call(bf16[2,768,5376]{2,1,0:T(8,128)(2,1)} %get-tuple-element.26.terms_in, bf16[2,3840,768]{2,1,0:T(8,128)(2,1)} %get-tuple-element.27.terms_out, f32[16,128]{1,0:T(8,128)} %reshape.219.gains, ...), custom_call_target="tpu_custom_call" | custom-call | tf_op jit(solution)/shard_map/scatter_terms/pallas_call | solution.py:558
  444.6 0.0 copy-start.3
  444.6 0.0 copy-done.5
  444.6 1.4 bitcast_convert_fusion
  446.0 0.3 copy-done.3
  446.3 1.9 maximum_select_fusion
  448.1 0.0 copy-done.7
  448.2 0.1 fusion.12
  448.2 0.6 constant_dynamic-slice_fusion
  448.8 0.6 constant_dynamic-slice_fusion.1
  449.4 0.6 dynamic-slice.4
  450.0 0.0 copy-done.2
  450.0 1.1 copy.31
  451.1 1.0 copy.32
  452.1 0.9 copy.33
  (27 shorter events, 0.2 us)
Async XLA Ops:
  0.6 0.7 copy-start
  0.7 6.6 %copy-start.10 = (bf16[1,48]{1,0:T(2,128)(2,1)S(1)}, bf16[1,48]{1,0:T(2,128)(2,1)}, u32[]{:S(2)}) copy-start(bf16[1,48]{1,0:T(2,128)(2,1)} %param.15) | copy-start | bytes 292
  0.7 6.6 %copy-start.9 = (bf16[1,4]{1,0:T(2,128)(2,1)S(1)}, bf16[1,4]{1,0:T(2,128)(2,1)}, u32[]{:S(2)}) copy-start(bf16[1,4]{1,0:T(2,128)(2,1)} %param.16) | copy-start | bytes 28
  0.7 6.6 %copy-start.8 = (bf16[1,4]{1,0:T(2,128)(2,1)S(1)}, bf16[1,4]{1,0:T(2,128)(2,1)}, u32[]{:S(2)}) copy-start(bf16[1,4]{1,0:T(2,128)(2,1)} %param.17) | copy-start | bytes 28
  286.5 158.1 %copy-start.5 = (bf16[512,768]{1,0:T(8,128)(2,1)S(1)}, bf16[512,768]{1,0:T(8,128)(2,1)}, u32[]{:S(2)}) copy-start(bf16[512,768]{1,0:T(8,128)(2,1)} %get-tuple-element.31) | copy-start | bytes 2359300
  444.6 1.6 copy-start.3
  446.3 1.9 copy-start.7
  446.3 3.7 copy-start.2
  448.1 3.0 copy-start.4
  448.1 4.0 copy-start.6
  450.0 3.0 copy-start.1

commit v5 on v4

--- a/solution.py
+++ b/solution.py
@@ -228,57 +228,90 @@
         loop(NZ, body)
 
 
-def gather_kernel(w_in, w_out, gains, full_in, full_out, full_gains, *sems):
-    place = Place()
-    greet(place)
-    arrays = ((w_in, full_in), (w_out, full_out), (gains, full_gains))
-    first, second, third = [Gather(place, array, *arrays[array], *sems[3 * array : 3 * array + 3]) for array in range(3)]
-    copies = []
-    for array, (own, full) in enumerate(arrays):
-        rows = BLOCK[array][0]
-        copy = pltpu.make_async_copy(own, full.at[place.x, pl.ds(pl.multiple_of(place.wide * rows, 16), rows), :], sems[9].at[array])
-        copy.start()
-        copies.append(copy)
-    third.begin()
-    first.begin()
-    third.square()
-    first.square()
-
-    def early(index):
-        first.z_step(index + 1)
-        first.a_step(index)
-        third.line(index + 1)
-        first.line(index + 1)
-    loop(NZ, early)
-    second.begin()
-    second.square()
-
-    def late(index):
-        first.b_step(index)
-        second.z_step(index + 1)
-        second.a_step(index)
-        second.line(index + 1)
-    loop(NZ, late)
-    loop(NZ, second.b_step)
-    for array in (third, first, second):
-        array.from_core()
-    for copy in copies:
-        copy.wait()
-    for array in (third, first, second):
-        array.drain()
-
-
-def gather_weights(w_in, w_out, gains):
-    any_space = pl.BlockSpec(memory_space=pl.ANY)
-    dma = pltpu.SemaphoreType.DMA
-    return pl.pallas_call(
-        gather_kernel,
-        out_shape=tuple(jax.ShapeDtypeStruct(dims, jnp.bfloat16) for dims in ((2, 768, 5376), (2, 3840, 768), (2, 256, 128))),
-        in_specs=[any_space] * 3, out_specs=(any_space,) * 3,
-        scratch_shapes=[dma((5, 3, 16)), dma((3, 16)), dma((3, 16))] * 3 + [dma((3,))],
-        compiler_params=pltpu.CompilerParams(collective_id=0, has_side_effects=True),
-        name="gather_weights",
-    )(w_in, w_out, gains)
+class Weights:
+    def __init__(self, place, own, full, tiles, tile_sem, sems):
+        self.place, self.full, self.tiles, self.tile_sem = place, full, tiles, tile_sem
+        self.copies = []
+        if place is None:
+            return
+        self.inner, self.outer, self.gains = [Gather(place, array, own[array], full[array], *sems[3 * array : 3 * array + 3]) for array in range(3)]
+        for array in range(3):
+            rows = BLOCK[array][0]
+            target = full[array].at[place.x, pl.ds(pl.multiple_of(place.wide * rows, 16), rows), :]
+            self.copies.append(pltpu.make_async_copy(own[array], target, sems[9].at[array]))
+
+    def begin(self):
+        greet(self.place)
+        for copy in self.copies:
+            copy.start()
+        self.gains.begin()
+        self.inner.begin()
+        self.gains.square()
+        self.inner.square()
+
+        def early(index):
+            self.inner.z_step(index + 1)
+            self.inner.a_step(index)
+            self.gains.line(index + 1)
+            self.inner.line(index + 1)
+        loop(NZ - 1, early)
+        self.outer.begin()
+        self.inner.a_step(NZ - 1)
+        self.outer.square()
+
+        def late(index):
+            self.inner.b_step(index)
+            pl.when(index == 1)(lambda: self.onward(0))
+        loop(NZ, late)
+        self.gains.from_core()
+        self.inner.from_core()
+        for copy in self.copies:
+            copy.wait()
+
+    def onward(self, index):
+        self.outer.z_step(index + 1)
+        self.outer.a_step(index)
+        self.outer.line(index + 1)
+
+    def end(self):
+        loop(NZ, self.outer.b_step)
+        self.outer.from_core()
+
+    def drain(self):
+        for array in (self.gains, self.inner, self.outer):
+            array.drain()
+
+    def fetch(self, t):
+        slot = t % 2
+        tile, sem = self.tiles.at[slot], self.tile_sem.at[slot]
+        project = uses_in(t)
+
+        def inner():
+            layer, index = in_tile(t)
+            return pltpu.make_async_copy(self.full[0].at[layer, :, pl.ds(pl.multiple_of(index * D, D), D)], tile, sem)
+
+        def outer():
+            layer, index = out_tile(t)
+            return pltpu.make_async_copy(self.full[1].at[layer, pl.ds(pl.multiple_of(index * D, D), D), :], tile, sem)
+        pl.when(project)(lambda: inner().start())
+        pl.when(jnp.logical_not(project))(lambda: outer().start())
+
+    def wait(self, t):
+        slot = t % 2
+        pltpu.make_async_copy(self.full[0].at[0, :, pl.ds(0, D)], self.tiles.at[slot], self.tile_sem.at[slot]).wait()
+
+    def step(self, t):
+        if self.place is not None:
+            pl.when(t == 0)(self.begin)
+            pl.when((t >= 2) & (t <= NZ))(lambda: self.onward(t - 1))
+            pl.when(t == FIRST_OUT)(self.end)
+            pl.when(t == STEPS - 1)(self.drain)
+            held_back = FIRST_OUT
+        else:
+            held_back = 0
+        pl.when((t == 0) | (t == held_back))(lambda: self.fetch(t))
+        pl.when((t + 1 < STEPS) & (t + 1 != held_back))(lambda: self.fetch(t + 1))
+        self.wait(t)
 
 
 def add_into(target, source):
@@ -623,6 +656,11 @@
     return layer, jnp.where(t < SECOND_OUT, forward, backward)
 
 
+def uses_in(t):
+    forward = (t < FIRST_OUT) | ((t >= SECOND_IN) & (t < SECOND_OUT))
+    return forward | ((t >= SECOND_BACK) & (t < LAST_OUT)) | (t >= LAST_BACK)
+
+
 def out_tile(t):
     layer = ((t >= SECOND_IN) & (t < SECOND_BACK)).astype(jnp.int32)
     tile = jnp.where(t < SECOND_IN, clip(t - FIRST_OUT, 4), jnp.where(t < SECOND_BACK, clip(t - SECOND_OUT, 4), clip(t - LAST_OUT, 4)))
@@ -640,9 +678,29 @@
     return 1 - late.astype(jnp.int32), jnp.where(late, clip(t - LAST_OUT, 4), clip(t - SECOND_OUT, 4))
 
 
-def compute_kernel(h_ref, cot_ref, w_in_ref, w_out_ref, ln_ref, qg_ref, kg_ref, augq_ref, augk_ref, spread_ref,
-                   section_out, grad_ref, grad_low, grad_land, gain_ref, terms_in_ref, terms_out_ref,
-                   hidden, normed, scale, q, k, v, rq, rk, linv, slope, combined, dy, dproj, acc, dq, dk, do, dhigh, dlow, *swap):
+def gains_of(rows, width, start, count, columns):
+    lane, column = lax.broadcasted_iota(jnp.int32, (128, columns), 0), lax.broadcasted_iota(jnp.int32, (128, columns), 1)
+    place = column % (count * width)
+    picked = dot(rows, jnp.where(lane == start + place % count, 1.0, 0.0).astype(BF16))
+    row = lax.broadcasted_iota(jnp.int32, picked.shape, 0)
+    owner = (lax.broadcasted_iota(jnp.int32, picked.shape, 1) % (count * width)) // count
+    return jnp.sum(jnp.where(row == owner * BLOCK[2][0], picked, 0.0), 0, keepdims=True)
+
+
+def compute_kernel(trading, counts, *refs):
+    if trading:
+        own, refs = refs[:3], refs[3:]
+        (h_ref, cot_ref, augq_ref, augk_ref, spread_ref, section_out, grad_ref, grad_low, grad_land, gain_ref, terms_in_ref, terms_out_ref,
+         full_in, full_out) = refs[:14]
+        sems, swap, refs = refs[14:24], refs[24:27], refs[27:]
+    else:
+        (full_in, full_out, full_gains, h_ref, cot_ref, augq_ref, augk_ref, spread_ref, section_out, grad_ref, grad_low, grad_land,
+         gain_ref, terms_in_ref, terms_out_ref) = refs[:15]
+        own, sems, swap, refs = None, None, (), refs[15:]
+    if trading:
+        full_gains, refs = refs[0], refs[1:]
+    (tiles, tile_sem, ln_ref, qg_ref, kg_ref, hidden, normed, scale, q, k, v, rq, rk, linv, slope, combined, dy, dproj, acc, dq, dk, do,
+     dhigh, dlow) = refs
     t = pl.program_id(0)
     layer = in_tile(t)[0]
     project = (t < FIRST_OUT) | ((t >= SECOND_IN) & (t < SECOND_OUT))
@@ -656,6 +714,9 @@
     if swap:
         trade = Trade(section, section_out, hidden, dy, grad_land, *swap)
     spread = spread_ref[...]
+    weights = Weights(Place() if trading else None, own, (full_in, full_out, full_gains), tiles, tile_sem, sems)
+    weights.step(t)
+    w_ref = tiles.at[t % 2]
 
     def halves(width=256):
         def run(body):
@@ -670,9 +731,12 @@
     @pl.when(t == 0)
     def _():
         hidden[0] = h_ref[...]
-        if trade:
-            trade.greet()
         gain_ref[...] = jnp.zeros_like(gain_ref)
+        starts = (0, counts[0], counts[0] + counts[1])
+        for which in range(2):
+            rows = full_gains[which]
+            for target, start, count, columns in zip((ln_ref, qg_ref, kg_ref), starts, counts, (D, 256, 256)):
+                target[which] = gains_of(rows, D // counts[0], start, count, columns)
 
     def low_lanes():
         return lax.broadcasted_iota(jnp.int32, (SLOTS, 128), 1) < HD
@@ -689,7 +753,7 @@
 
     @pl.when(project)
     def _():
-        acc[...] = dot(normed[layer], w_in_ref[...])
+        acc[...] = dot(normed[layer], w_ref[...])
 
         def heads(low_ref, root_ref, gain, factor):
             @halves()
@@ -733,7 +797,7 @@
 
     @pl.when(output | output_both)
     def _():
-        product = dot(combined[layer, tile], w_out_ref[...])
+        product = dot(combined[layer, tile], w_ref[...])
         pl.when(tile == 0)(lambda: dq.__setitem__(..., hidden[layer].astype(F32) + product))
         pl.when(tile > 0)(lambda: dq.__setitem__(..., dq[...] + product))
 
@@ -752,7 +816,7 @@
 
     @pl.when(output_both | back)
     def _():
-        acc[...] = dot(dy[...], w_out_ref[...], ACROSS)
+        acc[...] = dot(dy[...], w_ref[...], ACROSS)
         terms_out_ref[...] = dot(combined[layer, tile], dy[...], DOWN).astype(BF16)
 
         @pl.when(tile == 0)
@@ -813,7 +877,7 @@
 
     @pl.when(project_back)
     def _():
-        product = dot(dproj[tile], w_in_ref[...], ACROSS)
+        product = dot(dproj[tile], w_ref[...], ACROSS)
         pl.when(tile == up_first(0))(lambda: acc.__setitem__(..., product))
         pl.when(tile != up_first(0))(lambda: acc.__setitem__(..., acc[...] + product))
         terms_in_ref[...] = dot(normed[layer], dproj[tile], DOWN).astype(BF16)
@@ -849,11 +913,6 @@
         self.own_sem, self.send_sem, self.recv_sem = own_sem, send_sem, recv_sem
         self.pair = (1 - section, lax.axis_index("wide"))
 
-    def greet(self):
-        barrier = pltpu.get_barrier_semaphore()
-        pl.semaphore_signal(barrier, inc=1, device_id=self.pair, device_id_type=MESH)
-        pl.semaphore_wait(barrier, 1)
-
     def kept(self):
         return pltpu.make_async_copy(self.hidden.at[self.section + 1], self.section_out.at[self.section], self.own_sem)
 
@@ -883,48 +942,46 @@
         pl.when(self.section == 1)(lambda: self.grad().wait_recv())
 
 
-def both_layers(trading, h, cot, full_in, full_out, ln, qg, kg, augq, augk, spread):
+def both_layers(trading, counts, weights, gains, h, cot, augq, augk, spread):
     square = (SLOTS, D)
 
     def whole(*dims):
         return pl.BlockSpec(dims, lambda t: (0,) * len(dims))
 
-    def of_columns(where):
-        return pl.BlockSpec((None, D, D), lambda t: (where(t)[0], 0, where(t)[1]))
-
-    def of_rows(where):
-        return pl.BlockSpec((None, D, D), lambda t: (where(t)[0], where(t)[1], 0))
-
     low, wide = (lambda *dims: pltpu.VMEM(dims, BF16)), (lambda *dims: pltpu.VMEM(dims, F32))
     any_space, dma = pl.BlockSpec(memory_space=pl.ANY), pltpu.SemaphoreType.DMA
+    full = [jax.ShapeDtypeStruct(dims, BF16) for dims in ((2, D, TILES_IN * D), (2, TILES_OUT * D, D))]
     if trading:
-        out_specs = [any_space, whole(*square), whole(*square), any_space]
-        grad_shape, extra = square, [dma(()), dma((2,)), dma((2,))]
+        in_specs, operands = [any_space] * 3, (*weights, gains)
+        out_specs, more_specs = [any_space, whole(*square), whole(*square), any_space], [any_space] * 2
+        sems = [dma((5, 3, 16)), dma((3, 16)), dma((3, 16))] * 3 + [dma((3,))]
+        grad_shape, extra, more = square, sems + [dma(()), dma((2,)), dma((2,)), low(2, 16 * BLOCK[2][0], 128)], full
         params = dict(collective_id=2, has_side_effects=True)
     else:
-        out_specs = [whole(2, *square), whole(2, *square), whole(*square), whole(*square)]
-        grad_shape, extra, params = (2,) + square, [], {}
+        in_specs, operands = [any_space] * 2 + [whole(*gains.shape)], (*weights, gains)
+        out_specs, more_specs = [whole(2, *square), whole(2, *square), whole(*square), whole(*square)], []
+        grad_shape, extra, more, params = (2,) + square, [], [], {}
     return pl.pallas_call(
-        compute_kernel,
+        functools.partial(compute_kernel, trading, counts),
         grid=(STEPS,),
-        in_specs=[
-            whole(*square), whole(*square), of_columns(in_tile), of_rows(out_tile), whole(2, 1, D), whole(2, 1, 256), whole(2, 1, 256),
-            whole(SLOTS, 128), whole(SLOTS, 128), whole(256, 256),
-        ],
-        out_specs=out_specs + [whole(2, 8, D), of_columns(in_terms), of_rows(out_terms)],
-        scratch_shapes=[
+        in_specs=in_specs + [whole(*square), whole(*square), whole(SLOTS, 128), whole(SLOTS, 128), whole(256, 256)],
+        out_specs=out_specs + [
+            whole(2, 8, D), pl.BlockSpec((None, D, D), lambda t: (in_terms(t)[0], 0, in_terms(t)[1])),
+            pl.BlockSpec((None, D, D), lambda t: (out_terms(t)[0], out_terms(t)[1], 0)),
+        ] + more_specs,
+        scratch_shapes=extra + [
+            low(2, D, D), dma((2,)), wide(2, 1, D), wide(2, 1, 256), wide(2, 1, 256),
             low(3, *square), low(2, *square), wide(2, SLOTS, 128), low(2, *square), low(2, *square), low(2, *square), low(2, *square),
             low(2, *square), wide(2, *square), low(2, 4, *square), low(2, 5, *square), low(*square), low(7, *square), wide(*square),
             wide(*square), wide(*square), low(*square), low(*square), low(*square),
-        ] + extra,
+        ],
         out_shape=[
             jax.ShapeDtypeStruct((2,) + square, BF16), jax.ShapeDtypeStruct(grad_shape, F32), jax.ShapeDtypeStruct(square, BF16),
-            jax.ShapeDtypeStruct(square, BF16), jax.ShapeDtypeStruct((2, 8, D), F32), jax.ShapeDtypeStruct(full_in.shape, BF16),
-            jax.ShapeDtypeStruct(full_out.shape, BF16),
-        ],
+            jax.ShapeDtypeStruct(square, BF16), jax.ShapeDtypeStruct((2, 8, D), F32), *full,
+        ] + more,
         compiler_params=pltpu.CompilerParams(vmem_limit_bytes=63 * 2**20, **params),
         name="both_layers",
-    )(h, cot, full_in, full_out, ln, qg, kg, augq, augk, spread)
+    )(*operands, h, cot, augq, augk, spread)[:7]
 
 
 def augment(image_id, token_size):
@@ -958,18 +1015,15 @@
     for gain in (ln_gain, q_gain, k_gain):
         ends.append(ends[-1] + gain.shape[1])
     own_gains = jnp.concatenate([ln_gain, q_gain, k_gain], 1)
-    if blocks_fit:
-        padded = jnp.pad(own_gains, ((0, BLOCK[2][0] - 1), (0, BLOCK[2][1] - ends[3])))
-        full_in, full_out, full_gains = gather_weights(w_in[0], w_out[0], padded)
-        full_gains = full_gains.reshape((2, width) + BLOCK[2])[:, :, 0]
-    else:
-        full_in, full_out = gather_all(w_in, 1), gather_all(w_out, 1)
-        full_gains = gather_all(own_gains[:, None], 1)
-    ln, qg, kg = [full_gains[:, :, low:high].reshape(2, 1, -1).astype(F32) for low, high in zip(ends, ends[1:])]
+    gains = jnp.pad(own_gains, ((0, BLOCK[2][0] - 1), (0, BLOCK[2][1] - ends[3])))
+    weights = (w_in[0], w_out[0])
+    if not blocks_fit:
+        weights = (gather_all(w_in, 1), gather_all(w_out, 1))
+        gains = gather_all(gains[None], 1)
     augq, augk = augment(image_id[section, 0], token_size[section, 0])
     outs, grads, grad_low, grad_land, gain_terms, terms_in, terms_out = both_layers(
-        blocks_fit, inputs[section, 0], cotangent[section, 0], full_in, full_out, ln, jnp.tile(qg, (1, 1, 4)), jnp.tile(kg, (1, 1, 4)),
-        augq, augk, spread_matrix())
+        blocks_fit, tuple(gain.shape[1] for gain in (ln_gain, q_gain, k_gain)), weights, gains, inputs[section, 0],
+        cotangent[section, 0], augq, augk, spread_matrix())
     swap = [(0, 1), (1, 0)]
 
     def both_micro(pair):

time: 454 us -> 440 us (0.969)
  Pallas kernels: 430 us -> 420 us
    pallas_call x2 -> x1, Pallas kernels: 272 us -> 257 us  [both_layers(): pl.pallas_call(functools.partial(compute_kernel, trading, counts), grid=(...]
    pallas_call x1, Pallas kernels: 158 us -> 163 us  [scatter_terms(): pl.pallas_call(scatter_kernel, out_shape=tuple((jax.ShapeDtypeStruct(bloc...]
where the time goes in v5:
time: 440 us; the launch traced here: 439 us
  Pallas kernels  420 us (95%)
  local copies, waits for them, and re-layouts  12.5 us (3%)
  other arithmetic  6.24 us (1%)
    pallas_call x1, Pallas kernels, both_layers(): pl.pallas_call(functools.partial(compute_kernel, trading, counts), grid=(...  257 us
    pallas_call x1, Pallas kernels, scatter_terms(): pl.pallas_call(scatter_kernel, out_shape=tuple((jax.ShapeDtypeStruct(bloc...  163 us

profile of v5, /device:TPU:8, one launch (start us, length us, event | category | flops | bytes accessed | tf_op | source)
XLA Modules:
  0.0 439.3 jit_solution(5503883585952527141)
XLA Ops:
  0.6 0.0 copy-start
  0.7 0.0 copy-start.10
  0.7 0.0 copy-start.9
  0.7 0.0 copy-start.8
  0.7 0.6 copy-done
  1.3 0.7 bitcast_convert_fusion.1
  2.0 0.7 fusion.11
  2.7 0.1 pad.28.clone
  2.8 0.1 maximum_maximum_fusion.1
  2.9 0.8 copy.18.refs_6_
  3.7 2.6 dynamic-slice_bitcast_fusion
  6.3 0.1 pad.31.clone
  6.4 0.1 maximum_maximum_fusion
  6.5 0.8 copy.17.refs_5_
  7.3 0.8 select_convert_fusion.refs_7_
  8.0 0.0 copy-done.10
  8.0 0.0 copy-done.9
  8.0 0.0 copy-done.8
  8.0 0.7 fusion.10.refs_2_
  8.7 256.9 %both_layers.1 = (bf16[2,512,768]{2,1,0:T(8,128)(2,1)}, f32[512,768]{1,0:T(8,128)}, bf16[512,768]{1,0:T(8,128)(2,1)}, bf16[512,768]{1,0:T(8,128)(2,1)}, f32[2,8,...) custom-call(bf16[48,5376]{1,0:T(8,128)(2,1)} %bitcast.36, ...), custom_call_target="tpu_custom_call" | custom-call | tf_op jit(solution)/shard_map/both_layers/pallas_call | solution.py:964
  265.6 0.8 slice.19
  266.4 0.1 reshape.166
  266.5 0.1 reshape.167
  266.6 0.8 slice.18
  267.4 0.6 reshape.168.gains
  268.0 0.0 copy-start.5
  268.0 162.9 %scatter_terms.1 = (f32[48,5376]{1,0:T(8,128)}, f32[240,768]{1,0:T(8,128)}, f32[16,128]{1,0:T(8,128)}, bf16[512,768]{1,0:T(8,128)(2,1)}) custom-call(bf16[2,768,5376]{2,1,0:T(8,128)(2,1)} %get-tuple-element.20.terms_in, bf16[2,3840,768]{2,1,0:T(8,128)(2,1)} %get-tuple-element.21.terms_out, f32[16,128]{1,0:T(8,128)} %reshape.168.gains, ...), custom_call_target="tpu_custom_call" | custom-call | tf_op jit(solution)/shard_map/scatter_terms/pallas_call | solution.py:591
  431.0 0.0 copy-start.3
  431.0 0.0 copy-done.5
  431.0 1.4 bitcast_convert_fusion
  432.4 0.3 copy-done.3
  432.6 0.0 copy-start.7
  432.6 0.0 copy-start.2
  432.6 1.9 maximum_select_fusion
  434.5 0.0 copy-start.4
  434.5 0.0 copy-start.6
  434.5 0.0 copy-done.7
  434.5 0.1 fusion.12
  434.6 0.6 constant_dynamic-slice_fusion
  435.2 0.6 constant_dynamic-slice_fusion.1
  435.8 0.6 dynamic-slice.4
  436.3 0.0 copy-done.2
  436.3 1.1 copy.26
  437.5 0.0 copy-done.4
  437.5 1.0 copy.27
  438.5 0.0 copy-done.6
  438.5 0.9 copy.28
  439.3 0.0 copy-done.1
  (15 shorter events, 0.1 us)
Async XLA Ops:
  0.6 0.7 copy-start
  0.7 7.4 %copy-start.10 = (bf16[1,48]{1,0:T(2,128)(2,1)S(1)}, bf16[1,48]{1,0:T(2,128)(2,1)}, u32[]{:S(2)}) copy-start(bf16[1,48]{1,0:T(2,128)(2,1)} %param.15) | copy-start | bytes 292
  0.7 7.4 %copy-start.9 = (bf16[1,4]{1,0:T(2,128)(2,1)S(1)}, bf16[1,4]{1,0:T(2,128)(2,1)}, u32[]{:S(2)}) copy-start(bf16[1,4]{1,0:T(2,128)(2,1)} %param.16) | copy-start | bytes 28
  0.7 7.4 %copy-start.8 = (bf16[1,4]{1,0:T(2,128)(2,1)S(1)}, bf16[1,4]{1,0:T(2,128)(2,1)}, u32[]{:S(2)}) copy-start(bf16[1,4]{1,0:T(2,128)(2,1)} %param.17) | copy-start | bytes 28
  268.0 163.0 %copy-start.5 = (bf16[512,768]{1,0:T(8,128)(2,1)S(1)}, bf16[512,768]{1,0:T(8,128)(2,1)}, u32[]{:S(2)}) copy-start(bf16[512,768]{1,0:T(8,128)(2,1)} %get-tuple-element.25) | copy-start | bytes 2359300
  431.0 1.6 copy-start.3
  432.6 1.9 copy-start.7
  432.6 3.7 copy-start.2
  434.5 3.0 copy-start.4
  434.5 4.0 copy-start.6
  436.3 3.0 copy-start.1

commit v6 on v5

--- a/solution.py
+++ b/solution.py
@@ -41,8 +41,8 @@
         return self.at(self.x, self.y, self.z, 1 - self.c)
 
 
-def greet(place):
-    barrier = pltpu.get_barrier_semaphore()
+def greet(place, barrier=None):
+    barrier = pltpu.get_barrier_semaphore() if barrier is None else barrier
     x, y, z = place.x, place.y, place.z
 
     def signal(device):
@@ -282,7 +282,7 @@
             array.drain()
 
     def fetch(self, t):
-        slot = t % 2
+        slot = tile_slot(t)
         tile, sem = self.tiles.at[slot], self.tile_sem.at[slot]
         project = uses_in(t)
 
@@ -297,7 +297,7 @@
         pl.when(jnp.logical_not(project))(lambda: outer().start())
 
     def wait(self, t):
-        slot = t % 2
+        slot = tile_slot(t)
         pltpu.make_async_copy(self.full[0].at[0, :, pl.ds(0, D)], self.tiles.at[slot], self.tile_sem.at[slot]).wait()
 
     def step(self, t):
@@ -305,13 +305,14 @@
             pl.when(t == 0)(self.begin)
             pl.when((t >= 2) & (t <= NZ))(lambda: self.onward(t - 1))
             pl.when(t == FIRST_OUT)(self.end)
-            pl.when(t == STEPS - 1)(self.drain)
+            pl.when(t == LAST_OUT)(self.drain)
             held_back = FIRST_OUT
         else:
             held_back = 0
+        following = jnp.where(t == LAST_HEADS - 1, LAST_PROJECT, t + 1)
         pl.when((t == 0) | (t == held_back))(lambda: self.fetch(t))
-        pl.when((t + 1 < STEPS) & (t + 1 != held_back))(lambda: self.fetch(t + 1))
-        self.wait(t)
+        pl.when(has_tile(t) & (following < STEPS) & (following != held_back))(lambda: self.fetch(following))
+        pl.when(has_tile(t))(lambda: self.wait(t))
 
 
 def add_into(target, source):
@@ -330,13 +331,13 @@
         self.send_sem, self.recv_sem, self.rest_send, self.rest_recv, self.core_send, self.core_recv, self.local_sem = sems
 
     def part(self, block, colour):
-        return cut(self.held.at[number_of(block)], SCATTER_CUTS, self.array, colour)
+        return cut(self.held(number_of(block)), SCATTER_CUTS, self.array, colour)
 
     def copy(self, device, block, colour, slot):
         if colour is None:
-            target, send_sem, recv_sem = self.rest_land.at[slot], self.rest_send.at[slot], self.rest_recv.at[slot]
+            target, send_sem, recv_sem = self.rest_land(slot), self.rest_send.at[slot], self.rest_recv.at[slot]
         else:
-            target, send_sem, recv_sem = self.land.at[colour * 20 + slot], self.send_sem.at[colour, slot], self.recv_sem.at[colour, slot]
+            target, send_sem, recv_sem = self.land(colour, slot), self.send_sem.at[colour, slot], self.recv_sem.at[colour, slot]
         return pltpu.make_async_remote_copy(
             src_ref=self.part(block, colour), dst_ref=target, send_sem=send_sem, recv_sem=recv_sem, device_id=device,
             device_id_type=MESH)
@@ -348,7 +349,7 @@
     def arrive(self, block, colour, slot, drain):
         if not drain:
             self.copy(self.place.sibling(), block, colour, slot).wait_recv()
-            add_into(self.part(block, colour), self.rest_land.at[slot] if colour is None else self.land.at[colour * 20 + slot])
+            add_into(self.part(block, colour), self.rest_land(slot) if colour is None else self.land(colour, slot))
 
     def core_copy(self, block, mine):
         rows = BLOCK[self.array][0]
@@ -357,9 +358,9 @@
         start = (block[2] * 4 + block[1] * 2 + (place.c if mine else 1 - place.c)) * rows
         source = self.terms.at[block[0], pl.ds(pl.multiple_of(start, 16), rows), :]
         if mine:
-            return pltpu.make_async_copy(source, self.held.at[number], self.local_sem.at[number])
+            return pltpu.make_async_copy(source, self.held(number), self.local_sem.at[number])
         return pltpu.make_async_remote_copy(
-            src_ref=source, dst_ref=self.core_land.at[number], send_sem=self.core_send.at[number],
+            src_ref=source, dst_ref=self.core_land(number), send_sem=self.core_send.at[number],
             recv_sem=self.core_recv.at[number], device_id=place.sibling(), device_id_type=MESH)
 
     def sided(self, distance, body):
@@ -393,7 +394,7 @@
                     self.core_copy(block, True).wait()
                     copy = self.core_copy(block, False)
                     copy.wait_recv()
-                    add_into(self.held.at[number_of(block)], self.core_land.at[number_of(block)])
+                    add_into(self.held(number_of(block)), self.core_land(number_of(block)))
                     copy.wait_send()
 
                 def out(colour):
@@ -476,6 +477,39 @@
         self.square(True)
 
 
+    MICRO = 19
+
+    def begin(self):
+        loop(NZ, lambda index: self.start(NZ - 1 - index))
+
+    def micro(self, index):
+        distance = NZ - 1 - index // 4
+        turn = jnp.where(index < 16, index % 4, index - 12)
+        pl.when(turn == 0)(lambda: self.k_step(distance))
+        pl.when(turn == 1)(lambda: self.line(distance))
+
+        @pl.when((turn == 2) | (turn == 5))
+        def _():
+            self.b_step(jnp.where(turn == 2, distance + 1, 0))
+
+        @pl.when((turn == 2) | (turn == 6))
+        def _():
+            self.z_step(jnp.where(turn == 2, distance + 1, 0))
+        pl.when(turn == 3)(lambda: self.a_step(distance))
+        pl.when(turn == 4)(self.square)
+
+    def finish(self, result, sem):
+        copy = pltpu.make_async_copy(self.held(number_of((self.place.x, self.place.y, self.place.z))), result, sem)
+        copy.start()
+        self.drain()
+        copy.wait()
+
+
+def scatter_sems():
+    dma = pltpu.SemaphoreType.DMA
+    return [dma((2, 20)), dma((2, 20)), dma((35,)), dma((35,)), dma((16,)), dma((16,)), dma((16,)), dma(())]
+
+
 class Total:
     def __init__(self, place, own, out, run, land, send_sem, recv_sem):
         self.place, self.own, self.out, self.run, self.land = place, own, out, run, land
@@ -531,71 +565,43 @@
                 pl.when(sent)(lambda: self.copy(link).wait_send())
 
 
-def scatter_kernel(terms_in, terms_out, gains, grad, out_in, out_out, out_gains, grad_land, *rest):
+def scatter_kernel(terms, gains, grad, result, out_gains, grad_land, held, core_land, land, rest_land, run, small_land, send_sem, recv_sem,
+                   grad_sem, *sems):
     place = Place()
     greet(place)
     grad_copy = pltpu.make_async_remote_copy(
-        src_ref=grad, dst_ref=grad_land, send_sem=rest[26].at[0], recv_sem=rest[26].at[1],
+        src_ref=grad, dst_ref=grad_land, send_sem=grad_sem.at[0], recv_sem=grad_sem.at[1],
         device_id=place.at(1 - place.x, place.y, place.z), device_id_type=MESH)
-    pl.when(place.x == 1)(lambda: grad_copy.start())
-    total = Total(place, gains, out_gains, *rest[22:26])
-    arrays = [Scatter(place, array, (terms_in, terms_out)[array], *rest[4 * array : 4 * array + 4], rest[8 + 7 * array : 15 + 7 * array])
-              for array in range(2)]
-    order = arrays[::-1]
-
-    def begin(index):
-        for array in order:
-            array.start(NZ - 1 - index)
-    loop(NZ, begin)
+    total = Total(place, gains, out_gains, run, small_land, send_sem, recv_sem)
+    scatter = Scatter(place, 0, terms, lambda number: held.at[number], lambda number: core_land.at[number],
+                      lambda colour, slot: land.at[colour * 20 + slot], lambda slot: rest_land.at[slot], sems[:7])
+    scatter.begin()
 
     def body(index):
-        distance = NZ - 1 - index
-        for array in order:
-            array.k_step(distance)
-        total.step(index)
-        for array in order:
-            array.line(distance + 1)
-        for array in order:
-            array.a_step(distance + 1)
-        for array in order:
-            array.b_step(distance + 2)
-            array.z_step(distance + 2)
-    loop(NZ + 2, body)
-    for array in order:
-        array.square()
-    for array, out in zip(arrays, (out_in, out_out)):
-        number = number_of((place.x, place.y, place.z))
-
-        def last(step):
-            part = pl.ds(pl.multiple_of(step * 16, 16), 16)
-            out[part, :] = array.held[number, part, :].astype(jnp.float32)
-        loop(out.shape[0] // 16, last)
-    for array in order:
-        array.drain()
+        scatter.micro(index)
+        pl.when(index % 4 == 0)(lambda: total.step(index // 4))
+        pl.when((index == 15) & (place.x == 1))(lambda: grad_copy.start())
+    loop(Scatter.MICRO, body)
+    scatter.finish(result, sems[7])
     total.drain()
     pl.when(place.x == 1)(lambda: grad_copy.wait_send())
     pl.when(place.x == 0)(lambda: grad_copy.wait_recv())
 
 
-def scatter_terms(terms_in, terms_out, gains, grad):
-    any_space = pl.BlockSpec(memory_space=pl.ANY)
-    vmem = pl.BlockSpec(memory_space=pltpu.VMEM)
-    dma = pltpu.SemaphoreType.DMA
-    buffers, sems = [], []
-    for array in range(2):
-        buffers += [pltpu.VMEM((16,) + BLOCK[array], jnp.bfloat16)] * 2
-        buffers += [
-            pltpu.VMEM((count,) + part_shape(SCATTER_CUTS, array, colour), jnp.bfloat16) for count, colour in ((40, 0), (35, None))]
-        sems += [dma((2, 20)), dma((2, 20)), dma((35,)), dma((35,)), dma((16,)), dma((16,)), dma((16,))]
-    small = [pltpu.VMEM((5,) + BLOCK[2], jnp.float32)] * 2 + [dma((5,))] * 2 + [dma((2,))]
+def scatter_terms(terms, gains, grad):
+    any_space, vmem, dma = pl.BlockSpec(memory_space=pl.ANY), pl.BlockSpec(memory_space=pltpu.VMEM), pltpu.SemaphoreType.DMA
+    low = lambda *dims: pltpu.VMEM(dims, jnp.bfloat16)
     return pl.pallas_call(
         scatter_kernel,
-        out_shape=tuple(jax.ShapeDtypeStruct(block, jnp.float32) for block in BLOCK) + (jax.ShapeDtypeStruct(grad.shape, grad.dtype),),
-        in_specs=[any_space] * 2 + [vmem, any_space], out_specs=(vmem,) * 3 + (any_space,),
-        scratch_shapes=buffers + sems + small,
-        compiler_params=pltpu.CompilerParams(collective_id=1, has_side_effects=True, vmem_limit_bytes=58 * 2**20),
+        out_shape=(jax.ShapeDtypeStruct(BLOCK[0], jnp.bfloat16), jax.ShapeDtypeStruct(BLOCK[2], jnp.float32),
+                   jax.ShapeDtypeStruct(grad.shape, grad.dtype)),
+        in_specs=[any_space, vmem, any_space], out_specs=(any_space, vmem, any_space),
+        scratch_shapes=[
+            low(16, *BLOCK[0]), low(16, *BLOCK[0]), low(40, *part_shape(SCATTER_CUTS, 0, 0)), low(35, *part_shape(SCATTER_CUTS, 0, None)),
+            *[pltpu.VMEM((5,) + BLOCK[2], jnp.float32)] * 2, dma((5,)), dma((5,)), dma((2,)), *scatter_sems()],
+        compiler_params=pltpu.CompilerParams(collective_id=1, has_side_effects=True, vmem_limit_bytes=48 * 2**20),
         name="scatter_terms",
-    )(terms_in, terms_out, gains, grad)
+    )(terms, gains, grad)
 
 
 SLOTS, D, HD, PAIRS = 512, 768, 64, 6
@@ -637,7 +643,7 @@
     return pl.ds(pl.multiple_of(index * width, width), width)
 
 
-FIRST_OUT, SECOND_IN, SECOND_OUT, SECOND_BACK, LAST_OUT, LAST_BACK, STEPS = 7, 12, 19, 24, 31, 36, 43
+FIRST_OUT, SECOND_IN, SECOND_OUT, SECOND_BACK, LAST_OUT, LAST_BACK, LAST_HEADS, LAST_PROJECT, STEPS = 7, 12, 19, 24, 31, 36, 40, 46, 49
 LAST_TILE = 2
 
 
@@ -647,18 +653,30 @@
 
 def clip(index, high):
     return jnp.clip(index, 0, high)
+
+
+def last_back(t):
+    return up_first(jnp.where(t < LAST_HEADS, clip(t - LAST_BACK, 3), 4 + clip(t - LAST_PROJECT, 2)))
 
 
 def in_tile(t):
     layer = ((t >= FIRST_OUT) & (t < LAST_OUT)).astype(jnp.int32)
     forward = jnp.where(t < FIRST_OUT, t, clip(t - SECOND_IN, 6))
-    backward = up_first(jnp.where(t < LAST_OUT, clip(t - SECOND_BACK, 6), clip(t - LAST_BACK, 6)))
+    backward = jnp.where(t < LAST_OUT, up_first(clip(t - SECOND_BACK, 6)), last_back(t))
     return layer, jnp.where(t < SECOND_OUT, forward, backward)
+
+
+def has_tile(t):
+    return (t < LAST_HEADS) | (t >= LAST_PROJECT)
+
+
+def tile_slot(t):
+    return (t - (LAST_PROJECT - LAST_HEADS) * (t >= LAST_PROJECT)) % 2
 
 
 def uses_in(t):
     forward = (t < FIRST_OUT) | ((t >= SECOND_IN) & (t < SECOND_OUT))
-    return forward | ((t >= SECOND_BACK) & (t < LAST_OUT)) | (t >= LAST_BACK)
+    return forward | ((t >= SECOND_BACK) & (t < LAST_OUT)) | ((t >= LAST_BACK) & has_tile(t))
 
 
 def out_tile(t):
@@ -669,13 +687,7 @@
 
 def in_terms(t):
     late = t >= LAST_BACK
-    tile = up_first(jnp.where(late, t - LAST_BACK, clip(t - SECOND_BACK, 6)))
-    return 1 - late.astype(jnp.int32), tile
-
-
-def out_terms(t):
-    late = t >= LAST_OUT
-    return 1 - late.astype(jnp.int32), jnp.where(late, clip(t - LAST_OUT, 4), clip(t - SECOND_OUT, 4))
+    return 1 - late.astype(jnp.int32), jnp.where(late, last_back(t), up_first(clip(t - SECOND_BACK, 6)))
 
 
 def gains_of(rows, width, start, count, columns):
@@ -690,24 +702,24 @@
 def compute_kernel(trading, counts, *refs):
     if trading:
         own, refs = refs[:3], refs[3:]
-        (h_ref, cot_ref, augq_ref, augk_ref, spread_ref, section_out, grad_ref, grad_low, grad_land, gain_ref, terms_in_ref, terms_out_ref,
-         full_in, full_out) = refs[:14]
-        sems, swap, refs = refs[14:24], refs[24:27], refs[27:]
     else:
-        (full_in, full_out, full_gains, h_ref, cot_ref, augq_ref, augk_ref, spread_ref, section_out, grad_ref, grad_low, grad_land,
-         gain_ref, terms_in_ref, terms_out_ref) = refs[:15]
-        own, sems, swap, refs = None, None, (), refs[15:]
+        (full_in, full_out, full_gains), refs, own = refs[:3], refs[3:], None
+    (inputs, cotangent, augq_ref, augk_ref, spread_ref, section_out, grad_ref, grad_low, grad_land, gain_ref, terms_in_ref, terms_out), refs = (
+        refs[:12], refs[12:])
+    (tiles, tile_sem, ln_ref, qg_ref, kg_ref, hidden, saved, scale, slope, combined, dy, dproj, acc, dq, dk, do, dhigh, dlow, terms_tile,
+     terms_sem, entry_sem), refs = (refs[:21], refs[21:]) if not trading else (refs[3:24], refs[:3] + refs[24:])
+    sems, swap, scatter_refs = None, (), None
     if trading:
-        full_gains, refs = refs[0], refs[1:]
-    (tiles, tile_sem, ln_ref, qg_ref, kg_ref, hidden, normed, scale, q, k, v, rq, rk, linv, slope, combined, dy, dproj, acc, dq, dk, do,
-     dhigh, dlow) = refs
+        (full_in, full_out, own_out, full_gains), sems, swap, scatter_refs = refs[:4], refs[4:14], refs[14:17], refs[17:]
+    normed, q, k, v, rq, rk, linv = [Saved(saved, which) for which in range(7)]
     t = pl.program_id(0)
     layer = in_tile(t)[0]
     project = (t < FIRST_OUT) | ((t >= SECOND_IN) & (t < SECOND_OUT))
-    project_back = ((t >= SECOND_BACK) & (t < LAST_OUT)) | (t >= LAST_BACK)
+    project_back = ((t >= SECOND_BACK) & (t < LAST_OUT)) | ((t >= LAST_BACK) & has_tile(t))
     output = (t >= FIRST_OUT) & (t < SECOND_IN)
     output_both = (t >= SECOND_OUT) & (t < SECOND_BACK)
     back = (t >= LAST_OUT) & (t < LAST_BACK)
+    heads_now = (t == SECOND_BACK + 4) | ((t >= LAST_HEADS) & (t < LAST_PROJECT))
     layer = jnp.where(output, 0, layer)
     tile = jnp.where(project | project_back, in_tile(t)[1], out_tile(t)[1])
     section, trade = lax.axis_index("section"), None
@@ -716,7 +728,9 @@
     spread = spread_ref[...]
     weights = Weights(Place() if trading else None, own, (full_in, full_out, full_gains), tiles, tile_sem, sems)
     weights.step(t)
-    w_ref = tiles.at[t % 2]
+    w_ref = tiles.at[tile_slot(t)]
+    if trading:
+        pl.when(t >= LAST_BACK)(lambda: outer_scatter(t, terms_out, terms_tile, terms_sem, own_out, combined, slope, saved, *scatter_refs))
 
     def halves(width=256):
         def run(body):
@@ -730,7 +744,12 @@
 
     @pl.when(t == 0)
     def _():
-        hidden[0] = h_ref[...]
+        entries = [pltpu.make_async_copy(inputs.at[section, 0], hidden.at[0], entry_sem.at[0]),
+                   pltpu.make_async_copy(cotangent.at[section, 0], dy, entry_sem.at[1])]
+        for entry in entries:
+            entry.start()
+        for entry in entries:
+            entry.wait()
         gain_ref[...] = jnp.zeros_like(gain_ref)
         starts = (0, counts[0], counts[0] + counts[1])
         for which in range(2):
@@ -753,7 +772,7 @@
 
     @pl.when(project)
     def _():
-        acc[...] = dot(normed[layer], w_ref[...])
+        acc[...] = dot(normed[layer, :, :], w_ref[...])
 
         def heads(low_ref, root_ref, gain, factor):
             @halves()
@@ -769,7 +788,7 @@
 
         @pl.when(tile == 2)
         def _():
-            v[layer] = acc[...].astype(BF16)
+            v[layer, :, :] = acc[...].astype(BF16)
             low = low_lanes()
             augq, augk = augq_ref[...], augk_ref[...]
             ones = jnp.ones((SLOTS, 128), BF16)
@@ -783,7 +802,7 @@
                     scores = dot(jnp.where(mine, qp, augq), jnp.where(mine, kp, augk), ACROSS)
                     results.append(dot(jnp.exp2(scores).astype(BF16), jnp.where(mine, vp, ones)))
                 inverse = 1.0 / pltpu.roll(jnp.where(low, results[1], results[0]), HD, 1)
-                linv[layer, :, part] = inverse
+                linv[layer, :, part] = inverse.astype(BF16)
                 combined[layer, 0, :, part] = (jnp.where(low, results[0], results[1]) * inverse).astype(BF16)
             loop(PAIRS, pair)
 
@@ -810,20 +829,21 @@
             else:
                 section_out[layer] = result
 
-    @pl.when(output_both & (tile == 0))
-    def _():
-        dy[...] = cot_ref[...]
-
     @pl.when(output_both | back)
     def _():
         acc[...] = dot(dy[...], w_ref[...], ACROSS)
-        terms_out_ref[...] = dot(combined[layer, tile], dy[...], DOWN).astype(BF16)
+        made = jnp.where(t < LAST_OUT, t - SECOND_OUT, TILES_OUT + t - LAST_OUT)
+        pl.when(made >= 2)(lambda: terms_copy(terms_out, terms_tile, terms_sem, made % 2, 0, 0).wait())
+        terms_tile[made % 2] = dot(combined[layer, tile], dy[...], DOWN).astype(BF16)
+        terms_copy(terms_out, terms_tile, terms_sem, made % 2, layer, tile).start()
+        if not trading:
+            pl.when(t == LAST_BACK - 1)(lambda: terms_settled(terms_out, terms_tile, terms_sem))
 
         @pl.when(tile == 0)
         def _():
             @halves()
             def _(rows, columns):
-                grad, inverse = acc[rows, columns], linv[layer, rows, columns]
+                grad, inverse = acc[rows, columns], linv[layer, rows, columns].astype(F32)
                 do[rows, columns] = (grad * inverse).astype(BF16)
                 total = head_means(grad * combined[layer, 0, rows, columns].astype(F32), spread) * (inverse * -HD)
                 for half in (0, 128):
@@ -838,7 +858,7 @@
             def _(rows, columns):
                 dproj[tile + 2, rows, columns] = (acc[rows, columns] * slope[layer, tile - 1, rows, columns].astype(F32)).astype(BF16)
 
-    @pl.when(project_back & (tile == 0))
+    @pl.when(heads_now)
     def _():
         low = low_lanes()
         spot = lax.broadcasted_iota(jnp.int32, (SLOTS, 128), 1) % HD
@@ -863,7 +883,12 @@
             dq[:, part] = sums[0] * 0.125
             dk[:, part] = sums[1] * (1.0 / LOG2E)
             dproj[2, :, part] = sums[2].astype(BF16)
-        loop(PAIRS, pair)
+        late = t >= LAST_HEADS
+        first_pair = jnp.where(late, t - LAST_HEADS, 0)
+        loop(jnp.where(late, 1, PAIRS), lambda index: pair(first_pair + index))
+
+    @pl.when(project_back & (tile == 0))
+    def _():
         for which, grads, low_ref, root_ref, gain, factor in ((0, dq, q, rq, qg_ref, SCALE), (1, dk, k, rk, kg_ref, 1.0)):
             @halves()
             def _(rows, columns):
@@ -880,7 +905,7 @@
         product = dot(dproj[tile], w_ref[...], ACROSS)
         pl.when(tile == up_first(0))(lambda: acc.__setitem__(..., product))
         pl.when(tile != up_first(0))(lambda: acc.__setitem__(..., acc[...] + product))
-        terms_in_ref[...] = dot(normed[layer], dproj[tile], DOWN).astype(BF16)
+        terms_in_ref[...] = dot(normed[layer, :, :], dproj[tile], DOWN).astype(BF16)
 
         @pl.when(tile == LAST_TILE)
         def _():
@@ -907,6 +932,58 @@
                 pl.when(layer == 0)(trade.finish)
 
 
+class Saved:
+    def __init__(self, ref, which):
+        self.ref, self.which = ref, which
+
+    def __getitem__(self, index):
+        return self.ref[(index[0], self.which) + index[1:]]
+
+    def __setitem__(self, index, value):
+        self.ref[(index[0], self.which) + index[1:]] = value
+
+
+def terms_copy(terms_out, terms_tile, terms_sem, slot, layer, tile):
+    target = terms_out.at[layer, pl.ds(pl.multiple_of(tile * D, D), D), :]
+    return pltpu.make_async_copy(terms_tile.at[slot], target, terms_sem.at[slot])
+
+
+def terms_settled(terms_out, terms_tile, terms_sem):
+    for slot in range(2):
+        terms_copy(terms_out, terms_tile, terms_sem, slot, 0, 0).wait()
+
+
+def outer_scatter(t, terms_out, terms_tile, terms_sem, own_out, combined, slope, saved, rest_land, ready_sem, *sems):
+    place = Place()
+    rows = BLOCK[1][0]
+
+    def half(number):
+        return pl.ds(pl.multiple_of((number % 2) * rows, 16), rows)
+
+    def held(number):
+        return combined.at[number // 10, (number // 2) % 5, half(number)]
+
+    def core_land(number):
+        return slope.at[number // 8, (number // 2) % 4, half(number)]
+
+    def land(colour, slot):
+        piece = colour * 20 + slot
+        return saved.at[1, piece // 5, pl.ds(pl.multiple_of((piece % 5) * 96, 16), 96)]
+
+    scatter = Scatter(place, 1, terms_out, held, core_land, land, lambda slot: rest_land.at[slot], sems[:7])
+
+    @pl.when(t == LAST_BACK)
+    def _():
+        terms_settled(terms_out, terms_tile, terms_sem)
+        greet(place, ready_sem)
+        scatter.begin()
+
+    turn = t - LAST_BACK
+    count = jnp.where(turn == 0, 2, jnp.where(t == STEPS - 1, Scatter.MICRO - 13, 1))
+    loop(count, lambda index: scatter.micro(jnp.where(turn == 0, 0, turn + 1) + index))
+    pl.when(t == STEPS - 1)(lambda: scatter.finish(own_out, sems[7]))
+
+
 class Trade:
     def __init__(self, section, section_out, hidden, dy, grad_land, own_sem, send_sem, recv_sem):
         self.section, self.section_out, self.hidden, self.dy, self.grad_land = section, section_out, hidden, dy, grad_land
@@ -942,7 +1019,7 @@
         pl.when(self.section == 1)(lambda: self.grad().wait_recv())
 
 
-def both_layers(trading, counts, weights, gains, h, cot, augq, augk, spread):
+def both_layers(trading, counts, weights, gains, inputs, cotangent, augq, augk, spread):
     square = (SLOTS, D)
 
     def whole(*dims):
@@ -953,9 +1030,11 @@
     full = [jax.ShapeDtypeStruct(dims, BF16) for dims in ((2, D, TILES_IN * D), (2, TILES_OUT * D, D))]
     if trading:
         in_specs, operands = [any_space] * 3, (*weights, gains)
-        out_specs, more_specs = [any_space, whole(*square), whole(*square), any_space], [any_space] * 2
+        out_specs, more_specs = [any_space, whole(*square), whole(*square), any_space], [any_space] * 3
         sems = [dma((5, 3, 16)), dma((3, 16)), dma((3, 16))] * 3 + [dma((3,))]
-        grad_shape, extra, more = square, sems + [dma(()), dma((2,)), dma((2,)), low(2, 16 * BLOCK[2][0], 128)], full
+        extra = [low(2, 16 * BLOCK[2][0], 128)] + sems + [dma(()), dma((2,)), dma((2,))]
+        extra += [low(35, *part_shape(SCATTER_CUTS, 1, None)), pltpu.SemaphoreType.REGULAR] + scatter_sems()
+        grad_shape, more = square, full + [jax.ShapeDtypeStruct(BLOCK[1], BF16)]
         params = dict(collective_id=2, has_side_effects=True)
     else:
         in_specs, operands = [any_space] * 2 + [whole(*gains.shape)], (*weights, gains)
@@ -964,24 +1043,22 @@
     return pl.pallas_call(
         functools.partial(compute_kernel, trading, counts),
         grid=(STEPS,),
-        in_specs=in_specs + [whole(*square), whole(*square), whole(SLOTS, 128), whole(SLOTS, 128), whole(256, 256)],
+        in_specs=in_specs + [any_space, any_space, whole(SLOTS, 128), whole(SLOTS, 128), whole(256, 256)],
         out_specs=out_specs + [
-            whole(2, 8, D), pl.BlockSpec((None, D, D), lambda t: (in_terms(t)[0], 0, in_terms(t)[1])),
-            pl.BlockSpec((None, D, D), lambda t: (out_terms(t)[0], out_terms(t)[1], 0)),
+            whole(2, 8, D), pl.BlockSpec((None, D, D), lambda t: (in_terms(t)[0], 0, in_terms(t)[1])), any_space,
         ] + more_specs,
-        scratch_shapes=extra + [
+        scratch_shapes=[
             low(2, D, D), dma((2,)), wide(2, 1, D), wide(2, 1, 256), wide(2, 1, 256),
-            low(3, *square), low(2, *square), wide(2, SLOTS, 128), low(2, *square), low(2, *square), low(2, *square), low(2, *square),
-            low(2, *square), wide(2, *square), low(2, 4, *square), low(2, 5, *square), low(*square), low(7, *square), wide(*square),
-            wide(*square), wide(*square), low(*square), low(*square), low(*square),
-        ],
+            low(3, *square), low(2, 8, *square), wide(2, SLOTS, 128), low(2, 4, *square), low(2, 5, *square), low(*square), low(7, *square),
+            wide(*square), wide(*square), wide(*square), low(*square), low(*square), low(*square), low(2, D, D), dma((2,)), dma((2,)),
+        ] + extra,
         out_shape=[
             jax.ShapeDtypeStruct((2,) + square, BF16), jax.ShapeDtypeStruct(grad_shape, F32), jax.ShapeDtypeStruct(square, BF16),
             jax.ShapeDtypeStruct(square, BF16), jax.ShapeDtypeStruct((2, 8, D), F32), *full,
         ] + more,
         compiler_params=pltpu.CompilerParams(vmem_limit_bytes=63 * 2**20, **params),
         name="both_layers",
-    )(*operands, h, cot, augq, augk, spread)[:7]
+    )(*operands, inputs, cotangent, augq, augk, spread)
 
 
 def augment(image_id, token_size):
@@ -1021,9 +1098,9 @@
         weights = (gather_all(w_in, 1), gather_all(w_out, 1))
         gains = gather_all(gains[None], 1)
     augq, augk = augment(image_id[section, 0], token_size[section, 0])
-    outs, grads, grad_low, grad_land, gain_terms, terms_in, terms_out = both_layers(
-        blocks_fit, tuple(gain.shape[1] for gain in (ln_gain, q_gain, k_gain)), weights, gains, inputs[section, 0],
-        cotangent[section, 0], augq, augk, spread_matrix())
+    outs, grads, grad_low, grad_land, gain_terms, terms_in, terms_out, *more = both_layers(
+        blocks_fit, tuple(gain.shape[1] for gain in (ln_gain, q_gain, k_gain)), weights, gains, inputs,
+        cotangent, augq, augk, spread_matrix())
     swap = [(0, 1), (1, 0)]
 
     def both_micro(pair):
@@ -1037,11 +1114,11 @@
     places = (0, D, D + HD, D + 2 * HD)
     if blocks_fit:
         totals = jnp.pad(totals, ((0, 0), (0, 1024 - places[3]))).reshape(BLOCK[2])
-        own_in, own_out, totals, last_land = scatter_terms(terms_in, terms_out, totals, grad_low)
+        own_in, totals, last_land = scatter_terms(terms_in, totals, grad_low)
         other = jnp.where(section == 0, last_land, grad_land).astype(F32)
         grads = jnp.where(section == 0, jnp.stack([grads, other]), jnp.stack([other, grads]))[None, :, None]
         outs = outs[None, :, None]
-        own_in, own_out = own_in[None], own_out[None]
+        own_in, own_out = own_in[None].astype(F32), more[2][None].astype(F32)
         totals = totals.reshape(2, 1024)
     else:
         own_in = scatter_all(terms_in, 1).astype(F32)

time: 440 us -> 418 us (0.950)
  Pallas kernels: 420 us -> 396 us
  local copies, waits for them, and re-layouts: 12.5 us -> 7.76 us
    pallas_call x1, Pallas kernels: 163 us -> 90.5 us  [scatter_terms(): pl.pallas_call(scatter_kernel, out_shape=(jax.ShapeDtypeStruct(BLOCK[0],...]
    pallas_call x1, Pallas kernels: 257 us -> 306 us  [both_layers(): pl.pallas_call(functools.partial(compute_kernel, trading, counts), grid=(...]
where the time goes in v6:
time: 418 us; the launch traced here: 415 us
  Pallas kernels  396 us (95%)
  other arithmetic  9.84 us (2%)
  local copies, waits for them, and re-layouts  7.76 us (2%)
    pallas_call x1, Pallas kernels, both_layers(): pl.pallas_call(functools.partial(compute_kernel, trading, counts), grid=(...  306 us
    pallas_call x1, Pallas kernels, scatter_terms(): pl.pallas_call(scatter_kernel, out_shape=(jax.ShapeDtypeStruct(BLOCK[0],...  90.5 us

profile of v6, /device:TPU:8, one launch (start us, length us, event | category | flops | bytes accessed | tf_op | source)
XLA Modules:
  0.0 414.6 jit_solution(15440139336702217987)
XLA Ops:
  0.6 0.0 copy-start
  0.7 0.7 copy-done
  1.3 0.7 bitcast_convert_fusion.3
  2.0 0.7 fusion.11
  2.7 0.1 pad.28.clone
  2.8 0.1 maximum_maximum_fusion.1
  2.9 0.8 copy.18.refs_6_
  3.7 0.1 pad.31.clone
  3.8 0.1 maximum_maximum_fusion
  3.9 0.8 copy.17.refs_5_
  4.6 0.8 select_convert_fusion.refs_7_
  5.4 1.4 fusion.10.refs_2_
  6.8 305.8 %both_layers.1 = (bf16[2,512,768]{2,1,0:T(8,128)(2,1)}, f32[512,768]{1,0:T(8,128)}, bf16[512,768]{1,0:T(8,128)(2,1)}, bf16[512,768]{1,0:T(8,128)(2,1)}, f32[2,8,...) custom-call(bf16[48,5376]{1,0:T(8,128)(2,1)} %bitcast.34, ...), custom_call_target="tpu_custom_call" | custom-call | tf_op jit(solution)/shard_map/both_layers/pallas_call | solution.py:1043
  312.6 0.8 slice.19
  313.4 0.1 reshape.170
  313.5 0.1 reshape.171
  313.6 0.8 slice.18
  314.4 0.0 copy-start.2
  314.4 1.1 copy-done.2
  315.5 0.0 copy-start.4
  315.5 90.5 %scatter_terms.1 = (bf16[48,5376]{1,0:T(8,128)(2,1)S(1)}, f32[16,128]{1,0:T(8,128)S(1)}, bf16[512,768]{1,0:T(8,128)(2,1)S(1)}) custom-call(bf16[2,768,5376]{2,1,0:T(8,128)(2,1)} %get-tuple-element.19.terms, f32[16,128]{1,0:T(8,128)S(1)} %reshape.172.gains, bf16[512,768]{1,0:T(8,128)(2,1)S(1)} %copy-done.2), custom_call_target="tpu_custom_call" | custom-call | tf_op jit(solution)/shard_map/scatter_terms/pallas_call | solution.py:594
  406.0 0.1 fusion.12
  406.1 0.6 constant_dynamic-slice_fusion
  406.7 0.0 copy-done.4
  406.7 0.1 bitcast_convert_fusion
  406.8 0.0 copy-start.5
  406.8 0.0 copy-start.3
  406.8 0.0 copy-start.1
  406.8 4.1 maximum_select_fusion
  410.9 1.0 bitcast_convert_fusion.1
  412.0 0.6 dynamic-slice.4
  412.5 0.0 copy-done.5
  412.5 0.9 bitcast_convert_fusion.2
  413.5 0.0 copy-done.3
  413.5 1.1 copy.24
  414.6 0.0 copy-done.1
  (15 shorter events, 0.1 us)
Async XLA Ops:
  0.6 0.7 copy-start
  314.4 1.1 copy-start.2
  315.5 91.2 %copy-start.4 = (bf16[512,768]{1,0:T(8,128)(2,1)S(1)}, bf16[512,768]{1,0:T(8,128)(2,1)}, u32[]{:S(2)}) copy-start(bf16[512,768]{1,0:T(8,128)(2,1)} %get-tuple-element.23) | copy-start | bytes 2359300
  406.8 5.7 %copy-start.5 = (bf16[240,768]{1,0:T(8,128)(2,1)S(1)}, bf16[240,768]{1,0:T(8,128)(2,1)}, u32[]{:S(2)}) copy-start(bf16[240,768]{1,0:T(8,128)(2,1)} %get-tuple-element.25) | copy-start | bytes 1105924
  406.8 6.6 %copy-start.3 = (bf16[2,512,768]{2,1,0:T(8,128)(2,1)S(1)}, bf16[2,512,768]{2,1,0:T(8,128)(2,1)}, u32[]{:S(2)}) copy-start(bf16[2,512,768]{2,1,0:T(8,128)(2,1)} %get-tuple-element.17) | copy-start | bytes 4718596
  406.8 7.8 %copy-start.1 = (s32[2,1,512]{2,1,0:T(1,128)S(1)}, s32[2,1,512]{2,1,0:T(1,128)}, u32[]{:S(2)}) copy-start(s32[2,1,512]{2,1,0:T(1,128)} %param.12) | copy-start | bytes 12292

commit v7 on v6

--- a/solution.py
+++ b/solution.py
@@ -11,7 +11,7 @@
 NZ = 4
 BLOCK = ((48, 5376), (240, 768), (16, 128))
 GATHER_CUTS = (2176, 96)
-SCATTER_CUTS = (2176, 96)
+SCATTER_CUTS = (2048, 96)
 
 
 class Place:
@@ -316,12 +316,18 @@
 
 
 def add_into(target, source):
-    rows = target.shape[0]
-
     def body(step):
-        part = pl.ds(pl.multiple_of(step * 16, 16), 16)
-        target[part, :] = (target[part, :].astype(jnp.float32) + source[part, :].astype(jnp.float32)).astype(jnp.bfloat16)
-    loop(rows // 16, body)
+        part = pl.ds(pl.multiple_of(step * 48, 16), 48)
+        target[part, :] = target[part, :] + source[part, :]
+    loop(target.shape[0] // 48, body)
+
+
+OUTER_ORDER = (
+    ("k3", "l3"), (), ("a3", "k2"), (), ("l2",), ("b3", "k1"), ("a2", "z3"), (), ("l1",), (), ("k0", "b2"), ("z2", "a1", "l0"), (),
+    ("a0", "b1", "z1", "s", "b0", "z0"))
+INNER_ORDER = (
+    "k3", "k2", "l3", "k1", "l2", "a3", "k0", "l1", "b3", "a2", "z3", "a1", "l0", "b2", "z2", "b1", "a0", "z1", "s", "b0", "z0")
+INNER_GRAD = 14
 
 
 class Scatter:
@@ -477,26 +483,24 @@
         self.square(True)
 
 
-    MICRO = 19
+    STEPS = "klabzs"
 
     def begin(self):
         loop(NZ, lambda index: self.start(NZ - 1 - index))
 
-    def micro(self, index):
-        distance = NZ - 1 - index // 4
-        turn = jnp.where(index < 16, index % 4, index - 12)
-        pl.when(turn == 0)(lambda: self.k_step(distance))
-        pl.when(turn == 1)(lambda: self.line(distance))
-
-        @pl.when((turn == 2) | (turn == 5))
-        def _():
-            self.b_step(jnp.where(turn == 2, distance + 1, 0))
-
-        @pl.when((turn == 2) | (turn == 6))
-        def _():
-            self.z_step(jnp.where(turn == 2, distance + 1, 0))
-        pl.when(turn == 3)(lambda: self.a_step(distance))
-        pl.when(turn == 4)(self.square)
+    def run(self, order, first, count, also=None):
+        codes = [(self.STEPS.index(step[0]), int(step[1:] or 0)) for step in order]
+
+        def body(index):
+            index = first + index
+            which, distance = [sum((index == place).astype(jnp.int32) * code[part] for place, code in enumerate(codes)) for part in (0, 1)]
+            calls = (self.k_step, self.line, self.a_step, self.b_step, self.z_step)
+            for code, call in enumerate(calls):
+                pl.when(which == code)(lambda: call(distance))
+            pl.when(which == len(calls))(self.square)
+            if also:
+                also(index)
+        loop(count, body)
 
     def finish(self, result, sem):
         copy = pltpu.make_async_copy(self.held(number_of((self.place.x, self.place.y, self.place.z))), result, sem)
@@ -577,11 +581,10 @@
                       lambda colour, slot: land.at[colour * 20 + slot], lambda slot: rest_land.at[slot], sems[:7])
     scatter.begin()
 
-    def body(index):
-        scatter.micro(index)
+    def also(index):
         pl.when(index % 4 == 0)(lambda: total.step(index // 4))
-        pl.when((index == 15) & (place.x == 1))(lambda: grad_copy.start())
-    loop(Scatter.MICRO, body)
+        pl.when((index == INNER_GRAD) & (place.x == 1))(lambda: grad_copy.start())
+    scatter.run(INNER_ORDER, 0, len(INNER_ORDER), also)
     scatter.finish(result, sems[7])
     total.drain()
     pl.when(place.x == 1)(lambda: grad_copy.wait_send())
@@ -704,10 +707,10 @@
         own, refs = refs[:3], refs[3:]
     else:
         (full_in, full_out, full_gains), refs, own = refs[:3], refs[3:], None
-    (inputs, cotangent, augq_ref, augk_ref, spread_ref, section_out, grad_ref, grad_low, grad_land, gain_ref, terms_in_ref, terms_out), refs = (
+    (inputs, cotangent, augq_ref, augk_ref, spread_ref, section_out, grad_ref, grad_low, grad_land, totals_ref, terms_in_ref, terms_out), refs = (
         refs[:12], refs[12:])
     (tiles, tile_sem, ln_ref, qg_ref, kg_ref, hidden, saved, scale, slope, combined, dy, dproj, acc, dq, dk, do, dhigh, dlow, terms_tile,
-     terms_sem, entry_sem), refs = (refs[:21], refs[21:]) if not trading else (refs[3:24], refs[:3] + refs[24:])
+     terms_sem, entry_sem, gain_ref), refs = (refs[:22], refs[22:]) if not trading else (refs[3:25], refs[:3] + refs[25:])
     sems, swap, scatter_refs = None, (), None
     if trading:
         (full_in, full_out, own_out, full_gains), sems, swap, scatter_refs = refs[:4], refs[4:14], refs[14:17], refs[17:]
@@ -729,8 +732,6 @@
     weights = Weights(Place() if trading else None, own, (full_in, full_out, full_gains), tiles, tile_sem, sems)
     weights.step(t)
     w_ref = tiles.at[tile_slot(t)]
-    if trading:
-        pl.when(t >= LAST_BACK)(lambda: outer_scatter(t, terms_out, terms_tile, terms_sem, own_out, combined, slope, saved, *scatter_refs))
 
     def halves(width=256):
         def run(body):
@@ -759,6 +760,17 @@
 
     def low_lanes():
         return lax.broadcasted_iota(jnp.int32, (SLOTS, 128), 1) < HD
+
+    def fold_gains():
+        for which in range(2):
+            parts = [[gain_ref[which, row : row + 1, 128 * part : 128 * (part + 1)] for part in range(PAIRS)] for row in range(3)]
+            sums = [functools.reduce(jnp.add, row) for row in parts[1:]]
+            sums = [total + pltpu.roll(total, HD, 1) for total in sums]
+            for part in range(PAIRS):
+                totals_ref[8 * which + part : 8 * which + part + 1, :] = parts[0][part]
+            first = lax.broadcasted_iota(jnp.int32, (1, 128), 1) < HD
+            totals_ref[8 * which + 6 : 8 * which + 7, :] = jnp.where(first, *sums)
+            totals_ref[8 * which + 7 : 8 * which + 8, :] = jnp.zeros((1, 128), F32)
 
     @pl.when(project & (tile == 0))
     def _():
@@ -930,6 +942,11 @@
             if trade:
                 pl.when(layer == 1)(trade.give_grad)
                 pl.when(layer == 0)(trade.finish)
+            pl.when(layer == 0)(fold_gains)
+
+    if trading:
+        pl.when(t >= LAST_BACK - 1)(
+            lambda: outer_scatter(t, terms_out, terms_tile, terms_sem, own_out, combined, slope, saved, *scatter_refs))
 
 
 class Saved:
@@ -972,15 +989,18 @@
 
     scatter = Scatter(place, 1, terms_out, held, core_land, land, lambda slot: rest_land.at[slot], sems[:7])
 
-    @pl.when(t == LAST_BACK)
+    @pl.when(t == LAST_BACK - 1)
     def _():
         terms_settled(terms_out, terms_tile, terms_sem)
         greet(place, ready_sem)
         scatter.begin()
 
-    turn = t - LAST_BACK
-    count = jnp.where(turn == 0, 2, jnp.where(t == STEPS - 1, Scatter.MICRO - 13, 1))
-    loop(count, lambda index: scatter.micro(jnp.where(turn == 0, 0, turn + 1) + index))
+    first, count = 0, 0
+    for slot, steps in enumerate(OUTER_ORDER):
+        here = (t == LAST_BACK - 1 + slot).astype(jnp.int32)
+        first += here * sum(map(len, OUTER_ORDER[:slot]))
+        count += here * len(steps)
+    scatter.run([step for steps in OUTER_ORDER for step in steps], first, count)
     pl.when(t == STEPS - 1)(lambda: scatter.finish(own_out, sems[7]))
 
 
@@ -1045,16 +1065,17 @@
         grid=(STEPS,),
         in_specs=in_specs + [any_space, any_space, whole(SLOTS, 128), whole(SLOTS, 128), whole(256, 256)],
         out_specs=out_specs + [
-            whole(2, 8, D), pl.BlockSpec((None, D, D), lambda t: (in_terms(t)[0], 0, in_terms(t)[1])), any_space,
+            whole(16, 128), pl.BlockSpec((None, D, D), lambda t: (in_terms(t)[0], 0, in_terms(t)[1])), any_space,
         ] + more_specs,
         scratch_shapes=[
             low(2, D, D), dma((2,)), wide(2, 1, D), wide(2, 1, 256), wide(2, 1, 256),
             low(3, *square), low(2, 8, *square), wide(2, SLOTS, 128), low(2, 4, *square), low(2, 5, *square), low(*square), low(7, *square),
             wide(*square), wide(*square), wide(*square), low(*square), low(*square), low(*square), low(2, D, D), dma((2,)), dma((2,)),
+            wide(2, 8, D),
         ] + extra,
         out_shape=[
             jax.ShapeDtypeStruct((2,) + square, BF16), jax.ShapeDtypeStruct(grad_shape, F32), jax.ShapeDtypeStruct(square, BF16),
-            jax.ShapeDtypeStruct(square, BF16), jax.ShapeDtypeStruct((2, 8, D), F32), *full,
+            jax.ShapeDtypeStruct(square, BF16), jax.ShapeDtypeStruct((16, 128), F32), *full,
         ] + more,
         compiler_params=pltpu.CompilerParams(vmem_limit_bytes=63 * 2**20, **params),
         name="both_layers",
@@ -1098,7 +1119,7 @@
         weights = (gather_all(w_in, 1), gather_all(w_out, 1))
         gains = gather_all(gains[None], 1)
     augq, augk = augment(image_id[section, 0], token_size[section, 0])
-    outs, grads, grad_low, grad_land, gain_terms, terms_in, terms_out, *more = both_layers(
+    outs, grads, grad_low, grad_land, totals, terms_in, terms_out, *more = both_layers(
         blocks_fit, tuple(gain.shape[1] for gain in (ln_gain, q_gain, k_gain)), weights, gains, inputs,
         cotangent, augq, augk, spread_matrix())
     swap = [(0, 1), (1, 0)]
@@ -1109,23 +1130,20 @@
         other = lax.ppermute(other, "section", swap).astype(mine.dtype)
         return jnp.where(section == 0, jnp.stack([mine, other]), jnp.stack([other, mine]))[None, :, None]
 
-    heads = gain_terms[:, 1:3].reshape(2, 2, -1, HD).sum(2).reshape(2, -1)
-    totals = jnp.concatenate([gain_terms[:, 0], heads], 1)
     places = (0, D, D + HD, D + 2 * HD)
     if blocks_fit:
-        totals = jnp.pad(totals, ((0, 0), (0, 1024 - places[3]))).reshape(BLOCK[2])
         own_in, totals, last_land = scatter_terms(terms_in, totals, grad_low)
         other = jnp.where(section == 0, last_land, grad_land).astype(F32)
-        grads = jnp.where(section == 0, jnp.stack([grads, other]), jnp.stack([other, grads]))[None, :, None]
+        is_own = (jnp.arange(2) == section)[:, None, None]
+        grads = jnp.where(is_own, grads[None], other[None])[None, :, None]
         outs = outs[None, :, None]
         own_in, own_out = own_in[None].astype(F32), more[2][None].astype(F32)
-        totals = totals.reshape(2, 1024)
     else:
         own_in = scatter_all(terms_in, 1).astype(F32)
         own_out = scatter_all(terms_out, 1).astype(F32)
         totals = lax.psum(totals, ("section", "wide"))
         outs, grads = both_micro(outs), both_micro(grads)
-    mine = lax.dynamic_index_in_dim(totals, section, 0, False)
+    mine = lax.dynamic_index_in_dim(totals.reshape(2, 1024), section, 0, False)
     gain_grads = [
         lax.dynamic_slice_in_dim(mine[low:high], wide * gain.shape[1], gain.shape[1])[None]
         for low, high, gain in zip(places, places[1:], (ln_gain, q_gain, k_gain))

time: 418 us -> 410 us (0.981)
  Pallas kernels: 396 us -> 390 us
    pallas_call x1, Pallas kernels: 306 us -> 301 us  [both_layers(): pl.pallas_call(functools.partial(compute_kernel, trading, counts), grid=(...]
where the time goes in v7:
time: 410 us; the launch traced here: 406 us
  Pallas kernels  390 us (95%)
  local copies, waits for them, and re-layouts  7.94 us (2%)
  other arithmetic  7.67 us (2%)
    pallas_call x1, Pallas kernels, both_layers(): pl.pallas_call(functools.partial(compute_kernel, trading, counts), grid=(...  301 us
    pallas_call x1, Pallas kernels, scatter_terms(): pl.pallas_call(scatter_kernel, out_shape=(jax.ShapeDtypeStruct(BLOCK[0],...  89.3 us

profile of v7, /device:TPU:8, one launch (start us, length us, event | category | flops | bytes accessed | tf_op | source)
XLA Modules:
  0.0 406.2 jit_solution(2497032891751038763)
XLA Ops:
  0.6 0.0 copy-start
  0.7 0.7 copy-done
  1.3 0.7 bitcast_convert_fusion.2
  2.0 0.7 fusion.11
  2.7 0.1 pad.17.clone
  2.8 0.1 maximum_maximum_fusion.1
  2.9 0.8 copy.18.refs_6_
  3.7 0.1 pad.20.clone
  3.8 0.1 maximum_maximum_fusion
  3.9 0.8 copy.17.refs_5_
  4.6 0.8 select_convert_fusion.1.refs_7_
  5.4 1.4 fusion.10.refs_2_
  6.8 300.6 %both_layers.1 = (bf16[2,512,768]{2,1,0:T(8,128)(2,1)}, f32[512,768]{1,0:T(8,128)}, bf16[512,768]{1,0:T(8,128)(2,1)}, bf16[512,768]{1,0:T(8,128)(2,1)}, f32[16,1...) custom-call(bf16[48,5376]{1,0:T(8,128)(2,1)} %bitcast.26, ...), custom_call_target="tpu_custom_call" | custom-call | tf_op jit(solution)/shard_map/both_layers/pallas_call | solution.py:1063
  307.3 0.0 copy-start.2
  307.3 1.1 copy-done.2
  308.5 0.0 copy-start.3
  308.5 0.7 copy-done.3
  309.2 0.0 copy-start.6
  309.2 89.3 %scatter_terms.1 = (bf16[48,5376]{1,0:T(8,128)(2,1)S(1)}, f32[16,128]{1,0:T(8,128)S(1)}, bf16[512,768]{1,0:T(8,128)(2,1)S(1)}) custom-call(bf16[2,768,5376]{2,1,0:T(8,128)(2,1)} %get-tuple-element.19.terms, f32[16,128]{1,0:T(8,128)S(1)} %copy-done.3, bf16[512,768]{1,0:T(8,128)(2,1)S(1)} %copy-done.2), custom_call_target="tpu_custom_call" | custom-call | tf_op jit(solution)/shard_map/scatter_terms/pallas_call | solution.py:597
  398.5 0.1 fusion.12
  398.6 0.6 constant_dynamic-slice_fusion
  399.2 0.0 copy-done.6
  399.2 0.0 copy-start.5
  399.2 0.1 select_convert_fusion
  399.3 1.3 copy-done.5
  400.6 0.0 copy-start.7
  400.6 1.9 broadcast_select_fusion
  402.5 0.0 copy-start.4
  402.5 1.0 bitcast_convert_fusion
  403.5 0.6 dynamic-slice.4
  404.1 0.0 copy-done.7
  404.1 0.0 copy-start.1
  404.1 0.9 bitcast_convert_fusion.1
  405.0 0.0 copy-done.4
  405.0 1.1 copy.21
  406.2 0.0 copy-done.1
  (12 shorter events, 0.1 us)
Async XLA Ops:
  0.6 0.7 copy-start
  307.3 1.1 copy-start.2
  308.5 0.7 copy-start.3
  309.2 90.0 %copy-start.6 = (bf16[512,768]{1,0:T(8,128)(2,1)S(1)}, bf16[512,768]{1,0:T(8,128)(2,1)}, u32[]{:S(2)}) copy-start(bf16[512,768]{1,0:T(8,128)(2,1)} %get-tuple-element.23) | copy-start | bytes 2359300
  399.2 1.4 copy-start.5
  400.6 3.6 copy-start.7
  402.5 2.5 copy-start.4
  404.1 2.1 copy-start.1

commit v8 on v7

--- a/solution.py
+++ b/solution.py
@@ -323,7 +323,7 @@
 
 
 OUTER_ORDER = (
-    ("k3", "l3"), (), ("a3", "k2"), (), ("l2",), ("b3", "k1"), ("a2", "z3"), (), ("l1",), (), ("k0", "b2"), ("z2", "a1", "l0"), (),
+    ("k3", "l3"), (), ("a3", "k2"), (), ("l2",), ("b3", "k1", "a2", "z3"), ("l1",), ("k0", "b2"), ("z2", "a1", "l0"), (),
     ("a0", "b1", "z1", "s", "b0", "z0"))
 INNER_ORDER = (
     "k3", "k2", "l3", "k1", "l2", "a3", "k0", "l1", "b3", "a2", "z3", "a1", "l0", "b2", "z2", "b1", "a0", "z1", "s", "b0", "z0")
@@ -643,10 +643,10 @@
 
 
 def lanes(index, width):
-    return pl.ds(pl.multiple_of(index * width, width), width)
-
-
-FIRST_OUT, SECOND_IN, SECOND_OUT, SECOND_BACK, LAST_OUT, LAST_BACK, LAST_HEADS, LAST_PROJECT, STEPS = 7, 12, 19, 24, 31, 36, 40, 46, 49
+    return pl.ds(index * width if isinstance(index, int) else pl.multiple_of(index * width, width), width)
+
+
+FIRST_OUT, SECOND_IN, SECOND_OUT, SECOND_BACK, LAST_OUT, LAST_BACK, LAST_HEADS, LAST_PROJECT, STEPS = 7, 12, 19, 24, 31, 36, 40, 43, 46
 LAST_TILE = 2
 
 
@@ -733,12 +733,9 @@
     weights.step(t)
     w_ref = tiles.at[tile_slot(t)]
 
-    def halves(width=256):
-        def run(body):
-            def step(index):
-                body(pl.ds(pl.multiple_of((index % 2) * 256, 256), 256), lanes(index // 2, width))
-            loop(2 * D // width, step)
-        return run
+    def thirds(body):
+        for part in range(WIDE_PAIRS):
+            body(pl.ds(256 * part, 256))
 
     def by_rows(body):
         loop(SLOTS // 128, lambda index: body(pl.ds(pl.multiple_of(index * 128, 128), 128)))
@@ -784,23 +781,24 @@
 
     @pl.when(project)
     def _():
-        acc[...] = dot(normed[layer, :, :], w_ref[...])
+        def projected(columns):
+            return dot(normed[layer, :, :], w_ref[:, columns])
 
         def heads(low_ref, root_ref, gain, factor):
-            @halves()
-            def _(rows, columns):
-                x = acc[rows, columns]
+            @thirds
+            def _(columns):
+                x = projected(columns)
                 centred = x - head_means(x, spread)
                 root = lax.rsqrt(head_means(centred * centred, spread, False) + EPSILON)
-                root_ref[layer, rows, columns] = root.astype(BF16)
-                low_ref[layer, rows, columns] = (centred * root * (gain * factor)).astype(BF16)
+                root_ref[layer, :, columns] = root.astype(BF16)
+                low_ref[layer, :, columns] = (centred * root * (gain * factor)).astype(BF16)
 
         pl.when(tile == 0)(lambda: heads(q, rq, qg_ref[layer], SCALE))
         pl.when(tile == 1)(lambda: heads(k, rk, kg_ref[layer], 1.0))
 
         @pl.when(tile == 2)
         def _():
-            v[layer, :, :] = acc[...].astype(BF16)
+            v[layer, :, :] = projected(slice(None)).astype(BF16)
             low = low_lanes()
             augq, augk = augq_ref[...], augk_ref[...]
             ones = jnp.ones((SLOTS, 128), BF16)
@@ -816,21 +814,20 @@
                 inverse = 1.0 / pltpu.roll(jnp.where(low, results[1], results[0]), HD, 1)
                 linv[layer, :, part] = inverse.astype(BF16)
                 combined[layer, 0, :, part] = (jnp.where(low, results[0], results[1]) * inverse).astype(BF16)
-            loop(PAIRS, pair)
+            for index in range(PAIRS):
+                pair(index)
 
         @pl.when(tile > 2)
         def _():
-            @halves()
-            def _(rows, columns):
-                value, rise = gelu_and_slope(acc[rows, columns])
-                slope[layer, tile - 3, rows, columns] = rise.astype(BF16)
-                combined[layer, tile - 2, rows, columns] = value.astype(BF16)
+            @thirds
+            def _(columns):
+                value, rise = gelu_and_slope(projected(columns))
+                slope[layer, tile - 3, :, columns] = rise.astype(BF16)
+                combined[layer, tile - 2, :, columns] = value.astype(BF16)
 
     @pl.when(output | output_both)
     def _():
-        product = dot(combined[layer, tile], w_ref[...])
-        pl.when(tile == 0)(lambda: dq.__setitem__(..., hidden[layer].astype(F32) + product))
-        pl.when(tile > 0)(lambda: dq.__setitem__(..., dq[...] + product))
+        dq[...] = jnp.where(tile == 0, hidden[layer].astype(F32), dq[...]) + dot(combined[layer, tile], w_ref[...])
 
         @pl.when(tile == TILES_OUT - 1)
         def _():
@@ -843,9 +840,12 @@
 
     @pl.when(output_both | back)
     def _():
-        acc[...] = dot(dy[...], w_ref[...], ACROSS)
         made = jnp.where(t < LAST_OUT, t - SECOND_OUT, TILES_OUT + t - LAST_OUT)
         pl.when(made >= 2)(lambda: terms_copy(terms_out, terms_tile, terms_sem, made % 2, 0, 0).wait())
+
+        def grads(columns):
+            return dot(dy[...], w_ref[columns, :], ACROSS)
+
         terms_tile[made % 2] = dot(combined[layer, tile], dy[...], DOWN).astype(BF16)
         terms_copy(terms_out, terms_tile, terms_sem, made % 2, layer, tile).start()
         if not trading:
@@ -853,22 +853,22 @@
 
         @pl.when(tile == 0)
         def _():
-            @halves()
-            def _(rows, columns):
-                grad, inverse = acc[rows, columns], linv[layer, rows, columns].astype(F32)
-                do[rows, columns] = (grad * inverse).astype(BF16)
-                total = head_means(grad * combined[layer, 0, rows, columns].astype(F32), spread) * (inverse * -HD)
+            @thirds
+            def _(columns):
+                grad, inverse = grads(columns), linv[layer, :, columns].astype(F32)
+                do[:, columns] = (grad * inverse).astype(BF16)
+                total = head_means(grad * combined[layer, 0, :, columns].astype(F32), spread) * (inverse * -HD)
                 for half in (0, 128):
-                    part = pl.ds(pl.multiple_of(columns.start + half, 128), 128)
+                    part = pl.ds(columns.start + half, 128)
                     high, low = split(pltpu.roll(total[:, half : half + 128], HD, 1))
-                    dhigh[rows, part] = high
-                    dlow[rows, part] = low
+                    dhigh[:, part] = high
+                    dlow[:, part] = low
 
         @pl.when(tile > 0)
         def _():
-            @halves()
-            def _(rows, columns):
-                dproj[tile + 2, rows, columns] = (acc[rows, columns] * slope[layer, tile - 1, rows, columns].astype(F32)).astype(BF16)
+            @thirds
+            def _(columns):
+                dproj[tile + 2, :, columns] = (grads(columns) * slope[layer, tile - 1, :, columns].astype(F32)).astype(BF16)
 
     @pl.when(heads_now)
     def _():
@@ -896,27 +896,29 @@
             dk[:, part] = sums[1] * (1.0 / LOG2E)
             dproj[2, :, part] = sums[2].astype(BF16)
         late = t >= LAST_HEADS
-        first_pair = jnp.where(late, t - LAST_HEADS, 0)
-        loop(jnp.where(late, 1, PAIRS), lambda index: pair(first_pair + index))
+        first_pair = jnp.where(late, 2 * (t - LAST_HEADS), 0)
+
+        def two_pairs(index):
+            pair(first_pair + 2 * index)
+            pair(first_pair + 2 * index + 1)
+        loop(jnp.where(late, 1, PAIRS // 2), two_pairs)
 
     @pl.when(project_back & (tile == 0))
     def _():
         for which, grads, low_ref, root_ref, gain, factor in ((0, dq, q, rq, qg_ref, SCALE), (1, dk, k, rk, kg_ref, 1.0)):
-            @halves()
-            def _(rows, columns):
-                grad, gains = grads[rows, columns], gain[layer]
-                xhat = low_ref[layer, rows, columns].astype(F32) * (1.0 / (gains * factor))
+            @thirds
+            def _(columns):
+                grad, gains = grads[:, columns], gain[layer]
+                xhat = low_ref[layer, :, columns].astype(F32) * (1.0 / (gains * factor))
                 scaled = grad * gains
                 mean = head_means(scaled, spread, False)
                 along = head_means(scaled * xhat, spread, False)
-                dproj[which, rows, columns] = (root_ref[layer, rows, columns].astype(F32) * (scaled - mean - xhat * along)).astype(BF16)
+                dproj[which, :, columns] = (root_ref[layer, :, columns].astype(F32) * (scaled - mean - xhat * along)).astype(BF16)
                 gain_ref[layer, which + 1 : which + 2, columns] += jnp.sum(grad * xhat, 0, keepdims=True)
 
     @pl.when(project_back)
     def _():
-        product = dot(dproj[tile], w_ref[...], ACROSS)
-        pl.when(tile == up_first(0))(lambda: acc.__setitem__(..., product))
-        pl.when(tile != up_first(0))(lambda: acc.__setitem__(..., acc[...] + product))
+        acc[...] = jnp.where(tile == up_first(0), 0.0, acc[...]) + dot(dproj[tile], w_ref[...], ACROSS)
         terms_in_ref[...] = dot(normed[layer, :, :], dproj[tile], DOWN).astype(BF16)
 
         @pl.when(tile == LAST_TILE)
@@ -1083,12 +1085,13 @@
 
 
 def augment(image_id, token_size):
-    high, low = split(jnp.log2(token_size.astype(F32)))
-    same = (image_id[:, None] == jnp.arange(3)[None, :]).astype(BF16)
-    one = jnp.ones_like(high)
-    q = jnp.concatenate([one[:, None], one[:, None], same, one[:, None]], 1)
-    k = jnp.concatenate([high[:, None], low[:, None], same * APART, one[:, None] * -APART], 1)
-    return [jnp.tile(jnp.pad(part, ((0, 0), (0, HD - 6))), (1, 2)) for part in (q, k)]
+    lane = jnp.arange(128)[None, :] % HD
+    size = jnp.log2(token_size.astype(F32))[:, None]
+    high = size.astype(BF16).astype(F32)
+    same = image_id[:, None] == lane - 2
+    q = jnp.where((lane < 2) | (lane == 5) | same, 1.0, 0.0)
+    k = jnp.where(lane == 0, high, jnp.where(lane == 1, size - high, jnp.where(lane == 5, -APART, jnp.where(same, APART, 0.0))))
+    return q.astype(BF16), k.astype(BF16)
 
 
 def spread_matrix():

time: 410 us -> 380 us (0.927)
  Pallas kernels: 390 us -> 361 us
    pallas_call x1, Pallas kernels: 301 us -> 272 us  [both_layers(): pl.pallas_call(functools.partial(compute_kernel, trading, counts), grid=(...]
where the time goes in v8:
time: 380 us; the launch traced here: 376 us
  Pallas kernels  361 us (95%)
  other arithmetic  8.56 us (2%)
  local copies, waits for them, and re-layouts  6.11 us (2%)
    pallas_call x1, Pallas kernels, both_layers(): pl.pallas_call(functools.partial(compute_kernel, trading, counts), grid=(...  272 us
    pallas_call x1, Pallas kernels, scatter_terms(): pl.pallas_call(scatter_kernel, out_shape=(jax.ShapeDtypeStruct(BLOCK[0],...  88.1 us

profile of v8, /device:TPU:8, one launch (start us, length us, event | category | flops | bytes accessed | tf_op | source)
XLA Modules:
  0.0 376.0 jit_solution(1586251331347748833)
XLA Ops:
  0.6 0.0 copy-start
  0.7 0.7 log_multiply_fusion
  1.4 0.0 copy-done
  1.4 0.9 fusion.3.refs_6_
  2.4 0.8 select_convert_fusion.2.refs_5_
  3.2 0.8 select_convert_fusion.1.refs_7_
  3.9 1.4 fusion.12.refs_2_
  5.3 272.4 %both_layers.1 = (bf16[2,512,768]{2,1,0:T(8,128)(2,1)}, f32[512,768]{1,0:T(8,128)}, bf16[512,768]{1,0:T(8,128)(2,1)}, bf16[512,768]{1,0:T(8,128)(2,1)}, f32[16,1...) custom-call(bf16[48,5376]{1,0:T(8,128)(2,1)} %bitcast.14, ...), custom_call_target="tpu_custom_call" | custom-call | tf_op jit(solution)/shard_map/both_layers/pallas_call | solution.py:1065
  277.7 0.0 copy-start.2
  277.7 1.1 copy-done.2
  278.8 0.0 copy-start.3
  278.8 0.7 copy-done.3
  279.5 0.0 copy-start.6
  279.5 88.1 %scatter_terms.1 = (bf16[48,5376]{1,0:T(8,128)(2,1)S(1)}, f32[16,128]{1,0:T(8,128)S(1)}, bf16[512,768]{1,0:T(8,128)(2,1)S(1)}) custom-call(bf16[2,768,5376]{2,1,0:T(8,128)(2,1)} %get-tuple-element.19.terms, f32[16,128]{1,0:T(8,128)S(1)} %copy-done.3, bf16[512,768]{1,0:T(8,128)(2,1)S(1)} %copy-done.2), custom_call_target="tpu_custom_call" | custom-call | tf_op jit(solution)/shard_map/scatter_terms/pallas_call | solution.py:597
  367.7 0.0 copy-done.6
  367.7 0.0 copy-start.5
  367.7 0.1 select_convert_fusion
  367.8 1.3 copy-done.5
  369.1 0.0 copy-start.7
  369.1 1.9 broadcast_select_fusion
  371.0 0.0 copy-start.4
  371.0 1.0 bitcast_convert_fusion
  372.1 0.1 fusion.14
  372.1 0.6 constant_dynamic-slice_fusion
  372.7 0.6 constant_dynamic-slice_fusion.1
  373.3 0.6 dynamic-slice.4
  373.9 0.0 copy-done.7
  373.9 0.0 copy-start.1
  373.9 0.9 bitcast_convert_fusion.1
  374.8 0.0 copy-done.4
  374.8 1.1 copy.18
  375.9 0.0 copy-done.1
  (9 shorter events, 0.1 us)
Async XLA Ops:
  0.6 0.7 copy-start
  277.7 1.1 copy-start.2
  278.8 0.7 copy-start.3
  279.5 88.1 %copy-start.6 = (bf16[512,768]{1,0:T(8,128)(2,1)S(1)}, bf16[512,768]{1,0:T(8,128)(2,1)}, u32[]{:S(2)}) copy-start(bf16[512,768]{1,0:T(8,128)(2,1)} %get-tuple-element.23) | copy-start | bytes 2359300
  367.7 1.4 copy-start.5
  369.1 4.8 %copy-start.7 = (bf16[240,768]{1,0:T(8,128)(2,1)S(1)}, bf16[240,768]{1,0:T(8,128)(2,1)}, u32[]{:S(2)}) copy-start(bf16[240,768]{1,0:T(8,128)(2,1)} %get-tuple-element.25) | copy-start | bytes 1105924
  371.0 3.8 %copy-start.4 = (bf16[2,512,768]{2,1,0:T(8,128)(2,1)S(1)}, bf16[2,512,768]{2,1,0:T(8,128)(2,1)}, u32[]{:S(2)}) copy-start(bf16[2,512,768]{2,1,0:T(8,128)(2,1)} %get-tuple-element.17) | copy-start | bytes 4718596
  373.9 2.1 copy-start.1

commit v9 on v8

--- a/solution.py
+++ b/solution.py
@@ -738,7 +738,8 @@
             body(pl.ds(256 * part, 256))
 
     def by_rows(body):
-        loop(SLOTS // 128, lambda index: body(pl.ds(pl.multiple_of(index * 128, 128), 128)))
+        for index in range(SLOTS // 128):
+            body(pl.ds(index * 128, 128))
 
     @pl.when(t == 0)
     def _():
@@ -846,13 +847,13 @@
         def grads(columns):
             return dot(dy[...], w_ref[columns, :], ACROSS)
 
-        terms_tile[made % 2] = dot(combined[layer, tile], dy[...], DOWN).astype(BF16)
-        terms_copy(terms_out, terms_tile, terms_sem, made % 2, layer, tile).start()
-        if not trading:
-            pl.when(t == LAST_BACK - 1)(lambda: terms_settled(terms_out, terms_tile, terms_sem))
+        def terms():
+            terms_tile[made % 2] = dot(combined[layer, tile], dy[...], DOWN).astype(BF16)
 
         @pl.when(tile == 0)
         def _():
+            terms()
+
             @thirds
             def _(columns):
                 grad, inverse = grads(columns), linv[layer, :, columns].astype(F32)
@@ -866,9 +867,15 @@
 
         @pl.when(tile > 0)
         def _():
+            terms()
+
             @thirds
             def _(columns):
                 dproj[tile + 2, :, columns] = (grads(columns) * slope[layer, tile - 1, :, columns].astype(F32)).astype(BF16)
+
+        terms_copy(terms_out, terms_tile, terms_sem, made % 2, layer, tile).start()
+        if not trading:
+            pl.when(t == LAST_BACK - 1)(lambda: terms_settled(terms_out, terms_tile, terms_sem))
 
     @pl.when(heads_now)
     def _():

time: 380 us -> 377 us (level)
  no operation moved by 1% of the time
where the time goes in v9:
time: 377 us; the launch traced here: 373 us
  Pallas kernels  358 us (95%)
  other arithmetic  8.56 us (2%)
  local copies, waits for them, and re-layouts  6.11 us (2%)
    pallas_call x1, Pallas kernels, both_layers(): pl.pallas_call(functools.partial(compute_kernel, trading, counts), grid=(...  269 us
    pallas_call x1, Pallas kernels, scatter_terms(): pl.pallas_call(scatter_kernel, out_shape=(jax.ShapeDtypeStruct(BLOCK[0],...  88.2 us

profile of v9, /device:TPU:8, one launch (start us, length us, event | category | flops | bytes accessed | tf_op | source)
XLA Modules:
  0.0 373.0 jit_solution(11081173710961202755)
XLA Ops:
  0.6 0.0 copy-start
  0.7 0.7 log_multiply_fusion
  1.4 0.0 copy-done
  1.4 0.9 fusion.3.refs_6_
  2.4 0.8 select_convert_fusion.2.refs_5_
  3.2 0.8 select_convert_fusion.1.refs_7_
  3.9 1.4 fusion.12.refs_2_
  5.3 269.4 %both_layers.1 = (bf16[2,512,768]{2,1,0:T(8,128)(2,1)}, f32[512,768]{1,0:T(8,128)}, bf16[512,768]{1,0:T(8,128)(2,1)}, bf16[512,768]{1,0:T(8,128)(2,1)}, f32[16,1...) custom-call(bf16[48,5376]{1,0:T(8,128)(2,1)} %bitcast.14, ...), custom_call_target="tpu_custom_call" | custom-call | tf_op jit(solution)/shard_map/both_layers/pallas_call | solution.py:1072
  274.7 0.0 copy-start.2
  274.7 1.1 copy-done.2
  275.8 0.0 copy-start.3
  275.8 0.7 copy-done.3
  276.5 0.0 copy-start.6
  276.5 88.2 %scatter_terms.1 = (bf16[48,5376]{1,0:T(8,128)(2,1)S(1)}, f32[16,128]{1,0:T(8,128)S(1)}, bf16[512,768]{1,0:T(8,128)(2,1)S(1)}) custom-call(bf16[2,768,5376]{2,1,0:T(8,128)(2,1)} %get-tuple-element.19.terms, f32[16,128]{1,0:T(8,128)S(1)} %copy-done.3, bf16[512,768]{1,0:T(8,128)(2,1)S(1)} %copy-done.2), custom_call_target="tpu_custom_call" | custom-call | tf_op jit(solution)/shard_map/scatter_terms/pallas_call | solution.py:597
  364.7 0.0 copy-done.6
  364.7 0.0 copy-start.5
  364.7 0.1 select_convert_fusion
  364.9 1.3 copy-done.5
  366.1 0.0 copy-start.7
  366.1 1.9 broadcast_select_fusion
  368.1 0.0 copy-start.4
  368.1 1.0 bitcast_convert_fusion
  369.1 0.1 fusion.14
  369.2 0.6 constant_dynamic-slice_fusion
  369.8 0.6 constant_dynamic-slice_fusion.1
  370.3 0.6 dynamic-slice.4
  370.9 0.0 copy-done.7
  370.9 0.0 copy-start.1
  370.9 0.9 bitcast_convert_fusion.1
  371.8 0.0 copy-done.4
  371.8 1.1 copy.18
  373.0 0.0 copy-done.1
  (9 shorter events, 0.1 us)
Async XLA Ops:
  0.6 0.7 copy-start
  274.7 1.1 copy-start.2
  275.8 0.7 copy-start.3
  276.5 88.2 %copy-start.6 = (bf16[512,768]{1,0:T(8,128)(2,1)S(1)}, bf16[512,768]{1,0:T(8,128)(2,1)}, u32[]{:S(2)}) copy-start(bf16[512,768]{1,0:T(8,128)(2,1)} %get-tuple-element.23) | copy-start | bytes 2359300
  364.7 1.4 copy-start.5
  366.1 4.8 %copy-start.7 = (bf16[240,768]{1,0:T(8,128)(2,1)S(1)}, bf16[240,768]{1,0:T(8,128)(2,1)}, u32[]{:S(2)}) copy-start(bf16[240,768]{1,0:T(8,128)(2,1)} %get-tuple-element.25) | copy-start | bytes 1105924
  368.1 3.8 %copy-start.4 = (bf16[2,512,768]{2,1,0:T(8,128)(2,1)S(1)}, bf16[2,512,768]{2,1,0:T(8,128)(2,1)}, u32[]{:S(2)}) copy-start(bf16[2,512,768]{2,1,0:T(8,128)(2,1)} %get-tuple-element.17) | copy-start | bytes 4718596
  370.9 2.1 copy-start.1

commit v10 on v9

--- a/solution.py
+++ b/solution.py
@@ -323,7 +323,7 @@
 
 
 OUTER_ORDER = (
-    ("k3", "l3"), (), ("a3", "k2"), (), ("l2",), ("b3", "k1", "a2", "z3"), ("l1",), ("k0", "b2"), ("z2", "a1", "l0"), (),
+    ("k3", "l3"), (), ("a3", "k2"), (), ("l2", "b3", "k1"), ("a2", "z3", "l1"), ("k0", "b2"), ("z2", "a1", "l0"), (),
     ("a0", "b1", "z1", "s", "b0", "z0"))
 INNER_ORDER = (
     "k3", "k2", "l3", "k1", "l2", "a3", "k0", "l1", "b3", "a2", "z3", "a1", "l0", "b2", "z2", "b1", "a0", "z1", "s", "b0", "z0")
@@ -646,7 +646,7 @@
     return pl.ds(index * width if isinstance(index, int) else pl.multiple_of(index * width, width), width)
 
 
-FIRST_OUT, SECOND_IN, SECOND_OUT, SECOND_BACK, LAST_OUT, LAST_BACK, LAST_HEADS, LAST_PROJECT, STEPS = 7, 12, 19, 24, 31, 36, 40, 43, 46
+FIRST_OUT, SECOND_IN, SECOND_OUT, SECOND_BACK, LAST_OUT, LAST_BACK, LAST_HEADS, LAST_PROJECT, STEPS = 7, 12, 19, 24, 31, 36, 40, 42, 45
 LAST_TILE = 2
 
 
@@ -903,12 +903,12 @@
             dk[:, part] = sums[1] * (1.0 / LOG2E)
             dproj[2, :, part] = sums[2].astype(BF16)
         late = t >= LAST_HEADS
-        first_pair = jnp.where(late, 2 * (t - LAST_HEADS), 0)
-
-        def two_pairs(index):
-            pair(first_pair + 2 * index)
-            pair(first_pair + 2 * index + 1)
-        loop(jnp.where(late, 1, PAIRS // 2), two_pairs)
+        first_pair = jnp.where(late, 3 * (t - LAST_HEADS), 0)
+
+        def three_pairs(index):
+            for part in range(3):
+                pair(first_pair + 3 * index + part)
+        loop(jnp.where(late, 1, PAIRS // 3), three_pairs)
 
     @pl.when(project_back & (tile == 0))
     def _():

time: 377 us -> 373 us (0.989)
  Pallas kernels: 358 us -> 353 us
    pallas_call x1, Pallas kernels: 269 us -> 265 us  [both_layers(): pl.pallas_call(functools.partial(compute_kernel, trading, counts), grid=(...]
where the time goes in v10:
time: 373 us; the launch traced here: 368 us
  Pallas kernels  353 us (95%)
  other arithmetic  8.56 us (2%)
  local copies, waits for them, and re-layouts  6.11 us (2%)
    pallas_call x1, Pallas kernels, both_layers(): pl.pallas_call(functools.partial(compute_kernel, trading, counts), grid=(...  265 us
    pallas_call x1, Pallas kernels, scatter_terms(): pl.pallas_call(scatter_kernel, out_shape=(jax.ShapeDtypeStruct(BLOCK[0],...  87.8 us

profile of v10, /device:TPU:8, one launch (start us, length us, event | category | flops | bytes accessed | tf_op | source)
XLA Modules:
  0.0 368.5 jit_solution(18236046127139495965)
XLA Ops:
  0.6 0.0 copy-start
  0.7 0.7 log_multiply_fusion
  1.4 0.0 copy-done
  1.4 0.9 fusion.3.refs_6_
  2.4 0.8 select_convert_fusion.2.refs_5_
  3.2 0.8 select_convert_fusion.1.refs_7_
  3.9 1.4 fusion.12.refs_2_
  5.3 265.3 %both_layers.1 = (bf16[2,512,768]{2,1,0:T(8,128)(2,1)}, f32[512,768]{1,0:T(8,128)}, bf16[512,768]{1,0:T(8,128)(2,1)}, bf16[512,768]{1,0:T(8,128)(2,1)}, f32[16,1...) custom-call(bf16[48,5376]{1,0:T(8,128)(2,1)} %bitcast.14, ...), custom_call_target="tpu_custom_call" | custom-call | tf_op jit(solution)/shard_map/both_layers/pallas_call | solution.py:1072
  270.5 0.0 copy-start.2
  270.6 1.1 copy-done.2
  271.7 0.0 copy-start.3
  271.7 0.7 copy-done.3
  272.4 0.0 copy-start.6
  272.4 87.8 %scatter_terms.1 = (bf16[48,5376]{1,0:T(8,128)(2,1)S(1)}, f32[16,128]{1,0:T(8,128)S(1)}, bf16[512,768]{1,0:T(8,128)(2,1)S(1)}) custom-call(bf16[2,768,5376]{2,1,0:T(8,128)(2,1)} %get-tuple-element.19.terms, f32[16,128]{1,0:T(8,128)S(1)} %copy-done.3, bf16[512,768]{1,0:T(8,128)(2,1)S(1)} %copy-done.2), custom_call_target="tpu_custom_call" | custom-call | tf_op jit(solution)/shard_map/scatter_terms/pallas_call | solution.py:597
  360.2 0.0 copy-done.6
  360.2 0.0 copy-start.5
  360.2 0.1 select_convert_fusion
  360.3 1.3 copy-done.5
  361.6 0.0 copy-start.7
  361.6 1.9 broadcast_select_fusion
  363.5 0.0 copy-start.4
  363.5 1.0 bitcast_convert_fusion
  364.6 0.1 fusion.14
  364.7 0.6 constant_dynamic-slice_fusion
  365.2 0.6 constant_dynamic-slice_fusion.1
  365.8 0.6 dynamic-slice.4
  366.4 0.0 copy-done.7
  366.4 0.0 copy-start.1
  366.4 0.9 bitcast_convert_fusion.1
  367.3 0.0 copy-done.4
  367.3 1.1 copy.18
  368.5 0.0 copy-done.1
  (9 shorter events, 0.1 us)
Async XLA Ops:
  0.6 0.7 copy-start
  270.5 1.1 copy-start.2
  271.7 0.7 copy-start.3
  272.4 87.8 %copy-start.6 = (bf16[512,768]{1,0:T(8,128)(2,1)S(1)}, bf16[512,768]{1,0:T(8,128)(2,1)}, u32[]{:S(2)}) copy-start(bf16[512,768]{1,0:T(8,128)(2,1)} %get-tuple-element.23) | copy-start | bytes 2359300
  360.2 1.4 copy-start.5
  361.6 4.8 %copy-start.7 = (bf16[240,768]{1,0:T(8,128)(2,1)S(1)}, bf16[240,768]{1,0:T(8,128)(2,1)}, u32[]{:S(2)}) copy-start(bf16[240,768]{1,0:T(8,128)(2,1)} %get-tuple-element.25) | copy-start | bytes 1105924
  363.5 3.8 %copy-start.4 = (bf16[2,512,768]{2,1,0:T(8,128)(2,1)S(1)}, bf16[2,512,768]{2,1,0:T(8,128)(2,1)}, u32[]{:S(2)}) copy-start(bf16[2,512,768]{2,1,0:T(8,128)(2,1)} %get-tuple-element.17) | copy-start | bytes 4718596
  366.4 2.1 copy-start.1

commit v11 on v10

--- a/solution.py
+++ b/solution.py
@@ -323,7 +323,7 @@
 
 
 OUTER_ORDER = (
-    ("k3", "l3"), (), ("a3", "k2"), (), ("l2", "b3", "k1"), ("a2", "z3", "l1"), ("k0", "b2"), ("z2", "a1", "l0"), (),
+    ("k3", "l3"), (), ("a3", "k2"), (), ("l2", "b3", "k1", "k0"), ("a2", "z3", "l1", "b2"), ("z2", "a1", "l0"), (),
     ("a0", "b1", "z1", "s", "b0", "z0"))
 INNER_ORDER = (
     "k3", "k2", "l3", "k1", "l2", "a3", "k0", "l1", "b3", "a2", "z3", "a1", "l0", "b2", "z2", "b1", "a0", "z1", "s", "b0", "z0")
@@ -646,7 +646,7 @@
     return pl.ds(index * width if isinstance(index, int) else pl.multiple_of(index * width, width), width)
 
 
-FIRST_OUT, SECOND_IN, SECOND_OUT, SECOND_BACK, LAST_OUT, LAST_BACK, LAST_HEADS, LAST_PROJECT, STEPS = 7, 12, 19, 24, 31, 36, 40, 42, 45
+FIRST_OUT, SECOND_IN, SECOND_OUT, SECOND_BACK, LAST_OUT, LAST_BACK, LAST_HEADS, LAST_PROJECT, STEPS = 7, 12, 19, 24, 31, 36, 40, 41, 44
 LAST_TILE = 2
 
 
@@ -902,13 +902,8 @@
             dq[:, part] = sums[0] * 0.125
             dk[:, part] = sums[1] * (1.0 / LOG2E)
             dproj[2, :, part] = sums[2].astype(BF16)
-        late = t >= LAST_HEADS
-        first_pair = jnp.where(late, 3 * (t - LAST_HEADS), 0)
-
-        def three_pairs(index):
-            for part in range(3):
-                pair(first_pair + 3 * index + part)
-        loop(jnp.where(late, 1, PAIRS // 3), three_pairs)
+        for index in range(PAIRS):
+            pair(index)
 
     @pl.when(project_back & (tile == 0))
     def _():

time: 373 us -> 377 us (1.011)
  Pallas kernels: 353 us -> 358 us
    pallas_call x1, Pallas kernels: 265 us -> 270 us  [both_layers(): pl.pallas_call(functools.partial(compute_kernel, trading, counts), grid=(...]
where the time goes in v11:
time: 377 us; the launch traced here: 373 us
  Pallas kernels  358 us (95%)
  other arithmetic  8.56 us (2%)
  local copies, waits for them, and re-layouts  6.11 us (2%)
    pallas_call x1, Pallas kernels, both_layers(): pl.pallas_call(functools.partial(compute_kernel, trading, counts), grid=(...  270 us
    pallas_call x1, Pallas kernels, scatter_terms(): pl.pallas_call(scatter_kernel, out_shape=(jax.ShapeDtypeStruct(BLOCK[0],...  87.8 us

profile of v11, /device:TPU:8, one launch (start us, length us, event | category | flops | bytes accessed | tf_op | source)
XLA Modules:
  0.0 373.0 jit_solution(13981472838571875830)
XLA Ops:
  0.6 0.0 copy-start
  0.7 0.7 log_multiply_fusion
  1.4 0.0 copy-done
  1.4 0.9 fusion.3.refs_6_
  2.4 0.8 select_convert_fusion.2.refs_5_
  3.2 0.8 select_convert_fusion.1.refs_7_
  3.9 1.4 fusion.12.refs_2_
  5.3 269.8 %both_layers.1 = (bf16[2,512,768]{2,1,0:T(8,128)(2,1)}, f32[512,768]{1,0:T(8,128)}, bf16[512,768]{1,0:T(8,128)(2,1)}, bf16[512,768]{1,0:T(8,128)(2,1)}, f32[16,1...) custom-call(bf16[48,5376]{1,0:T(8,128)(2,1)} %bitcast.14, ...), custom_call_target="tpu_custom_call" | custom-call | tf_op jit(solution)/shard_map/both_layers/pallas_call | solution.py:1067
  275.1 0.0 copy-start.2
  275.1 1.1 copy-done.2
  276.2 0.0 copy-start.3
  276.2 0.7 copy-done.3
  276.9 0.0 copy-start.6
  276.9 87.8 %scatter_terms.1 = (bf16[48,5376]{1,0:T(8,128)(2,1)S(1)}, f32[16,128]{1,0:T(8,128)S(1)}, bf16[512,768]{1,0:T(8,128)(2,1)S(1)}) custom-call(bf16[2,768,5376]{2,1,0:T(8,128)(2,1)} %get-tuple-element.19.terms, f32[16,128]{1,0:T(8,128)S(1)} %copy-done.3, bf16[512,768]{1,0:T(8,128)(2,1)S(1)} %copy-done.2), custom_call_target="tpu_custom_call" | custom-call | tf_op jit(solution)/shard_map/scatter_terms/pallas_call | solution.py:597
  364.7 0.0 copy-done.6
  364.7 0.0 copy-start.5
  364.8 0.1 select_convert_fusion
  364.9 1.3 copy-done.5
  366.2 0.0 copy-start.7
  366.2 1.9 broadcast_select_fusion
  368.1 0.0 copy-start.4
  368.1 1.0 bitcast_convert_fusion
  369.1 0.1 fusion.14
  369.2 0.6 constant_dynamic-slice_fusion
  369.8 0.6 constant_dynamic-slice_fusion.1
  370.4 0.6 dynamic-slice.4
  371.0 0.0 copy-done.7
  371.0 0.0 copy-start.1
  371.0 0.9 bitcast_convert_fusion.1
  371.9 0.0 copy-done.4
  371.9 1.1 copy.18
  373.0 0.0 copy-done.1
  (9 shorter events, 0.1 us)
Async XLA Ops:
  0.6 0.7 copy-start
  275.1 1.1 copy-start.2
  276.2 0.7 copy-start.3
  276.9 87.8 %copy-start.6 = (bf16[512,768]{1,0:T(8,128)(2,1)S(1)}, bf16[512,768]{1,0:T(8,128)(2,1)}, u32[]{:S(2)}) copy-start(bf16[512,768]{1,0:T(8,128)(2,1)} %get-tuple-element.23) | copy-start | bytes 2359300
  364.7 1.4 copy-start.5
  366.2 4.8 %copy-start.7 = (bf16[240,768]{1,0:T(8,128)(2,1)S(1)}, bf16[240,768]{1,0:T(8,128)(2,1)}, u32[]{:S(2)}) copy-start(bf16[240,768]{1,0:T(8,128)(2,1)} %get-tuple-element.25) | copy-start | bytes 1105924
  368.1 3.8 %copy-start.4 = (bf16[2,512,768]{2,1,0:T(8,128)(2,1)S(1)}, bf16[2,512,768]{2,1,0:T(8,128)(2,1)}, u32[]{:S(2)}) copy-start(bf16[2,512,768]{2,1,0:T(8,128)(2,1)} %get-tuple-element.17) | copy-start | bytes 4718596
  371.0 2.1 copy-start.1
